TPU v7x, 32 devices: a whole 2x2x4 slice. The times are simulated.
32 devices in a mesh: dp: 4 (over y, x), seq: 8 (over z, core).
Axes of the slice: x: 2, y: 2, z: 4, core: 2. Of those that a mesh axis runs over, the one named last changes fastest.
Arguments:
- tokens: bfloat16 [32768, 1024], P(('dp', 'seq')), may hold values from -6 to 6
- segments: int32 [4, 8192], P('dp', 'seq'), may hold values from 0 to 1, never falling along the last dimension, each value on 1 to 6144 neighbouring positions
- cotangent: bfloat16 [32768, 1024], P(('dp', 'seq')), may hold values from -6 to 6
- tile_of_slot: int32 [768], replicated, may hold values from 0 to 767, as said below
- tiles: float32 [768, 128, 128], P(('dp', 'seq'))
- left_bases: float32 [768, 128, 128], P(('dp', 'seq')), as said below
- right_bases: float32 [768, 128, 128], P(('dp', 'seq')), as said below
- first_moments: float32 [768, 128, 128], P(('dp', 'seq'))
- second_moments: float32 [768, 128, 128], P(('dp', 'seq')), as said below
- small_params: float32 [12288], P(('dp', 'seq'))
- small_first: float32 [12288], P(('dp', 'seq'))
- small_second: float32 [12288], P(('dp', 'seq')), as said below
- threshold: float32 [1], replicated, may hold values from 1.5 to 2.5
Outputs:
- block_output: bfloat16 [32768, 1024], P(('dp', 'seq'))
- input_grad: float32 [32768, 1024], P(('dp', 'seq'))
- tile_grads: float32 [768, 128, 128], P(('dp', 'seq'))
- small_grads: float32 [12288], P(('dp', 'seq'))
- new_tiles: float32 [768, 128, 128], P(('dp', 'seq'))
- new_tiles_low: bfloat16 [768, 128, 128], P(('dp', 'seq'))
- new_first_moments: float32 [768, 128, 128], P(('dp', 'seq'))
- new_second_moments: float32 [768, 128, 128], P(('dp', 'seq'))
- new_small: float32 [12288], P(('dp', 'seq'))
- new_small_low: bfloat16 [12288], P(('dp', 'seq'))
- new_small_first: float32 [12288], P(('dp', 'seq'))
- new_small_second: float32 [12288], P(('dp', 'seq'))
- clip_factors: float32 [16], replicated
Inputs may be any that keep to these rules, and one draw needn't show every extreme that they name: `tile_of_slot`: a permutation of the numbers 0 to 767. `segments`: segment numbers never fall along a row; each row holds two documents, each of 2048 tokens or more. `left_bases`: every tile is an orthogonal matrix. `right_bases`: every tile is an orthogonal matrix. `second_moments`: all entries are positive. `small_second`: all entries are positive.
All inputs are finite; a program needn't handle non-finite values.
Results may differ from a plain program's by a relative error of at most 0.011.
Values may be sent and summed in bfloat16 or wider, within the bound.
A program may use at most 448 MiB of HBM per device.

v0:
```python
import jax
import jax.numpy as jnp
from jax import lax
from jax.sharding import PartitionSpec as P

D = 1024
FF = 4096
HEADS = 16
HEAD = 64
ROT = 16
BLK = 128
WINDOW = 1024
QBLK = 512


NORM_EPS = 1e-05
ADAM_EPS = 1e-08
BETA = 0.5
LEARN = 0.03
SMALL_LEARN = 0.2
ROPE_BASE = 10000.0
MASKED = -1e30
HIGH = lax.Precision.HIGHEST


def passed_along(value, axis, steps):
    count = lax.axis_size(axis)
    leading, last = (max(0, -steps), min(count, count - steps))
    return lax.ppermute(value, axis, [(source, source + steps) for source in range(leading, last)])


def untile(tile_block, height, breadth):
    tile_grid = tile_block.reshape(height // BLK, breadth // BLK, BLK, BLK)
    return tile_grid.transpose(0, 2, 1, 3).reshape(height, breadth)


def retile(matrix):
    height, breadth = matrix.shape
    tile_grid = matrix.reshape(height // BLK, BLK, breadth // BLK, BLK)
    return tile_grid.transpose(0, 2, 1, 3).reshape(-1, BLK, BLK)


def split_tiles(by_number):
    count_qkv = D // BLK * (3 * D // BLK)
    count_out = D // BLK * (D // BLK)
    count_up = D // BLK * (FF // BLK)
    second_end = count_qkv + count_out
    third_end = second_end + count_up
    return (
        untile(by_number[:count_qkv], D, 3 * D),
        untile(by_number[count_qkv:second_end], D, D),
        untile(by_number[second_end:third_end], D, FF),
        untile(by_number[third_end:], FF, D),
    )


def split_small(small_vector):
    small_table = small_vector.reshape(D, 12)
    return (
        small_table[:, 0],
        small_table[:, 1],
        small_table[:, 2],
        small_table[:, 3:7].reshape(FF),
        small_table[:, 7],
        small_table[:, 8],
        small_table[:, 9],
        small_table[:, 10],
        small_table[:, 11],
    )


def rope_tables(positions):
    half_rot = ROT // 2
    exponent = jnp.arange(half_rot, dtype=jnp.float32) * (2.0 / ROT)
    frequency = jnp.power(ROPE_BASE, -exponent)
    angle = positions.astype(jnp.float32)[:, None] * frequency[None, :]
    return (jnp.cos(angle), jnp.sin(angle))


def rotate(heads_value, cosine_table, sine_table, direction):
    half_rot = ROT // 2
    first_half = heads_value[..., :half_rot]
    second_half = heads_value[..., half_rot:ROT]
    rest_part = heads_value[..., ROT:]
    cos_part = cosine_table[:, None, :]
    sin_part = sine_table[:, None, :] * direction
    return jnp.concatenate(
        [
            first_half * cos_part - second_half * sin_part,
            second_half * cos_part + first_half * sin_part,
            rest_part,
        ],
        axis=-1,
    )


def allowed_mask(query_place, key_place, query_seg, key_seg):
    distance = query_place[:, None] - key_place[None, :]
    inside = key_place[None, :] >= 0
    return (distance >= 0) & (distance < WINDOW) & inside & (query_seg[:, None] == key_seg[None, :])


def gelu_exact(value):
    return jax.nn.gelu(value, approximate=False)


def column_scales(tile_ids, factors):
    count_qkv = D // BLK * (3 * D // BLK)
    columns = (tile_ids % (3 * D // BLK))[:, None] * BLK + jnp.arange(BLK, dtype=jnp.int32)[None, :]
    head_index = columns % D // HEAD
    root_factor = jnp.sqrt(factors)
    picked = jnp.sum(
        jnp.where(head_index[..., None] == jnp.arange(HEADS, dtype=jnp.int32), root_factor, 0.0),
        axis=-1,
    )
    clipped = (tile_ids[:, None] < count_qkv) & (columns < 2 * D)
    return jnp.where(clipped, picked, 1.0)


def rotate_update(grads, weights, left, right, first_moment, second_moment, column_scale):
    turned = jnp.einsum("sji,sjk->sik", left, grads, precision=HIGH)
    turned = jnp.einsum("sik,skl->sil", turned, right, precision=HIGH)
    first_new = BETA * first_moment + (1.0 - BETA) * turned
    second_new = BETA * second_moment + (1.0 - BETA) * turned * turned
    ratio = first_new / (jnp.sqrt(second_new) + ADAM_EPS)
    back_turned = jnp.einsum("sij,sjk->sik", left, ratio, precision=HIGH)
    back_turned = jnp.einsum("sik,slk->sil", back_turned, right, precision=HIGH)
    updated = (weights - LEARN * back_turned) * column_scale[:, None, :]
    return (updated, first_new, second_new)


def small_update(grads, params, first_moment, second_moment):
    first_new = BETA * first_moment + (1.0 - BETA) * grads
    second_new = BETA * second_moment + (1.0 - BETA) * grads * grads
    updated = params - SMALL_LEARN * first_new / (jnp.sqrt(second_new) + ADAM_EPS)
    return (updated, first_new, second_new)


def on_device(
    tokens,
    segments,
    cotangent,
    tile_of_slot,
    tiles,
    left_bases,
    right_bases,
    first_moments,
    second_moments,
    small_params,
    small_first,
    small_second,
    threshold,
):
    row_count = tokens.shape[0]
    key_count = WINDOW + QBLK
    score_scale = HEAD ** (-0.5)
    contract_rows = (((0,), (0,)), ((), ()))
    contract_cols = (((1,), (1,)), ((), ()))
    seq_index = lax.axis_index("seq")
    first_place = seq_index * row_count
    positions = first_place + jnp.arange(row_count, dtype=jnp.int32)
    seg_local = segments.reshape(row_count)
    inverse = jnp.argsort(tile_of_slot)
    tiles_low = tiles.astype(jnp.bfloat16)
    small_low = small_params.astype(jnp.bfloat16)

    def collect():
        whole_tiles, whole_small = (
            lax.all_gather(tiles_low, ("dp", "seq"), axis=0, tiled=True),
            lax.all_gather(small_low, ("dp", "seq"), axis=0, tiled=True),
        )
        return (split_tiles(whole_tiles[inverse]), split_small(whole_small.astype(jnp.float32)))

    (w_qkv, w_out, w_up, w_down), smalls = collect()
    q_bias, v_bias, out_bias, up_bias, down_bias, gain_one, shift_one, gain_two, shift_two = smalls
    x_float = tokens.astype(jnp.float32)
    centered = x_float - jnp.mean(x_float, axis=-1, keepdims=True)
    inv_deviation = lax.rsqrt(jnp.mean(centered * centered, axis=-1, keepdims=True) + NORM_EPS)
    normed = centered * inv_deviation
    attn_in = (normed * gain_one + shift_one).astype(jnp.bfloat16)
    mlp_in = (normed * gain_two + shift_two).astype(jnp.bfloat16)
    bias_qkv = jnp.concatenate([q_bias, jnp.zeros((D,), jnp.float32), v_bias])
    projected = jnp.dot(attn_in, w_qkv, preferred_element_type=jnp.float32) + bias_qkv
    cosine_table, sine_table = rope_tables(positions)
    queries = rotate(
        projected[:, :D].reshape(row_count, HEADS, HEAD), cosine_table, sine_table, 1.0
    ).astype(jnp.bfloat16)
    key_rows = rotate(
        projected[:, D : 2 * D].reshape(row_count, HEADS, HEAD), cosine_table, sine_table, 1.0
    )
    key_rows = key_rows.reshape(row_count, D).astype(jnp.bfloat16)
    value_rows = projected[:, 2 * D :].astype(jnp.bfloat16)
    prev_keys, prev_values, prev_seg = passed_along(
        (key_rows, value_rows, seg_local.astype(jnp.bfloat16)), "seq", 1
    )
    keys_all = jnp.concatenate([prev_keys, key_rows], 0).reshape(2 * row_count, HEADS, HEAD)
    values_all = jnp.concatenate([prev_values, value_rows], 0).reshape(2 * row_count, HEADS, HEAD)
    seg_all = jnp.concatenate([prev_seg.astype(jnp.int32), seg_local], 0)
    key_places = first_place - row_count + jnp.arange(2 * row_count, dtype=jnp.int32)

    def block_scores(start):
        offset = start + row_count - WINDOW
        query_block = lax.dynamic_slice_in_dim(queries, start, QBLK, 0)
        key_block = lax.dynamic_slice_in_dim(keys_all, offset, key_count, 0)
        value_block = lax.dynamic_slice_in_dim(values_all, offset, key_count, 0)
        allowed = allowed_mask(
            first_place + start + jnp.arange(QBLK, dtype=jnp.int32),
            lax.dynamic_slice_in_dim(key_places, offset, key_count, 0),
            lax.dynamic_slice_in_dim(seg_local, start, QBLK, 0),
            lax.dynamic_slice_in_dim(seg_all, offset, key_count, 0),
        )
        scores = (
            jnp.einsum("qhd,khd->hqk", query_block, key_block, preferred_element_type=jnp.float32)
            * score_scale
        )
        masked = jnp.where(allowed[None], scores, MASKED)
        return (query_block, key_block, value_block, masked)

    def forward_block(start):
        query_block, key_block, value_block, masked = block_scores(start)
        row_top = jnp.max(masked, axis=-1, keepdims=True)
        exp_terms = jnp.exp(masked - row_top)
        row_total = jnp.sum(exp_terms, axis=-1, keepdims=True)
        attn_prob = (exp_terms / row_total).astype(jnp.bfloat16)
        block_out = jnp.einsum(
            "hqk,khd->qhd", attn_prob, value_block, preferred_element_type=jnp.float32
        )
        return (
            block_out.astype(jnp.bfloat16),
            row_top + jnp.log(row_total),
            jnp.max(row_top, axis=(1, 2)),
        )

    block_starts = jnp.arange(row_count // QBLK, dtype=jnp.int32) * QBLK
    block_outs, log_sums, block_peaks = lax.map(forward_block, block_starts)
    attn_out = block_outs.reshape(row_count, D)
    head_peak = lax.pmax(jnp.max(block_peaks, axis=0), ("dp", "seq"))
    attn_result = jnp.dot(attn_out, w_out, preferred_element_type=jnp.float32) + out_bias
    up_pre = jnp.dot(mlp_in, w_up, preferred_element_type=jnp.float32) + up_bias
    hidden_float, gelu_back = jax.vjp(gelu_exact, up_pre)
    hidden = hidden_float.astype(jnp.bfloat16)
    mlp_result = jnp.dot(hidden, w_down, preferred_element_type=jnp.float32) + down_bias
    block_output = (x_float + attn_result + mlp_result).astype(jnp.bfloat16)
    (w_qkv, w_out, w_up, w_down), smalls = collect()
    gain_one = smalls[5]
    gain_two = smalls[7]
    grad_float = cotangent.astype(jnp.float32)
    d_w_out = lax.dot_general(
        attn_out, cotangent, contract_rows, preferred_element_type=jnp.float32
    )
    d_w_down = lax.dot_general(hidden, cotangent, contract_rows, preferred_element_type=jnp.float32)
    d_hidden = lax.dot_general(cotangent, w_down, contract_cols, preferred_element_type=jnp.float32)
    d_up = gelu_back(d_hidden)[0].astype(jnp.bfloat16)
    d_w_up = lax.dot_general(mlp_in, d_up, contract_rows, preferred_element_type=jnp.float32)
    d_mlp_in = lax.dot_general(d_up, w_up, contract_cols, preferred_element_type=jnp.float32)
    d_attn_out = lax.dot_general(
        cotangent, w_out, contract_cols, preferred_element_type=jnp.float32
    )
    d_attn_out = d_attn_out.astype(jnp.bfloat16).reshape(row_count, HEADS, HEAD)

    def backward_block(carry, block_items):
        grad_keys_all, grad_values_all = carry
        start, log_sum = block_items
        query_block, key_block, value_block, masked = block_scores(start)
        attn_prob = jnp.exp(masked - log_sum)
        grad_out_block = lax.dynamic_slice_in_dim(d_attn_out, start, QBLK, 0)
        grad_values = jnp.einsum(
            "hqk,qhd->khd",
            attn_prob.astype(jnp.bfloat16),
            grad_out_block,
            preferred_element_type=jnp.float32,
        )
        grad_prob = jnp.einsum(
            "qhd,khd->hqk", grad_out_block, value_block, preferred_element_type=jnp.float32
        )
        grad_scores = attn_prob * (
            grad_prob - jnp.sum(attn_prob * grad_prob, axis=-1, keepdims=True)
        )
        grad_scores = grad_scores.astype(jnp.bfloat16)
        grad_query = (
            jnp.einsum("hqk,khd->qhd", grad_scores, key_block, preferred_element_type=jnp.float32)
            * score_scale
        )
        grad_key = (
            jnp.einsum("hqk,qhd->khd", grad_scores, query_block, preferred_element_type=jnp.float32)
            * score_scale
        )
        offset = start + row_count - WINDOW
        grad_keys_all = lax.dynamic_update_slice_in_dim(
            grad_keys_all,
            lax.dynamic_slice_in_dim(grad_keys_all, offset, key_count, 0) + grad_key,
            offset,
            0,
        )
        grad_values_all = lax.dynamic_update_slice_in_dim(
            grad_values_all,
            lax.dynamic_slice_in_dim(grad_values_all, offset, key_count, 0) + grad_values,
            offset,
            0,
        )
        return ((grad_keys_all, grad_values_all), grad_query)

    zero_heads = jnp.zeros((2 * row_count, HEADS, HEAD), jnp.float32)
    (grad_keys_all, grad_values_all), grad_queries = lax.scan(
        backward_block, (zero_heads, zero_heads), (block_starts, log_sums)
    )
    back_keys, back_values = (
        passed_along(
            grad_keys_all[:row_count].reshape(row_count, D).astype(jnp.bfloat16), "seq", -1
        ).astype(jnp.float32),
        passed_along(
            grad_values_all[:row_count].reshape(row_count, D).astype(jnp.bfloat16), "seq", -1
        ).astype(jnp.float32),
    )
    grad_key_rows = grad_keys_all[row_count:].reshape(row_count, D) + back_keys
    grad_value_rows = grad_values_all[row_count:].reshape(row_count, D) + back_values
    grad_query_rows = rotate(
        grad_queries.reshape(row_count, HEADS, HEAD), cosine_table, sine_table, -1.0
    )
    grad_key_heads = rotate(
        grad_key_rows.reshape(row_count, HEADS, HEAD), cosine_table, sine_table, -1.0
    )
    d_projected = jnp.concatenate(
        [
            grad_query_rows.reshape(row_count, D),
            grad_key_heads.reshape(row_count, D),
            grad_value_rows,
        ],
        axis=1,
    ).astype(jnp.bfloat16)
    projected_float = d_projected.astype(jnp.float32)
    d_q_bias = jnp.sum(projected_float[:, :D], axis=0)
    d_v_bias = jnp.sum(projected_float[:, 2 * D :], axis=0)
    d_w_qkv = lax.dot_general(
        attn_in, d_projected, contract_rows, preferred_element_type=jnp.float32
    )
    d_attn_in = lax.dot_general(
        d_projected, w_qkv, contract_cols, preferred_element_type=jnp.float32
    )
    d_up_bias = jnp.sum(d_up.astype(jnp.float32), axis=0)
    d_out_bias = jnp.sum(grad_float, axis=0)
    d_gain_one = jnp.sum(d_attn_in * normed, axis=0)
    d_shift_one = jnp.sum(d_attn_in, axis=0)
    d_gain_two = jnp.sum(d_mlp_in * normed, axis=0)
    d_shift_two = jnp.sum(d_mlp_in, axis=0)
    d_normed = d_attn_in * gain_one + d_mlp_in * gain_two
    input_grad = grad_float + inv_deviation * (
        d_normed
        - jnp.mean(d_normed, axis=-1, keepdims=True)
        - normed * jnp.mean(d_normed * normed, axis=-1, keepdims=True)
    )
    grad_by_number = jnp.concatenate(
        [retile(d_w_qkv), retile(d_w_out), retile(d_w_up), retile(d_w_down)], axis=0
    )
    slot_grads = grad_by_number[tile_of_slot]
    small_terms = jnp.concatenate(
        [
            d_q_bias[:, None],
            d_v_bias[:, None],
            d_out_bias[:, None],
            d_up_bias.reshape(D, FF // D),
            d_out_bias[:, None],
            d_gain_one[:, None],
            d_shift_one[:, None],
            d_gain_two[:, None],
            d_shift_two[:, None],
        ],
        axis=1,
    ).reshape(-1)
    tile_grads, small_grads = (
        lax.psum_scatter(slot_grads, ("dp", "seq"), scatter_dimension=0, tiled=True),
        lax.psum_scatter(small_terms, ("dp", "seq"), scatter_dimension=0, tiled=True),
    )
    slot_count = tile_grads.shape[0]
    owner_index = lax.axis_index(("dp", "seq"))
    local_ids = lax.dynamic_slice_in_dim(tile_of_slot, owner_index * slot_count, slot_count, 0)
    limit = threshold[0]
    factors = limit / jnp.maximum(head_peak, limit)
    column_scale = column_scales(local_ids, factors)
    new_tiles, new_first, new_second = rotate_update(
        tile_grads, tiles, left_bases, right_bases, first_moments, second_moments, column_scale
    )
    new_small, new_small_first, new_small_second = small_update(
        small_grads, small_params, small_first, small_second
    )
    return (
        block_output,
        input_grad,
        tile_grads,
        small_grads,
        new_tiles,
        new_tiles.astype(jnp.bfloat16),
        new_first,
        new_second,
        new_small,
        new_small.astype(jnp.bfloat16),
        new_small_first,
        new_small_second,
        factors,
    )


def solution(mesh):
    in_specs = (
        P(("dp", "seq"), None),
        P("dp", "seq"),
        P(("dp", "seq"), None),
        P(),
        P(("dp", "seq"), None, None),
        P(("dp", "seq"), None, None),
        P(("dp", "seq"), None, None),
        P(("dp", "seq"), None, None),
        P(("dp", "seq"), None, None),
        P(("dp", "seq")),
        P(("dp", "seq")),
        P(("dp", "seq")),
        P(),
    )
    out_specs = (
        P(("dp", "seq"), None),
        P(("dp", "seq"), None),
        P(("dp", "seq"), None, None),
        P(("dp", "seq")),
        P(("dp", "seq"), None, None),
        P(("dp", "seq"), None, None),
        P(("dp", "seq"), None, None),
        P(("dp", "seq"), None, None),
        P(("dp", "seq")),
        P(("dp", "seq")),
        P(("dp", "seq")),
        P(("dp", "seq")),
        P(),
    )
    return jax.shard_map(
        on_device, mesh=mesh, in_specs=in_specs, out_specs=out_specs, check_vma=False
    )
```

profile of v0, /device:TPU:16, one launch (start us, length us, event | category | flops | bytes accessed | tf_op | source)
XLA Modules:
  0.0 1813.4 jit_solution(1341632918072693743)
XLA Ops:
  13.2 37.8 %all-gather = bf16[32,1,384]{2,1,0:T(2,128)(2,1)S(1)} all-gather(bf16[1,1,384]{2,1,0:T(2,128)(2,1)S(1)} %reshape.582), channel_id=1, replica_groups=mesh['dp'=4,'seq'=8] {'dp','seq'}, dimensions={0}, use_global_device_ids=true | all-gather | bytes 25344 | tf_op jit(solution)/shard_map/all_gather | solution.py:170
  68.4 98.4 %all-gather.3.cloned.1.call-done = bf16[768,128,128]{2,1,0:T(8,128)(2,1)} async-done(((bf16[24,128,128]{2,1,0:T(8,128)(2,1)}), bf16[768,128,128]{2,1,0:T(8,128)(2,1)}) %all-gather.3.cloned.1.call-update) | async-done | bytes 25165840 | tf_op jit(solution)/shard_map/all_gather | solution.py:169
  166.8 27.4 %gather_fusion = bf16[768,128,128]{2,1,0:T(8,128)(2,1)} fusion(bf16[768,128,128]{2,1,0:T(8,128)(2,1)} %all-gather.3.cloned.1.call-done, s32[1024]{0:T(1024)S(1)} %pad_clamp_fusion.1), kind=kCustom, calls=%fused_computation | custom fusion | bytes 50334720 | tf_op jit(solution)/shard_map/gather | solution.py:172
  298.3 52.4 %multiply_convert_fusion.1 = (bf16[1024,4096]{1,0:T(8,128)(2,1)}, f32[1024,4096]{1,0:T(8,128)}, f32[1024,4096]{1,0:T(8,128)}) fusion(f32[4096]{0:T(1024)S(1)} %add.401, bf16[128,8,32,128]{3,2,1,0:T(8,128)(2,1)} %bitcast.229, bf16[1024,1024]{1,0:T(8,128)(2,1)S(1)} %copy-done.4, f32[1024]{0:T(1024)S(1)} %get-tuple-element.573, ...), kind=kOutput, calls=%fused_computation.75 | convolution fusion | flops 8873050112 | bytes 52461568 | tf_op jit(solution)/shard_map/dot_general | solution.py:239
  350.7 24.6 %convert_reduce_fusion = (f32[4096]{0:T(1024)}, bf16[1024,4096]{1,0:T(8,128)(2,1)}) fusion(f32[1024,4096]{1,0:T(8,128)} %get-tuple-element.644, bf16[1024,1024]{1,0:T(8,128)(2,1)S(1)} %copy-done.18, bf16[512,8,8,128]{3,2,1,0:T(8,128)(2,1)} %bitcast.227, f32[1024,4096]{1,0:T(8,128)} %get-tuple-element.677, f32[4096]{0:T(1024)S(1)} %add.401), kind=kOutput, calls=%fused_computation.74 | convolution fusion | flops 8661233664 | bytes 52461568 | tf_op jit(solution)/shard_map/dot_general | solution.py:252
  407.1 157.5 %while.36 = (s32[]{:T(128)}, bf16[2,512,16,64]{1,3,2,0:T(8,128)(2,1)}, f32[2,16,512,1]{2,1,3,0:T(8,128)S(1)}, f32[2,16]{1,0:T(2,128)}, s32[2]{0:T(128)S(1)}, /*i...) while((s32[]{:T(128)}, ...), condition=%wide.region_7.8_spmd, body=%wide.region_3.7_spmd.sunk | while | flops 3390826496 | bytes 162842064 | solution.py:235
  573.2 589.6 %while.37 = (s32[]{:T(128)}, f32[2048,16,64]{0,2,1:T(8,128)}, f32[2048,16,64]{0,2,1:T(8,128)}, f32[2,512,16,64]{1,0,3,2:T(2,128)}, s32[2]{0:T(128)S(1)}, /*index...) while((s32[]{:T(128)}, f32[2048,16,64]{0,2,1:T(8,128)}, ...), condition=%wide.region_10.11_spmd, body=%wide.region_8.10_spmd.sunk | while | flops 8252549120 | bytes 463750464 | solution.py:304
  617.9 27.1 %bitcast_add_fusion.7 = f32[1536,16,64]{0,2,1:T(8,128)} fusion(f32[2048,16,64]{0,2,1:T(8,128)} %get-tuple-element.930, s32[]{:T(128)S(6)} %select_n.179, f32[16,512,1536]{2,1,0:T(8,128)} %fusion.201, f32[16,512]{1,0:T(8,128)S(1)} %dynamic-slice_bitcast_fusion.2, pred[512,1536]{1,0:T(8,128)(4,1)S(1)} %fusion.202, ...), kind=kOutput, calls=%fused_computation.34.clone.1 | convolution fusion | flops 1662517248 | bytes 64782344 | tf_op jit(solution)/shard_map/while/body/eval_jaxpr/hqk,qhd->khd/dot_general | solution.py:267
  645.0 37.4 %dynamic_update_slice.70 = f32[2048,16,64]{0,2,1:T(8,128)} dynamic-update-slice(f32[2048,16,64]{0,2,1:T(8,128)} %get-tuple-element.930, f32[1536,16,64]{0,2,1:T(8,128)} %bitcast_add_fusion.7, s32[]{:T(128)S(6)} %select_n.179, s32[]{:T(128)} %constant.266.clone.1..sunk.1, s32[]{:T(128)} %constant.266.clone.1..sunk.1) | dynamic-update-slice | bytes 12582916 | tf_op jit(solution)/shard_map/while/body/eval_jaxpr/dynamic_update_slice | solution.py:295
  682.5 38.1 %multiply_reduce_fusion.2 = (f32[16,512]{1,0:T(8,128)S(1)}, f32[16,512,1536]{2,1,0:T(8,128)}) fusion(f32[16,512,1536]{2,1,0:T(8,128)} %fusion.201, f32[16,512]{1,0:T(8,128)S(1)} %dynamic-slice_bitcast_fusion.2, pred[512,1536]{1,0:T(8,128)(4,1)S(1)} %fusion.202, bf16[2048,16,64]{0,2,1:T(8,128)(2,1)} %get-tuple-element.959, s32[]{:T(128)S(6)} %select_n.179, ...), kind=kOutput, calls=%fused_computation.29.clone.1 | convolution fusion | flops 1673519104 | bytes 105709576 | tf_op jit(solution)/shard_map/while/body/eval_jaxpr/qhd,khd->hqk/dot_general | solution.py:273
  720.6 41.0 %multiply_convert_fusion.3 = bf16[16,512,1536]{2,1,0:T(8,128)(2,1)} fusion(f32[16,512,1536]{2,1,0:T(8,128)} %get-tuple-element.860, f32[16,512,1536]{2,1,0:T(8,128)} %fusion.201, f32[16,512]{1,0:T(8,128)S(1)} %get-tuple-element.861, f32[16,512]{1,0:T(8,128)S(1)} %dynamic-slice_bitcast_fusion.2, pred[512,1536]{1,0:T(8,128)(4,1)S(1)} %fusion.202), kind=kLoop, calls=%fused_computation.28.clone.1 | loop fusion | flops 75497472 | bytes 126681088 | tf_op jit(solution)/shard_map/while/body/eval_jaxpr/convert_element_type | solution.py:279
  797.6 38.0 %dynamic_update_slice.71 = f32[2,512,16,64]{1,0,3,2:T(2,128)} dynamic-update-slice(f32[2,512,16,64]{1,0,3,2:T(2,128)} %get-tuple-element.931, f32[1,512,16,64]{1,0,3,2:T(1,128)} %copy.176, s32[]{:T(128)S(6)} %copy.199, s32[]{:T(128)} %constant.266.clone.1..sunk.1, s32[]{:T(128)} %constant.266.clone.1..sunk.1, s32[]{:T(128)} %constant.266.clone.1..sunk.1) | dynamic-update-slice | bytes 4194308 | tf_op jit(solution)/shard_map/while/body/jit(dynamic_update_index_in_dim)/dynamic_update_slice | solution.py:304
  835.6 37.5 %dynamic_update_slice.69 = f32[2048,16,64]{0,2,1:T(8,128)} dynamic-update-slice(f32[2048,16,64]{0,2,1:T(8,128)} %get-tuple-element.929, f32[1536,16,64]{0,2,1:T(8,128)} %bitcast_add_fusion.6, s32[]{:T(128)S(6)} %select_n.179, s32[]{:T(128)} %constant.266.clone.1..sunk.1, s32[]{:T(128)} %constant.266.clone.1..sunk.1) | dynamic-update-slice | bytes 12582916 | tf_op jit(solution)/shard_map/while/body/eval_jaxpr/dynamic_update_slice | solution.py:289
  900.6 26.9 %bitcast_add_fusion.7 = f32[1536,16,64]{0,2,1:T(8,128)} fusion(f32[2048,16,64]{0,2,1:T(8,128)} %get-tuple-element.930, s32[]{:T(128)S(6)} %select_n.179, f32[16,512,1536]{2,1,0:T(8,128)} %fusion.201, f32[16,512]{1,0:T(8,128)S(1)} %dynamic-slice_bitcast_fusion.2, pred[512,1536]{1,0:T(8,128)(4,1)S(1)} %fusion.202, ...), kind=kOutput, calls=%fused_computation.34.clone.1 | convolution fusion | flops 1662517248 | bytes 64782344 | tf_op jit(solution)/shard_map/while/body/eval_jaxpr/hqk,qhd->khd/dot_general | solution.py:267
  927.6 36.8 %dynamic_update_slice.70 = f32[2048,16,64]{0,2,1:T(8,128)} dynamic-update-slice(f32[2048,16,64]{0,2,1:T(8,128)} %get-tuple-element.930, f32[1536,16,64]{0,2,1:T(8,128)} %bitcast_add_fusion.7, s32[]{:T(128)S(6)} %select_n.179, s32[]{:T(128)} %constant.266.clone.1..sunk.1, s32[]{:T(128)} %constant.266.clone.1..sunk.1) | dynamic-update-slice | bytes 12582916 | tf_op jit(solution)/shard_map/while/body/eval_jaxpr/dynamic_update_slice | solution.py:295
  964.4 38.1 %multiply_reduce_fusion.2 = (f32[16,512]{1,0:T(8,128)S(1)}, f32[16,512,1536]{2,1,0:T(8,128)}) fusion(f32[16,512,1536]{2,1,0:T(8,128)} %fusion.201, f32[16,512]{1,0:T(8,128)S(1)} %dynamic-slice_bitcast_fusion.2, pred[512,1536]{1,0:T(8,128)(4,1)S(1)} %fusion.202, bf16[2048,16,64]{0,2,1:T(8,128)(2,1)} %get-tuple-element.959, s32[]{:T(128)S(6)} %select_n.179, ...), kind=kOutput, calls=%fused_computation.29.clone.1 | convolution fusion | flops 1673519104 | bytes 105709576 | tf_op jit(solution)/shard_map/while/body/eval_jaxpr/qhd,khd->hqk/dot_general | solution.py:273
  1002.5 41.0 %multiply_convert_fusion.3 = bf16[16,512,1536]{2,1,0:T(8,128)(2,1)} fusion(f32[16,512,1536]{2,1,0:T(8,128)} %get-tuple-element.860, f32[16,512,1536]{2,1,0:T(8,128)} %fusion.201, f32[16,512]{1,0:T(8,128)S(1)} %get-tuple-element.861, f32[16,512]{1,0:T(8,128)S(1)} %dynamic-slice_bitcast_fusion.2, pred[512,1536]{1,0:T(8,128)(4,1)S(1)} %fusion.202), kind=kLoop, calls=%fused_computation.28.clone.1 | loop fusion | flops 75497472 | bytes 126681088 | tf_op jit(solution)/shard_map/while/body/eval_jaxpr/convert_element_type | solution.py:279
  1079.1 38.0 %dynamic_update_slice.71 = f32[2,512,16,64]{1,0,3,2:T(2,128)} dynamic-update-slice(f32[2,512,16,64]{1,0,3,2:T(2,128)} %get-tuple-element.931, f32[1,512,16,64]{1,0,3,2:T(1,128)} %copy.176, s32[]{:T(128)S(6)} %copy.199, s32[]{:T(128)} %constant.266.clone.1..sunk.1, s32[]{:T(128)} %constant.266.clone.1..sunk.1, s32[]{:T(128)} %constant.266.clone.1..sunk.1) | dynamic-update-slice | bytes 4194308 | tf_op jit(solution)/shard_map/while/body/jit(dynamic_update_index_in_dim)/dynamic_update_slice | solution.py:304
  1117.1 36.8 %dynamic_update_slice.69 = f32[2048,16,64]{0,2,1:T(8,128)} dynamic-update-slice(f32[2048,16,64]{0,2,1:T(8,128)} %get-tuple-element.929, f32[1536,16,64]{0,2,1:T(8,128)} %bitcast_add_fusion.6, s32[]{:T(128)S(6)} %select_n.179, s32[]{:T(128)} %constant.266.clone.1..sunk.1, s32[]{:T(128)} %constant.266.clone.1..sunk.1) | dynamic-update-slice | bytes 12582916 | tf_op jit(solution)/shard_map/while/body/eval_jaxpr/dynamic_update_slice | solution.py:289
  1290.3 34.9 %pad_maximum_fusion = f32[768,128,128]{2,1,0:T(8,128)} fusion(f32[256,128,128]{2,1,0:T(8,128)} %bitcast.213, f32[256,128,128]{2,1,0:T(8,128)} %bitcast.212, f32[64,128,128]{2,1,0:T(8,128)} %bitcast.241, f32[192,128,128]{2,1,0:T(8,128)} %bitcast.214), kind=kLoop, calls=%fused_computation.62 | loop fusion | flops 37748736 | bytes 100663296 | tf_op jit(solution)/shard_map/concatenate | solution.py:352
  1325.1 35.3 %gather_fusion.1 = f32[768,128,128]{2,1,0:T(8,128)} fusion(f32[768,128,128]{2,1,0:T(8,128)} %pad_maximum_fusion, s32[1024]{0:T(1024)S(1)} %copy-done.45), kind=kCustom, calls=%fused_computation.1 | custom fusion | bytes 100666368 | tf_op jit(solution)/shard_map/gather | solution.py:355
  1379.5 39.5 %pmax.7 = f32[16]{0:T(128)S(1)} all-reduce(f32[16]{0:T(128)S(1)} %reduce_max.39), channel_id=1, replica_groups=mesh['dp'=4,'seq'=8] {'dp','seq'}, use_global_device_ids=true, to_apply=%region_24.25 | all-reduce | flops 16 | bytes 128 | tf_op jit(solution)/shard_map/pmax | solution.py:237
  1489.4 44.1 %all-reduce = f32[12288]{0:T(1024)S(1)} all-reduce(f32[12288]{0:T(1024)S(1)} %reshape.561), channel_id=3, replica_groups=mesh['dp'=4,'seq'=8] {'dp','seq'}, use_global_device_ids=true, to_apply=%region_22.23.clone | all-reduce | flops 12288 | bytes 98304
  1534.2 258.0 %reduce-scatter.2.cloned.1.call-done = f32[24,128,128]{2,1,0:T(8,128)} async-done(((f32[768,128,128]{2,1,0:T(8,128)}), f32[24,128,128]{2,1,0:T(8,128)}) %reduce-scatter.2.cloned.1.call-update) | async-done | bytes 1572880 | tf_op jit(solution)/shard_map/reduce_scatter | solution.py:371
  (308 shorter events, 666.7 us)
Async XLA Ops:
  7.2 1789.7 %copy-start = (f32[24,128,128]{2,1,0:T(8,128)S(1)}, f32[24,128,128]{2,1,0:T(8,128)}, u32[]{:S(2)}) copy-start(f32[24,128,128]{2,1,0:T(8,128)} %param.23) | copy-start | bytes 4718596
  7.2 159.7 %all-gather.3.cloned.1.call-start = ((), (), s32[]{:S(2)}) async-start(), calls=%async_computation.1 | async-start | bytes 25952256 | tf_op jit(solution)/shard_map/all_gather | solution.py:169
  9.8 1782.4 %reduce-scatter.2.cloned.1.call-start = ((), (), s32[]{:S(2)}) async-start(), calls=%async_computation.2 | async-start | bytes 51904512 | tf_op jit(solution)/shard_map/reduce_scatter | solution.py:371
  10.5 57.3 %collective-permute-start.1 = (bf16[1024]{0:T(1024)(128)(2,1)S(1)}, bf16[1024]{0:T(1024)(128)(2,1)S(1)}, u32[]{:S(2)}, u32[]{:S(2)}) collective-permute-start(bf16[1024]{0:T(1024)(128)(2,1)S(1)} %convert_element_type.124), channel_id=1, source_target_pairs={{0,1},{1,2},{2,3},{3,4},{4,5},{5,6},{6,7},{8,9},{9,10},{10,11},{11... | collective-permute-start | bytes 6152 | tf_op jit(solution)/shard_map/ppermute | solution.py:29
  60.9 150.3 %copy-start.51 = (f32[1024]{0:T(1024)}, f32[1024]{0:T(1024)S(1)}, u32[]{:S(2)}) copy-start(f32[1024]{0:T(1024)S(1)} %get-tuple-element.578) | copy-start | bytes 12292
  60.9 150.3 %copy-start.55 = (f32[1024]{0:T(1024)}, f32[1024]{0:T(1024)S(1)}, u32[]{:S(2)}) copy-start(f32[1024]{0:T(1024)S(1)} %get-tuple-element.577) | copy-start | bytes 12292
  60.9 237.4 %copy-start.48 = (f32[1024]{0:T(1024)}, f32[1024]{0:T(1024)S(1)}, u32[]{:S(2)}) copy-start(f32[1024]{0:T(1024)S(1)} %get-tuple-element.574) | copy-start | bytes 12292
  60.9 237.4 %copy-start.57 = (f32[1024]{0:T(1024)}, f32[1024]{0:T(1024)S(1)}, u32[]{:S(2)}) copy-start(f32[1024]{0:T(1024)S(1)} %get-tuple-element.573) | copy-start | bytes 12292
  61.3 237.0 %copy-start.41 = (f32[1024]{0:T(1024)}, f32[1024]{0:T(1024)S(1)}, u32[]{:S(2)}) copy-start(f32[1024]{0:T(1024)S(1)} %broadcast_multiply_fusion.3) | copy-start | bytes 12292
  62.0 236.2 %copy-start.43 = (f32[1024]{0:T(1024)}, f32[1024]{0:T(1024)S(1)}, u32[]{:S(2)}) copy-start(f32[1024]{0:T(1024)S(1)} %add_rsqrt_fusion) | copy-start | bytes 12292
  62.8 229.5 %copy-start.36 = (f32[1024,8]{0,1:T(8,128)}, f32[1024,8]{0,1:T(8,128)S(1)}, u32[]{:S(2)}) copy-start(f32[1024,8]{0,1:T(8,128)S(1)} %get-tuple-element.676) | copy-start | bytes 98308
  281.6 110.1 %collective-permute-start = (bf16[1024,1024]{1,0:T(8,128)(2,1)}, bf16[1024,1024]{1,0:T(8,128)(2,1)}, u32[]{:S(2)}, u32[]{:S(2)}) collective-permute-start(bf16[1024,1024]{1,0:T(8,128)(2,1)} %slice.220), channel_id=1, source_target_pairs={{0,1},{1,2},{2,3},{3,4},{4,5},{5,6},{6,7},{8,9},{9,10},{10,11},{11... | collective-permute-start | bytes 6291464 | tf_op jit(solution)/shard_map/ppermute | solution.py:29
  296.0 106.2 %collective-permute-start.2 = (bf16[1024,1024]{0,1:T(8,128)(2,1)}, bf16[1024,1024]{0,1:T(8,128)(2,1)}, u32[]{:S(2)}, u32[]{:S(2)}) collective-permute-start(bf16[1024,1024]{0,1:T(8,128)(2,1)} %bitcast.17), channel_id=1, source_target_pairs={{0,1},{1,2},{2,3},{3,4},{4,5},{5,6},{6,7},{8,9},{9,10},{10,11},{11... | collective-permute-start | bytes 6291464 | tf_op jit(solution)/shard_map/ppermute | solution.py:29
  298.3 52.4 %copy-start.18 = (bf16[1024,1024]{1,0:T(8,128)(2,1)S(1)}, bf16[1024,1024]{1,0:T(8,128)(2,1)}, u32[]{:S(2)}) copy-start(bf16[1024,1024]{1,0:T(8,128)(2,1)} %param.19) | copy-start | bytes 6291460
  350.7 24.6 %copy-start.22 = (bf16[1024,16,48]{0,2,1:T(8,128)(2,1)S(1)}, bf16[1024,16,48]{0,2,1:T(8,128)(2,1)}, u32[]{:S(2)}) copy-start(bf16[1024,16,48]{0,2,1:T(8,128)(2,1)} %slice.224) | copy-start | bytes 4718596
  1170.6 77.1 %collective-permute-start.4 = (bf16[1024,1024]{0,1:T(8,128)(2,1)}, bf16[1024,1024]{0,1:T(8,128)(2,1)}, u32[]{:S(2)}, u32[]{:S(2)}) collective-permute-start(bf16[1024,1024]{0,1:T(8,128)(2,1)} %bitcast.33), channel_id=1, source_target_pairs={{1,0},{2,1},{3,2},{4,3},{5,4},{6,5},{7,6},{9,8},{10,9},{11,10},{12... | collective-permute-start | bytes 6291464 | tf_op jit(solution)/shard_map/ppermute | solution.py:29
  1174.0 68.5 %collective-permute-start.3 = (bf16[1024,1024]{0,1:T(8,128)(2,1)}, bf16[1024,1024]{0,1:T(8,128)(2,1)}, u32[]{:S(2)}, u32[]{:S(2)}) collective-permute-start(bf16[1024,1024]{0,1:T(8,128)(2,1)} %bitcast.29), channel_id=1, source_target_pairs={{1,0},{2,1},{3,2},{4,3},{5,4},{6,5},{7,6},{9,8},{10,9},{11,10},{12... | collective-permute-start | bytes 6291464 | tf_op jit(solution)/shard_map/ppermute | solution.py:29
  1203.5 18.3 %slice-start = ((s8[8388608]{0:T(1024)(128)(4,1)}), s8[4194304]{0:T(1024)(128)(4,1)S(1)}, s32[]{:S(2)}) async-start(s8[8388608]{0:T(1024)(128)(4,1)} %bitcast.205), calls=%async_computation.3 | async-start | bytes 8388608
  1203.5 20.5 %slice-start.4 = ((s8[8388608]{0:T(1024)(128)(4,1)}), s8[4194304]{0:T(1024)(128)(4,1)S(1)}, s32[]{:S(2)}) async-start(s8[8388608]{0:T(1024)(128)(4,1)} %bitcast.218), calls=%async_computation.7 | async-start | bytes 8388608
  1290.3 34.9 %copy-start.45 = (s32[1024]{0:T(1024)S(1)}, s32[1024]{0:T(1024)}, u32[]{:S(2)}) copy-start(s32[1024]{0:T(1024)} %pad_clamp_fusion) | copy-start | bytes 12292
  1478.7 54.8 %copy-start.47 = (f32[384]{0:T(512)S(1)}, f32[384]{0:T(512)}, u32[]{:S(2)}) copy-start(f32[384]{0:T(512)} %param.26) | copy-start | bytes 4612
  1478.7 54.8 %copy-start.59 = (f32[384]{0:T(512)S(1)}, f32[384]{0:T(512)}, u32[]{:S(2)}) copy-start(f32[384]{0:T(512)} %param.27) | copy-start | bytes 4612
  1478.7 54.8 %copy-start.60 = (f32[384]{0:T(512)S(1)}, f32[384]{0:T(512)}, u32[]{:S(2)}) copy-start(f32[384]{0:T(512)} %param.28) | copy-start | bytes 4612
  1487.9 309.1 %copy-start.28 = (f32[24,128,128]{2,1,0:T(8,128)S(1)}, f32[24,128,128]{2,1,0:T(8,128)}, u32[]{:S(2)}) copy-start(f32[24,128,128]{2,1,0:T(8,128)} %param.25) | copy-start | bytes 4718596
  (53 other events, 420.6 us)
Sparse Core Ops, SparseCore 0:
  11.6 155.1 all-gather.2
  1360.6 431.6 reduce-scatter.1
where the time goes:
time: 1840 us; the launch traced here: 1810 us
  matrix products  530 us (29%)
  local copies, waits for them, and re-layouts  507 us (28%)
  waiting for transfers between devices  356 us (19%)
  other arithmetic  229 us (12%)
  blocking collectives  121 us (7%)
  loops' own time  41.7 us (2%)
    reduce_scatter x1, waiting for transfers between devices, on_device(): lax.psum_scatter(slot_grads, ('dp', 'seq'), scatter_dimension=0, tiled=True)  258 us
    all_gather x1, waiting for transfers between devices, collect(): lax.all_gather(tiles_low, ('dp', 'seq'), axis=0, tiled=True)  98.4 us
    dot_general x4, matrix products, block_scores(): jnp.einsum('qhd,khd->hqk', query_block, key_block, preferred_element_type...  89.7 us
    dynamic_update_slice x4, local copies, waits for them, and re-layouts, on_device(): lax.scan(backward_block, (zero_heads, zero_heads), (block_starts, log_sums))  83 us
    convert_element_type x2, other arithmetic, backward_block(): grad_scores = grad_scores.astype(jnp.bfloat16)  82 us
    dot_general x2, matrix products, backward_block(): jnp.einsum('qhd,khd->hqk', grad_out_block, value_block, preferred_element...  76.2 us
    dynamic_update_slice x2, local copies, waits for them, and re-layouts, backward_block(): lax.dynamic_update_slice_in_dim(grad_keys_all, lax.dynamic_slice_in_dim(g...  74.3 us
    dynamic_update_slice x2, local copies, waits for them, and re-layouts, backward_block(): lax.dynamic_update_slice_in_dim(grad_values_all, lax.dynamic_slice_in_dim...  74.3 us
  transfers between devices with their start and end apart: 7, of which 2 were waited for; matrix products, arithmetic and copies ran while one was open for 16% of the time, Pallas kernels for 0%

commit v1 on v0

v1 whole, which is shorter than its diff:
```python
import functools

import jax
import jax.numpy as jnp
from jax import lax
from jax.experimental import pallas as pl
from jax.experimental.pallas import tpu as pltpu
from jax.sharding import PartitionSpec as P

D = 1024
FF = 4096
HEADS = 16
HEAD = 64
ROT = 16
BLK = 128
WINDOW = 1024
TILES = 768
SMALL = 12288
QKV_TILES = D // BLK * (3 * D // BLK)
OUT_TILES = D // BLK * (D // BLK)
UP_TILES = D // BLK * (FF // BLK)
OUT_BASE = QKV_TILES
UP_BASE = QKV_TILES + OUT_TILES
DOWN_BASE = UP_BASE + UP_TILES

NORM_EPS = 1e-05
ADAM_EPS = 1e-08
BETA = 0.5
LEARN = 0.03
SMALL_LEARN = 0.2
ROPE_BASE = 10000.0
MASKED = -1e30
HIGH = lax.Precision.HIGHEST

F32 = jnp.float32
BF16 = jnp.bfloat16
MESH = pl.DeviceIdType.MESH
ANY = pl.BlockSpec(memory_space=pl.ANY)
VMEM = pl.BlockSpec(memory_space=pltpu.VMEM)
VMEM_LIMIT = 58 << 20

NN = (((1,), (0,)), ((), ()))
NT = (((1,), (1,)), ((), ()))
TN = (((0,), (0,)), ((), ()))


def dot(a, b, dims=NN, precision=None):
    return lax.dot_general(a, b, dims, precision=precision, preferred_element_type=F32)


def params(**kw):
    return pltpu.CompilerParams(vmem_limit_bytes=VMEM_LIMIT, **kw)


def norm_rows(x):
    centered = x - jnp.mean(x, axis=-1, keepdims=True)
    inv = lax.rsqrt(jnp.mean(centered * centered, axis=-1, keepdims=True) + NORM_EPS)
    return centered * inv, inv


def tile_loop(first, count, body):
    def step(t, carry):
        body(t)
        return carry

    lax.fori_loop(first, first + count, step, 0)


ROWS_PER_TILE = BLK
HALF_ROWS = 1536


def gather_weights(payload, tokens, seg_rows):
    rows = payload.shape[0]
    top = pl.ds(0, HALF_ROWS)
    low = pl.ds(HALF_ROWS, rows - HALF_ROWS)

    def kernel(x_ref, tok_ref, seg_ref, out_ref, ptok_ref, pseg_ref, lsem, ss, rs, hss, hrs, hls):
        d = lax.axis_index("dp")
        s = lax.axis_index("seq")
        z = s // 2
        c = s % 2
        xn = d + 1 - 2 * (d % 2)
        yn = d + 2 - 4 * (d // 2)
        xyn = 3 - d
        sib = z * 2 + 1 - c
        halo = s - 1 + 2 * c
        halo_ok = ((c == 0) & (z > 0)) | ((c == 1) & (z < 3))

        barrier = pltpu.get_barrier_semaphore()

        def greet(dev):
            pl.semaphore_signal(barrier, inc=1, device_id=dev, device_id_type=MESH)

        greet((d, sib))
        greet((xn, s))
        greet((yn, s))

        @pl.when(z > 0)
        def _():
            greet((d, s - 2))

        @pl.when(z < 3)
        def _():
            greet((d, s + 2))

        @pl.when(halo_ok)
        def _():
            greet((d, halo))

        below, above = (z + 2) // 3, (5 - z) // 3
        pl.semaphore_wait(barrier, 3 + below + above + (1 - c) * below + c * above)

        def place(dd, zz):
            return out_ref.at[dd * 8 + zz * 2 + c]

        def remote(src, dst, kind, zz, dev):
            return pltpu.make_async_remote_copy(
                src_ref=src,
                dst_ref=dst,
                send_sem=ss.at[kind, zz],
                recv_sem=rs.at[kind, zz],
                device_id=dev,
                device_id_type=MESH,
            )

        def block_of(zz, own):
            return x_ref if own else place(d, zz)

        def up(zz, own):
            return remote(block_of(zz, own), place(d, zz), 0, zz, (d, s + 2))

        def down(zz, own):
            return remote(block_of(zz, own), place(d, zz), 1, zz, (d, s - 2))

        def to_x(zz, own):
            return remote(block_of(zz, own), place(d, zz), 2, zz, (xn, s))

        def to_y(zz, own):
            return remote(block_of(zz, own), place(d, zz), 3, zz, (yn, s))

        def on_y(zz):
            return remote(place(xn, zz).at[top], place(xn, zz).at[top], 4, zz, (yn, s))

        def on_x(zz):
            return remote(place(yn, zz).at[low], place(yn, zz).at[low], 5, zz, (xn, s))

        def to_sib(dd, zz, kind, own=False):
            src = x_ref if own else place(dd, zz)
            return remote(src, place(dd, zz), kind, zz, (d, sib))

        def from_x(zz):
            return remote(x_ref, place(xn, zz), 2, zz, (xn, s))

        def from_y(zz):
            return remote(x_ref, place(yn, zz), 3, zz, (yn, s))

        def diag_top(zz):
            return remote(x_ref.at[top], place(xyn, zz).at[top], 4, zz, (yn, s))

        def diag_low(zz):
            return remote(x_ref.at[low], place(xyn, zz).at[low], 5, zz, (xn, s))

        order = [z, 1 + z % 2, (2 + 3 * z) % 5, 3 * (1 - z // 2)]
        local = pltpu.make_async_copy(x_ref, place(d, z), lsem)
        local.start()

        def halo_copies(dev):
            tok = pltpu.make_async_remote_copy(
                src_ref=tok_ref,
                dst_ref=ptok_ref,
                send_sem=hss.at[0],
                recv_sem=hrs.at[0],
                device_id=dev,
                device_id_type=MESH,
            )
            seg = pltpu.make_async_remote_copy(
                src_ref=seg_ref,
                dst_ref=pseg_ref,
                send_sem=hss.at[1],
                recv_sem=hrs.at[1],
                device_id=dev,
                device_id_type=MESH,
            )
            return tok, seg

        def launch(k):
            zz = order[k]
            own = k == 0
            if own:

                @pl.when(z < 3)
                def _():
                    up(zz, True).start()

                @pl.when(z > 0)
                def _():
                    down(zz, True).start()
            else:

                @pl.when(zz < z)
                def _():
                    up(zz, False).wait_recv()

                @pl.when((zz < z) & (z < 3))
                def _():
                    up(zz, False).start()

                @pl.when(zz > z)
                def _():
                    down(zz, False).wait_recv()

                @pl.when((zz > z) & (z > 0))
                def _():
                    down(zz, False).start()

            to_x(zz, own).start()
            to_y(zz, own).start()
            to_sib(d, zz, 6, own).start()

        def second(k):
            zz = order[k]
            from_x(zz).wait_recv()
            on_y(zz).start()
            to_sib(xn, zz, 7).start()
            from_y(zz).wait_recv()
            on_x(zz).start()
            to_sib(yn, zz, 8).start()

        def third(k):
            zz = order[k]
            diag_top(zz).wait_recv()
            diag_low(zz).wait_recv()
            to_sib(xyn, zz, 9).start()

        launch(0)
        own_tok = pltpu.make_async_copy(tok_ref, ptok_ref, hls.at[0])
        own_seg = pltpu.make_async_copy(seg_ref, pseg_ref, hls.at[1])

        @pl.when(s < 7)
        def _():
            for cp in halo_copies((d, s + 1)):
                cp.start()

        @pl.when(s == 0)
        def _():
            own_tok.start()
            own_seg.start()

        launch(1)
        second(0)
        launch(2)
        second(1)
        third(0)
        launch(3)
        second(2)
        third(1)
        second(3)
        third(2)
        third(3)

        local.wait()
        other = 1 - c

        def sib_place(dd, zz):
            return out_ref.at[dd * 8 + zz * 2 + other]

        for k in range(4):
            zz = order[k]
            own = k == 0
            for kind, dd in ((6, d), (7, xn), (8, yn), (9, xyn)):
                remote(sib_place(dd, zz), sib_place(dd, zz), kind, zz, (d, sib)).wait_recv()
                to_sib(dd, zz, kind, own and kind == 6).wait_send()
            to_x(zz, own).wait_send()
            to_y(zz, own).wait_send()
            on_y(zz).wait_send()
            on_x(zz).wait_send()

            @pl.when((zz <= z) & (z < 3))
            def _():
                up(zz, own).wait_send()

            @pl.when((zz >= z) & (z > 0))
            def _():
                down(zz, own).wait_send()

        @pl.when(s < 7)
        def _():
            for cp in halo_copies((d, s + 1)):
                cp.wait_send()

        @pl.when(s > 0)
        def _():
            for cp in halo_copies((d, s - 1)):
                cp.wait_recv()

        @pl.when(s == 0)
        def _():
            own_tok.wait()
            own_seg.wait()

    return pl.pallas_call(
        kernel,
        out_shape=[
            jax.ShapeDtypeStruct((32, rows, BLK), BF16),
            jax.ShapeDtypeStruct(tokens.shape, BF16),
            jax.ShapeDtypeStruct(seg_rows.shape, jnp.int32),
        ],
        in_specs=[ANY, ANY, ANY],
        out_specs=[ANY, ANY, ANY],
        scratch_shapes=[
            pltpu.SemaphoreType.DMA,
            pltpu.SemaphoreType.DMA((10, 4)),
            pltpu.SemaphoreType.DMA((10, 4)),
            pltpu.SemaphoreType.DMA((2,)),
            pltpu.SemaphoreType.DMA((2,)),
            pltpu.SemaphoreType.DMA((2,)),
        ],
        compiler_params=params(collective_id=0, has_side_effects=True),
        name="gather_weights",
    )(payload, tokens, seg_rows)


OWNED = 24 * BLK
HALF = OWNED // 2
SMALL_ROWS = SMALL // BLK
EXTRA_ROWS = SMALL_ROWS + 8


def add_rows(dst, terms, rows, step=256):
    def body(i, carry):
        at = pl.ds(pl.multiple_of(i * step, step), step)
        total = terms[0][at].astype(F32)
        for term in terms[1:]:
            total = total + term[at].astype(F32)
        dst[at] = total.astype(dst.dtype)
        return carry

    lax.fori_loop(0, rows // step, body, 0)


def sum_gradients(grads, extra):
    def kernel(g_ref, e_ref, out_ref, eout_ref, own, crecv, s1a, s1b, s2, zup, zdn, epart, erecv, ls, ss, rs, zss, zrs, es, er):
        d = lax.axis_index("dp")
        s = lax.axis_index("seq")
        z = s // 2
        c = s % 2
        xn = d + 1 - 2 * (d % 2)
        yn = d + 2 - 4 * (d // 2)
        xyn = 3 - d
        sib = z * 2 + 1 - c
        zpair = s + 2 - 4 * (z % 2)
        zfar = s + 4 - 8 * (z // 2)
        top = pl.ds(0, HALF)
        low = pl.ds(HALF, HALF)

        barrier = pltpu.get_barrier_semaphore()

        def greet(dev):
            pl.semaphore_signal(barrier, inc=1, device_id=dev, device_id_type=MESH)

        greet((d, sib))
        greet((xn, s))
        greet((yn, s))
        greet((d, zfar))

        @pl.when(z > 0)
        def _():
            greet((d, s - 2))

        @pl.when(z < 3)
        def _():
            greet((d, s + 2))

        order = [3 * (1 - z // 2), (2 + 3 * z) % 5, 1 + z % 2, z]

        def owner_rows(dd, zz, cc):
            return g_ref.at[pl.ds(pl.multiple_of((dd * 8 + zz * 2 + cc) * OWNED, OWNED), OWNED)]

        def load(zz, dd):
            return pltpu.make_async_copy(owner_rows(dd, zz, c), own.at[zz, dd], ls.at[zz, dd])

        for k in range(4):
            for dd in range(4):
                load(order[k], dd).start()

        pl.semaphore_wait(barrier, 4 + (z + 2) // 3 + (5 - z) // 3)

        def remote(src, dst, ssem, rsem, dev):
            return pltpu.make_async_remote_copy(
                src_ref=src, dst_ref=dst, send_sem=ssem, recv_sem=rsem, device_id=dev, device_id_type=MESH
            )

        def core(zz, dd):
            return remote(owner_rows(dd, zz, 1 - c), crecv.at[zz, dd], ss.at[zz, dd], rs.at[zz, dd], (d, sib))

        def y_own(zz):
            return remote(own.at[zz, yn, top], s1a.at[zz, 0], ss.at[zz, 4], rs.at[zz, 4], (yn, s))

        def y_cross(zz):
            return remote(own.at[zz, xyn, top], s1a.at[zz, 1], ss.at[zz, 5], rs.at[zz, 5], (yn, s))

        def x_own(zz):
            return remote(own.at[zz, xn, low], s1b.at[zz, 0], ss.at[zz, 6], rs.at[zz, 6], (xn, s))

        def x_cross(zz):
            return remote(own.at[zz, xyn, low], s1b.at[zz, 1], ss.at[zz, 7], rs.at[zz, 7], (xn, s))

        def x_last(zz):
            return remote(own.at[zz, xn, top], s2.at[zz, top], ss.at[zz, 8], rs.at[zz, 8], (xn, s))

        def y_last(zz):
            return remote(own.at[zz, yn, low], s2.at[zz, low], ss.at[zz, 9], rs.at[zz, 9], (yn, s))

        def z_up(zz):
            return remote(own.at[zz, d], zup.at[zz], zss.at[0, zz], zrs.at[0, zz], (d, s + 2))

        def z_dn(zz):
            return remote(own.at[zz, d], zdn.at[zz], zss.at[1, zz], zrs.at[1, zz], (d, s - 2))

        def extra_step(i, dev):
            return remote(epart.at[i], erecv.at[i], es.at[i], er.at[i], dev)

        extra_devs = [(d, sib), (xn, s), (yn, s), (d, zpair), (d, zfar)]

        def extra_add(i):
            extra_step(i, extra_devs[i]).wait_recv()
            a = epart[i]
            b = erecv[i]
            row = lax.broadcasted_iota(jnp.int32, a.shape, 0)
            total = jnp.where(row < SMALL_ROWS, a + b, jnp.maximum(a, b))
            if i < 4:
                epart[i + 1] = total
                extra_step(i + 1, extra_devs[i + 1]).start()
            else:
                eout_ref[...] = total

        for k in range(4):
            for dd in range(4):
                core(order[k], dd).start()
            if k == 0:
                epart[0] = e_ref[...]
                extra_step(0, extra_devs[0]).start()

        def first(k):
            zz = order[k]

            def one(dd, start):
                load(zz, dd).wait()
                core(zz, dd).wait_recv()
                add_rows(own.at[zz, dd], [own.at[zz, dd], crecv.at[zz, dd]], OWNED)
                for cp in start:
                    cp.start()

            one(xyn, [y_cross(zz), x_cross(zz)])
            one(yn, [y_own(zz)])
            one(xn, [x_own(zz)])
            one(d, [])

        def second(k):
            zz = order[k]
            y_cross(zz).wait_recv()
            a = own.at[zz, xn, top]
            add_rows(a, [a, s1a.at[zz, 1]], HALF)
            x_last(zz).start()
            x_cross(zz).wait_recv()
            b = own.at[zz, yn, low]
            add_rows(b, [b, s1b.at[zz, 1]], HALF)
            y_last(zz).start()

        def third(k):
            zz = order[k]
            y_own(zz).wait_recv()
            x_own(zz).wait_recv()
            x_last(zz).wait_recv()
            y_last(zz).wait_recv()
            a = own.at[zz, d, top]
            b = own.at[zz, d, low]
            if k < 3:

                @pl.when((zz > z) & (z > 0))
                def _():
                    z_up(zz).wait_recv()
                    add_rows(a, [a, s1a.at[zz, 0], s2.at[zz, top], zup.at[zz, top]], HALF)
                    add_rows(b, [b, s1b.at[zz, 0], s2.at[zz, low], zup.at[zz, low]], HALF)

                @pl.when((zz < z) & (z < 3))
                def _():
                    z_dn(zz).wait_recv()
                    add_rows(a, [a, s1a.at[zz, 0], s2.at[zz, top], zdn.at[zz, top]], HALF)
                    add_rows(b, [b, s1b.at[zz, 0], s2.at[zz, low], zdn.at[zz, low]], HALF)

                @pl.when(((zz > z) & (z == 0)) | ((zz < z) & (z == 3)))
                def _():
                    add_rows(a, [a, s1a.at[zz, 0], s2.at[zz, top]], HALF)
                    add_rows(b, [b, s1b.at[zz, 0], s2.at[zz, low]], HALF)

                @pl.when(zz > z)
                def _():
                    z_up(zz).start()

                @pl.when(zz < z)
                def _():
                    z_dn(zz).start()
            else:

                @pl.when(z > 0)
                def _():
                    z_up(zz).wait_recv()

                @pl.when(z < 3)
                def _():
                    z_dn(zz).wait_recv()

                o_top = out_ref.at[top]
                o_low = out_ref.at[low]

                @pl.when((z > 0) & (z < 3))
                def _():
                    add_rows(o_top, [a, s1a.at[zz, 0], s2.at[zz, top], zup.at[zz, top], zdn.at[zz, top]], HALF)
                    add_rows(o_low, [b, s1b.at[zz, 0], s2.at[zz, low], zup.at[zz, low], zdn.at[zz, low]], HALF)

                @pl.when(z == 0)
                def _():
                    add_rows(o_top, [a, s1a.at[zz, 0], s2.at[zz, top], zdn.at[zz, top]], HALF)
                    add_rows(o_low, [b, s1b.at[zz, 0], s2.at[zz, low], zdn.at[zz, low]], HALF)

                @pl.when(z == 3)
                def _():
                    add_rows(o_top, [a, s1a.at[zz, 0], s2.at[zz, top], zup.at[zz, top]], HALF)
                    add_rows(o_low, [b, s1b.at[zz, 0], s2.at[zz, low], zup.at[zz, low]], HALF)

        first(0)
        first(1)
        extra_add(0)
        second(0)
        first(2)
        extra_add(1)
        third(0)
        second(1)
        first(3)
        extra_add(2)
        third(1)
        second(2)
        extra_add(3)
        third(2)
        second(3)
        extra_add(4)
        third(3)

        for i in range(5):
            extra_step(i, extra_devs[i]).wait_send()
        for k in range(4):
            zz = order[k]
            for dd in range(4):
                core(zz, dd).wait_send()
            for cp in (y_own(zz), y_cross(zz), x_own(zz), x_cross(zz), x_last(zz), y_last(zz)):
                cp.wait_send()
            if k < 3:

                @pl.when(zz > z)
                def _():
                    z_up(zz).wait_send()

                @pl.when(zz < z)
                def _():
                    z_dn(zz).wait_send()

    return pl.pallas_call(
        kernel,
        out_shape=[
            jax.ShapeDtypeStruct((OWNED, BLK), F32),
            jax.ShapeDtypeStruct((EXTRA_ROWS, BLK), F32),
        ],
        in_specs=[ANY, VMEM],
        out_specs=[VMEM, VMEM],
        scratch_shapes=[
            pltpu.VMEM((4, 4, OWNED, BLK), BF16),
            pltpu.VMEM((4, 4, OWNED, BLK), BF16),
            pltpu.VMEM((4, 2, HALF, BLK), BF16),
            pltpu.VMEM((4, 2, HALF, BLK), BF16),
            pltpu.VMEM((4, OWNED, BLK), BF16),
            pltpu.VMEM((4, OWNED, BLK), BF16),
            pltpu.VMEM((4, OWNED, BLK), BF16),
            pltpu.VMEM((5, EXTRA_ROWS, BLK), F32),
            pltpu.VMEM((5, EXTRA_ROWS, BLK), F32),
            pltpu.SemaphoreType.DMA((4, 4)),
            pltpu.SemaphoreType.DMA((4, 10)),
            pltpu.SemaphoreType.DMA((4, 10)),
            pltpu.SemaphoreType.DMA((2, 4)),
            pltpu.SemaphoreType.DMA((2, 4)),
            pltpu.SemaphoreType.DMA((5,)),
            pltpu.SemaphoreType.DMA((5,)),
        ],
        compiler_params=params(collective_id=1, has_side_effects=True),
        name="sum_gradients",
    )(grads, extra)


ROWB = 256


def rope_rows(value, cos_t, fwd_t, back_t):
    pieces = []
    for j in range(value.shape[1] // BLK):
        p = value[:, j * BLK : (j + 1) * BLK]
        pieces.append(
            p * cos_t + pltpu.roll(p, BLK - ROT // 2, 1) * fwd_t + pltpu.roll(p, ROT // 2, 1) * back_t
        )
    return jnp.concatenate(pieces, axis=1)


def project(w_rows, w_all, prev_tokens, tokens, cotangent, smalls, tables):
    rows = tokens.shape[0]
    steps = rows // ROWB
    cos_t, fwd_t, back_t = tables

    def kernel(
        w_rows_ref, w_ref, prev_ref, tok_ref, g_ref, small_ref, cos_ref, fwd_ref, back_ref,
        q_ref, k_ref, v_ref, do_ref, m_ref, wqkv, wo, sems,
    ):
        i = pl.program_id(0)

        def third_copy(third):
            def body(t):
                r, cc = t // 8, t % 8
                src = w_ref.at[pl.ds(pl.multiple_of(w_rows_ref[r * 24 + third * 8 + cc], 16), BLK)]
                dst = wqkv.at[pl.ds(pl.multiple_of(r * BLK, BLK), BLK), pl.ds(pl.multiple_of(third * D + cc * BLK, BLK), BLK)]
                pltpu.make_async_copy(src, dst, sems.at[third]).start()

            tile_loop(0, 64, body)

        def third_wait(third):
            part = wqkv.at[:, pl.ds(third * D, D)]
            pltpu.make_async_copy(part, part, sems.at[third]).wait()

        @pl.when(i == 0)
        def _():
            third_copy(1)
            third_copy(2)
            third_copy(0)

            def body(t):
                r, cc = t // 8, t % 8
                src = w_ref.at[pl.ds(pl.multiple_of(w_rows_ref[OUT_BASE + t], 16), BLK)]
                dst = wo.at[pl.ds(pl.multiple_of(r * BLK, BLK), BLK), pl.ds(pl.multiple_of(cc * BLK, BLK), BLK)]
                pltpu.make_async_copy(src, dst, sems.at[3]).start()

            tile_loop(0, 64, body)
            third_wait(1)
            third_wait(2)

        @pl.when(i == steps)
        def _():
            third_wait(0)
            pltpu.make_async_copy(wo, wo, sems.at[3]).wait()

        def keys(x):
            normed, _ = norm_rows(x)
            attn_in = (normed * small_ref[4:5, :] + small_ref[5:6, :]).astype(BF16)
            k = dot(attn_in, wqkv[:, D : 2 * D])
            v = dot(attn_in, wqkv[:, 2 * D :]) + small_ref[1:2, :]
            k_ref[...] = rope_rows(k, cos_ref[...], fwd_ref[...], back_ref[...]).astype(BF16)
            v_ref[...] = v.astype(BF16)
            return normed, attn_in

        @pl.when(i < steps)
        def _():
            keys(prev_ref[...].astype(F32))

        @pl.when(i >= steps)
        def _():
            normed, attn_in = keys(tok_ref[...].astype(F32))
            m_ref[...] = (normed * small_ref[6:7, :] + small_ref[7:8, :]).astype(BF16)
            q = dot(attn_in, wqkv[:, :D]) + small_ref[0:1, :]
            q = rope_rows(q, cos_ref[...], fwd_ref[...], back_ref[...])
            q_ref[...] = q.astype(BF16)
            do_ref[...] = dot(g_ref[...], wo[...], NT).astype(BF16)

    own = lambda i, *_: (jnp.maximum(i - steps, 0), 0)
    prev = lambda i, *_: (jnp.minimum(i, steps - 1), 0)
    here = lambda i, *_: (i, 0)
    block = lambda m: pl.BlockSpec((ROWB, D), m)
    table = pl.BlockSpec((ROWB, BLK), here)
    return pl.pallas_call(
        kernel,
        grid_spec=pltpu.PrefetchScalarGridSpec(
            num_scalar_prefetch=1,
            grid=(2 * steps,),
            in_specs=[
                ANY, block(prev), block(own), block(own),
                pl.BlockSpec((16, D), lambda i, *_: (0, 0)), table, table, table,
            ],
            out_specs=[block(own), block(here), block(here), block(own), block(own)],
            scratch_shapes=[
                pltpu.VMEM((D, 3 * D), BF16),
                pltpu.VMEM((D, D), BF16),
                pltpu.SemaphoreType.DMA((4,)),
            ],
        ),
        out_shape=[
            jax.ShapeDtypeStruct((rows, D), BF16),
            jax.ShapeDtypeStruct((2 * rows, D), BF16),
            jax.ShapeDtypeStruct((2 * rows, D), BF16),
            jax.ShapeDtypeStruct((rows, D), BF16),
            jax.ShapeDtypeStruct((rows, D), BF16),
        ],
        compiler_params=params(dimension_semantics=("arbitrary",)),
        name="project",
    )(w_rows, w_all, prev_tokens, tokens, cotangent, smalls, cos_t, fwd_t, back_t)


QB = 256
SPAN = WINDOW + QB


def attend(q, k, v, d_out, seg_q, seg_k, cos8, sin8):
    rows = q.shape[0]
    blocks = rows // QB
    pairs = HEADS // 2
    scale = HEAD ** (-0.5)
    half = ROT // 2

    def kernel(
        q_ref, k_ref, v_ref, do_ref, sq_ref, sk_ref, cos_ref, sin_ref,
        o_ref, dq_ref, dk_ref, dv_ref, peak_ref, bias, kt, vt,
    ):
        p = pl.program_id(0)
        i = pl.program_id(1)
        start = pl.multiple_of(i * QB, QB)
        span = pl.ds(start, SPAN)

        @pl.when(p == 0)
        def _():
            gap = (
                WINDOW
                + lax.broadcasted_iota(jnp.int32, (SPAN, QB), 1)
                - lax.broadcasted_iota(jnp.int32, (SPAN, QB), 0)
            )
            allowed = (gap >= 0) & (gap < WINDOW) & (sk_ref[span, :] == sq_ref[...])
            bias[i] = jnp.where(allowed, 0.0, MASKED)

        @pl.when(i == 0)
        def _():
            kt[...] = k_ref[...].T
            vt[...] = v_ref[...].T
            dk_ref[...] = jnp.zeros_like(dk_ref)
            dv_ref[...] = jnp.zeros_like(dv_ref)

        k_pair = k_ref[span, :]
        v_pair = v_ref[span, :]
        lane = lax.broadcasted_iota(jnp.int32, (QB, BLK), 1)
        q_all = (q_ref[...].astype(F32) * scale).astype(BF16)
        do_all = do_ref[...]
        outs, dqs = [], []
        dk_sum = None
        for h in range(2):
            mine = (lane >= h * HEAD) & (lane < (h + 1) * HEAD)
            q_h = jnp.where(mine, q_all, jnp.zeros_like(q_all))
            do_h = jnp.where(mine, do_all, jnp.zeros_like(do_all))
            st = dot(k_pair, q_h, NT) + bias[i]
            top = jnp.max(st, axis=0, keepdims=True)
            e = jnp.exp(st - top)
            prob = e * (1.0 / jnp.sum(e, axis=0, keepdims=True))
            prob_low = prob.astype(BF16)
            dpt = dot(v_pair, do_h, NT)
            mean = jnp.sum(prob * dpt, axis=0, keepdims=True)
            dst = (prob * (dpt - mean)).astype(BF16)
            at = pl.ds(h * HEAD, HEAD)
            outs.append(dot(vt[at, span], prob_low))
            dq = dot(kt[at, span], dst) * scale
            a, b = dq[:half], dq[half:ROT]
            cos_t, sin_t = cos_ref[...], sin_ref[...]
            dqs += [a * cos_t + b * sin_t, b * cos_t - a * sin_t, dq[ROT:]]
            dv_h = dot(prob_low, do_h)
            dk_h = dot(dst, q_h)
            dk_sum = dk_h if h == 0 else dk_sum + dk_h
            dv_sum = dv_h if h == 0 else dv_sum + dv_h
            row = pl.ds(h, 1)

            @pl.when(i == 0)
            def _():
                peak_ref[row, :] = top

            @pl.when(i > 0)
            def _():
                peak_ref[row, :] = jnp.maximum(peak_ref[row, :], top)

        dk_ref[span, :] += dk_sum
        dv_ref[span, :] += dv_sum
        o_ref[...] = jnp.concatenate(outs, axis=0).T.astype(BF16)
        dq_ref[...] = jnp.concatenate(dqs, axis=0).T.astype(BF16)

    qblock = pl.BlockSpec((QB, BLK), lambda p, i: (i, p))
    kblock = pl.BlockSpec((2 * rows, BLK), lambda p, i: (0, p))
    rot = pl.BlockSpec((half, QB), lambda p, i: (0, i))
    return pl.pallas_call(
        kernel,
        grid=(pairs, blocks),
        in_specs=[
            qblock, kblock, kblock, qblock,
            pl.BlockSpec((1, QB), lambda p, i: (0, i)),
            pl.BlockSpec((2 * rows, 1), lambda p, i: (0, 0)),
            rot, rot,
        ],
        out_specs=[qblock, qblock, kblock, kblock, pl.BlockSpec((8, QB), lambda p, i: (p, 0))],
        out_shape=[
            jax.ShapeDtypeStruct((rows, D), BF16),
            jax.ShapeDtypeStruct((rows, D), BF16),
            jax.ShapeDtypeStruct((2 * rows, D), F32),
            jax.ShapeDtypeStruct((2 * rows, D), F32),
            jax.ShapeDtypeStruct((8 * pairs, QB), F32),
        ],
        scratch_shapes=[
            pltpu.VMEM((blocks, SPAN, QB), F32),
            pltpu.VMEM((BLK, 2 * rows), BF16),
            pltpu.VMEM((BLK, 2 * rows), BF16),
        ],
        compiler_params=params(dimension_semantics=("arbitrary", "arbitrary")),
        cost_estimate=pl.CostEstimate(flops=40 << 30, bytes_accessed=32 << 20, transcendentals=20 << 20),
        name="attend",
    )(q, k, v, d_out, seg_q, seg_k, cos8, sin8)


FB = 512


def gelu_parts(v):
    a = jnp.abs(v)
    t = 1.0 / (1.0 + a * (0.3275911 * 0.7071067811865476))
    poly = t * (
        0.5 * 0.254829592
        + t * (0.5 * -0.284496736 + t * (0.5 * 1.421413741 + t * (0.5 * -1.453152027 + t * (0.5 * 1.061405429))))
    )
    e = jnp.exp(v * v * -0.5)
    tail = poly * e
    cdf = jnp.where(v >= 0, 1.0 - tail, tail)
    return v * cdf, cdf + v * e * 0.3989422804014327


def feed_forward(w_rows, g_rows, w_all, m, cotangent, b_up):
    rows = m.shape[0]
    steps = FF // FB

    def kernel(
        w_rows_ref, g_rows_ref, w_ref, m_ref, g_ref, b_ref, out_ref, dm_ref, db_ref, gr_ref,
        mt, wup, wdn, hs, dus, gup, gdn, wsem, gsem,
    ):
        f = pl.program_id(0)
        slot = f % 2
        per = FB // BLK

        def up_at(buf, t):
            return buf.at[pl.ds(pl.multiple_of((t // per) * BLK, BLK), BLK), pl.ds(pl.multiple_of((t % per) * BLK, BLK), BLK)]

        def up_tile(ff, t):
            return UP_BASE + (t // per) * (FF // BLK) + ff * per + t % per

        def down_at(buf, t):
            return buf.at[pl.ds(pl.multiple_of((t // 8) * BLK, BLK), BLK), pl.ds(pl.multiple_of((t % 8) * BLK, BLK), BLK)]

        def down_tile(ff, t):
            return DOWN_BASE + ff * per * 8 + t

        def fetch(ff, sl):
            def body(t):
                src = w_ref.at[pl.ds(pl.multiple_of(w_rows_ref[up_tile(ff, t)], 16), BLK)]
                pltpu.make_async_copy(src, up_at(wup.at[sl], t), wsem.at[0, sl]).start()
                src = w_ref.at[pl.ds(pl.multiple_of(w_rows_ref[down_tile(ff, t)], 16), BLK)]
                pltpu.make_async_copy(src, down_at(wdn.at[sl], t), wsem.at[1, sl]).start()

            tile_loop(0, 8 * per, body)

        def store(ff, sl):
            def body(t):
                dst = gr_ref.at[pl.ds(pl.multiple_of(g_rows_ref[up_tile(ff, t)], 16), BLK)]
                pltpu.make_async_copy(up_at(gup.at[sl], t), dst, gsem.at[0, sl]).start()
                dst = gr_ref.at[pl.ds(pl.multiple_of(g_rows_ref[down_tile(ff, t)], 16), BLK)]
                pltpu.make_async_copy(down_at(gdn.at[sl], t), dst, gsem.at[1, sl]).start()

            tile_loop(0, 8 * per, body)

        def whole_wait(buf, sem):
            pltpu.make_async_copy(buf, buf, sem).wait()

        @pl.when(f == 0)
        def _():
            fetch(0, 0)
            mt[...] = m_ref[...].T
            out_ref[...] = jnp.zeros_like(out_ref)
            dm_ref[...] = jnp.zeros_like(dm_ref)

        whole_wait(wup.at[slot], wsem.at[0, slot])
        whole_wait(wdn.at[slot], wsem.at[1, slot])

        @pl.when(f + 1 < steps)
        def _():
            fetch(f + 1, 1 - slot)

        @pl.when(f >= 2)
        def _():
            whole_wait(gup.at[slot], gsem.at[0, slot])
            whole_wait(gdn.at[slot], gsem.at[1, slot])

        w_u = wup[slot]
        w_d = wdn[slot]
        u = dot(m_ref[...], w_u) + b_ref[...]
        dh = dot(g_ref[...], w_d, NT)
        hidden, slope = gelu_parts(u)
        hs[...] = hidden.astype(BF16)
        du = (dh * slope).astype(BF16)
        dus[...] = du
        db_ref[...] = jnp.sum(du.astype(F32), axis=0, keepdims=True)
        out_ref[...] += dot(hs[...], w_d)
        dm_ref[...] += dot(dus[...], w_u, NT)
        gdn[slot] = dot(hs[...], g_ref[...], TN).astype(BF16)
        gup[slot] = dot(mt[...], dus[...]).astype(BF16)
        store(f, slot)

        @pl.when(f == steps - 1)
        def _():
            for sl in range(2):
                whole_wait(gup.at[sl], gsem.at[0, sl])
                whole_wait(gdn.at[sl], gsem.at[1, sl])

    full = pl.BlockSpec((rows, D), lambda f, *_: (0, 0))
    bias = pl.BlockSpec((1, FB), lambda f, *_: (0, f))
    return pl.pallas_call(
        kernel,
        grid_spec=pltpu.PrefetchScalarGridSpec(
            num_scalar_prefetch=2,
            grid=(steps,),
            in_specs=[ANY, full, full, bias],
            out_specs=[full, full, bias, ANY],
            scratch_shapes=[
                pltpu.VMEM((D, rows), BF16),
                pltpu.VMEM((2, D, FB), BF16),
                pltpu.VMEM((2, FB, D), BF16),
                pltpu.VMEM((rows, FB), BF16),
                pltpu.VMEM((rows, FB), BF16),
                pltpu.VMEM((2, D, FB), BF16),
                pltpu.VMEM((2, FB, D), BF16),
                pltpu.SemaphoreType.DMA((2, 2)),
                pltpu.SemaphoreType.DMA((2, 2)),
            ],
        ),
        out_shape=[
            jax.ShapeDtypeStruct((rows, D), F32),
            jax.ShapeDtypeStruct((rows, D), F32),
            jax.ShapeDtypeStruct((1, FF), F32),
            jax.ShapeDtypeStruct((TILES * BLK, BLK), BF16),
        ],
        compiler_params=params(dimension_semantics=("arbitrary",)),
        cost_estimate=pl.CostEstimate(flops=52 << 30, bytes_accessed=48 << 20, transcendentals=8 << 20),
        name="feed_forward",
    )(w_rows, g_rows, w_all, m, cotangent, b_up)


def finish(w_rows, w_all, tokens, cotangent, smalls, attn_out, mlp_out, dm, dq, dk, dv, dk_back, dv_back, tables):
    rows = tokens.shape[0]
    steps = rows // ROWB
    cos_t, fwd_t, back_t = tables

    def kernel(
        w_rows_ref, w_ref, tok_ref, g_ref, small_ref, o_ref, mlp_ref, dm_ref, dq_ref, dk_ref, dv_ref, dkb_ref, dvb_ref,
        cos_ref, fwd_ref, back_ref,
        out_ref, dx_ref, dp_ref, a_ref, sum_ref, wqkv, wo, sems,
    ):
        i = pl.program_id(0)

        @pl.when(i == 0)
        def _():
            def body(t):
                src = w_ref.at[pl.ds(pl.multiple_of(w_rows_ref[OUT_BASE + t], 16), BLK)]
                dst = wo.at[pl.ds(pl.multiple_of((t // 8) * BLK, BLK), BLK), pl.ds(pl.multiple_of((t % 8) * BLK, BLK), BLK)]
                pltpu.make_async_copy(src, dst, sems.at[0]).start()

            tile_loop(0, 64, body)

            def body(t):
                src = w_ref.at[pl.ds(pl.multiple_of(w_rows_ref[t], 16), BLK)]
                dst = wqkv.at[pl.ds(pl.multiple_of((t // 24) * BLK, BLK), BLK), pl.ds(pl.multiple_of((t % 24) * BLK, BLK), BLK)]
                pltpu.make_async_copy(src, dst, sems.at[1]).start()

            tile_loop(0, 192, body)
            pltpu.make_async_copy(wo, wo, sems.at[0]).wait()
            sum_ref[...] = jnp.zeros_like(sum_ref)

        x = tok_ref[...].astype(F32)
        grad = g_ref[...].astype(F32)
        normed, inv = norm_rows(x)
        g1, g2 = small_ref[4:5, :], small_ref[6:7, :]
        a_ref[...] = (normed * g1 + small_ref[5:6, :]).astype(BF16)
        attn = dot(o_ref[...], wo[...]) + small_ref[2:3, :]
        out_ref[...] = (x + attn + (mlp_ref[...] + small_ref[3:4, :])).astype(BF16)
        dk_all = dk_ref[...] + dkb_ref[...].astype(F32)
        dk_all = rope_rows(dk_all, cos_ref[...], -fwd_ref[...], -back_ref[...])
        dv_all = dv_ref[...] + dvb_ref[...].astype(F32)
        dq_low = dq_ref[...]
        dv_low = dv_all.astype(BF16)
        dp_ref[:, :D] = dq_low
        dp_ref[:, D : 2 * D] = dk_all.astype(BF16)
        dp_ref[:, 2 * D :] = dv_low

        @pl.when(i == 0)
        def _():
            pltpu.make_async_copy(wqkv, wqkv, sems.at[1]).wait()

        da = dot(dp_ref[...], wqkv[...], NT)
        dmv = dm_ref[...]
        dn = da * g1 + dmv * g2
        mean_dn = jnp.mean(dn, axis=-1, keepdims=True)
        mean_dnn = jnp.mean(dn * normed, axis=-1, keepdims=True)
        dx_ref[...] = grad + inv * (dn - mean_dn - normed * mean_dnn)

        def add(row, value):
            sum_ref[row : row + 1, :] += jnp.sum(value, axis=0, keepdims=True)

        add(0, dq_low.astype(F32))
        add(1, dv_low.astype(F32))
        add(2, grad)
        add(3, da * normed)
        add(4, da)
        add(5, dmv * normed)
        add(6, dmv)

    here = lambda i, *_: (i, 0)
    later = lambda i, *_: (i + steps, 0)
    block = pl.BlockSpec((ROWB, D), here)
    upper = pl.BlockSpec((ROWB, D), later)
    table = pl.BlockSpec((ROWB, BLK), later)
    return pl.pallas_call(
        kernel,
        grid_spec=pltpu.PrefetchScalarGridSpec(
            num_scalar_prefetch=1,
            grid=(steps,),
            in_specs=[
                ANY, block, block, pl.BlockSpec((16, D), lambda i, *_: (0, 0)),
                block, block, block, block, upper, upper, block, block, table, table, table,
            ],
            out_specs=[
                block, block, pl.BlockSpec((ROWB, 3 * D), here), block,
                pl.BlockSpec((8, D), lambda i, *_: (0, 0)),
            ],
            scratch_shapes=[
                pltpu.VMEM((D, 3 * D), BF16),
                pltpu.VMEM((D, D), BF16),
                pltpu.SemaphoreType.DMA((2,)),
            ],
        ),
        out_shape=[
            jax.ShapeDtypeStruct((rows, D), BF16),
            jax.ShapeDtypeStruct((rows, D), F32),
            jax.ShapeDtypeStruct((rows, 3 * D), BF16),
            jax.ShapeDtypeStruct((rows, D), BF16),
            jax.ShapeDtypeStruct((8, D), F32),
        ],
        compiler_params=params(dimension_semantics=("arbitrary",)),
        name="finish",
    )(w_rows, w_all, tokens, cotangent, smalls, attn_out, mlp_out, dm, dq, dk, dv, dk_back, dv_back, cos_t, fwd_t, back_t)


def attention_weight_grads(g_rows, grads, attn_in, d_proj, attn_out, cotangent):
    rows = attn_in.shape[0]
    steps = 4 * D // FB

    def kernel(g_rows_ref, a_ref, dp_ref, o_ref, g_ref, _, gr_ref, at, ot, stage, sem):
        i = pl.program_id(0)
        slot = i % 2
        per = FB // BLK

        @pl.when(i == 0)
        def _():
            at[...] = a_ref[...].T

        @pl.when(i == 3 * D // FB)
        def _():
            ot[...] = o_ref[...].T

        @pl.when(i >= 2)
        def _():
            pltpu.make_async_copy(stage.at[slot], stage.at[slot], sem.at[slot]).wait()

        def piece(buf, t):
            return buf.at[pl.ds(pl.multiple_of((t // per) * BLK, BLK), BLK), pl.ds(pl.multiple_of((t % per) * BLK, BLK), BLK)]

        @pl.when(i < 3 * D // FB)
        def _():
            stage[slot] = dot(at[...], dp_ref[...]).astype(BF16)

            def body(t):
                tile = (t // per) * 24 + i * per + t % per
                dst = gr_ref.at[pl.ds(pl.multiple_of(g_rows_ref[tile], 16), BLK)]
                pltpu.make_async_copy(piece(stage.at[slot], t), dst, sem.at[slot]).start()

            tile_loop(0, 8 * per, body)

        @pl.when(i >= 3 * D // FB)
        def _():
            stage[slot] = dot(ot[...], g_ref[...]).astype(BF16)

            def body(t):
                tile = OUT_BASE + (t // per) * 8 + (i - 3 * D // FB) * per + t % per
                dst = gr_ref.at[pl.ds(pl.multiple_of(g_rows_ref[tile], 16), BLK)]
                pltpu.make_async_copy(piece(stage.at[slot], t), dst, sem.at[slot]).start()

            tile_loop(0, 8 * per, body)

        @pl.when(i == steps - 1)
        def _():
            for sl in range(2):
                pltpu.make_async_copy(stage.at[sl], stage.at[sl], sem.at[sl]).wait()

    full = pl.BlockSpec((rows, D), lambda i, *_: (0, 0))
    last = 3 * D // FB - 1
    return pl.pallas_call(
        kernel,
        grid_spec=pltpu.PrefetchScalarGridSpec(
            num_scalar_prefetch=1,
            grid=(steps,),
            in_specs=[
                full,
                pl.BlockSpec((rows, FB), lambda i, *_: (0, jnp.minimum(i, last))),
                full,
                pl.BlockSpec((rows, FB), lambda i, *_: (0, jnp.maximum(i - last - 1, 0))),
                ANY,
            ],
            out_specs=ANY,
            scratch_shapes=[
                pltpu.VMEM((D, rows), BF16),
                pltpu.VMEM((D, rows), BF16),
                pltpu.VMEM((2, D, FB), BF16),
                pltpu.SemaphoreType.DMA((2,)),
            ],
        ),
        out_shape=jax.ShapeDtypeStruct(grads.shape, BF16),
        input_output_aliases={5: 0},
        compiler_params=params(dimension_semantics=("arbitrary",)),
        name="attention_weight_grads",
    )(g_rows, attn_in, d_proj, attn_out, cotangent, grads)


def update_tiles(grads, tiles, left, right, first, second, scale):
    count = tiles.shape[0]
    group = max(g for g in (1, 2, 3, 4) if count % g == 0)

    def kernel(g_ref, w_ref, l_ref, r_ref, m_ref, v_ref, s_ref, w_out, low_out, m_out, v_out):
        for t in range(group):
            l, r = l_ref[t], r_ref[t]
            turned = dot(dot(l, g_ref[t], TN, HIGH), r, NN, HIGH)
            m_new = BETA * m_ref[t] + (1.0 - BETA) * turned
            v_new = BETA * v_ref[t] + (1.0 - BETA) * turned * turned
            ratio = m_new / (jnp.sqrt(v_new) + ADAM_EPS)
            back = dot(dot(l, ratio, NN, HIGH), r, NT, HIGH)
            w_new = (w_ref[t] - LEARN * back) * s_ref[t]
            w_out[t] = w_new
            low_out[t] = w_new.astype(BF16)
            m_out[t] = m_new
            v_out[t] = v_new

    block = pl.BlockSpec((group, BLK, BLK), lambda i: (i, 0, 0))
    row = pl.BlockSpec((group, 1, BLK), lambda i: (i, 0, 0))
    like = lambda t: jax.ShapeDtypeStruct(tiles.shape, t)
    return pl.pallas_call(
        kernel,
        grid=(count // group,),
        in_specs=[block] * 6 + [row],
        out_specs=[block] * 4,
        out_shape=[like(F32), like(BF16), like(F32), like(F32)],
        compiler_params=params(dimension_semantics=("arbitrary",)),
        name="update_tiles",
    )(grads, tiles, left, right, first, second, scale)


def column_scales(tile_ids, factors):
    columns = (tile_ids % (3 * D // BLK))[:, None] * BLK + jnp.arange(BLK, dtype=jnp.int32)[None, :]
    head_index = columns % D // HEAD
    root_factor = jnp.sqrt(factors)
    picked = jnp.sum(
        jnp.where(head_index[..., None] == jnp.arange(HEADS, dtype=jnp.int32), root_factor, 0.0),
        axis=-1,
    )
    clipped = (tile_ids[:, None] < QKV_TILES) & (columns < 2 * D)
    return jnp.where(clipped, picked, 1.0)


def small_update(grads, params_, first_moment, second_moment):
    first_new = BETA * first_moment + (1.0 - BETA) * grads
    second_new = BETA * second_moment + (1.0 - BETA) * grads * grads
    updated = params_ - SMALL_LEARN * first_new / (jnp.sqrt(second_new) + ADAM_EPS)
    return (updated, first_new, second_new)


def passed_along(value, axis, steps):
    count = lax.axis_size(axis)
    leading, last = (max(0, -steps), min(count, count - steps))
    return lax.ppermute(value, axis, [(source, source + steps) for source in range(leading, last)])


def on_device(
    ring,
    tokens,
    segments,
    cotangent,
    tile_of_slot,
    tiles,
    left_bases,
    right_bases,
    first_moments,
    second_moments,
    small_params,
    small_first,
    small_second,
    threshold,
):
    rows = tokens.shape[0]
    slot_count = tiles.shape[0]
    small_count = small_params.shape[0]
    axes = ("dp", "seq")
    seq_index = lax.axis_index("seq")
    owner_index = lax.axis_index(axes)
    first_place = seq_index * rows
    seg_local = segments.reshape(1, rows)

    numbers = jnp.arange(TILES, dtype=jnp.int32)
    slot_of_tile = jnp.sum(
        jnp.where(tile_of_slot[None, :] == numbers[:, None], numbers[None, :], 0), axis=1
    ).astype(jnp.int32)
    g_rows = slot_of_tile * BLK

    if ring:
        small_block = jnp.zeros((16 * BLK,), BF16).at[:small_count].set(small_params.astype(BF16))
        payload = jnp.concatenate(
            [tiles.astype(BF16).reshape(slot_count * BLK, BLK), small_block.reshape(16, BLK)], axis=0
        )
        seg_rows = jnp.broadcast_to(seg_local, (8, rows))
        gathered, prev_tokens, prev_seg = gather_weights(payload, tokens, seg_rows)
        stride = payload.shape[0]
        w_all = gathered.reshape(-1, BLK)
        w_rows = slot_of_tile // slot_count * stride + slot_of_tile % slot_count * BLK
        tail = slot_count * BLK
        small_all = gathered[:, tail : tail + small_count // BLK, :].reshape(SMALL)
        prev_seg = prev_seg[:1]
    else:
        w_all = lax.all_gather(tiles.astype(BF16), axes, axis=0, tiled=True).reshape(-1, BLK)
        w_rows = g_rows
        small_all = lax.all_gather(small_params.astype(BF16), axes, axis=0, tiled=True)
        prev_tokens, prev_seg = passed_along((tokens, seg_local), "seq", 1)

    table = small_all.astype(F32).reshape(D, 12)
    smalls = jnp.concatenate(
        [
            jnp.stack([table[:, r] for r in (0, 1, 2, 7, 8, 9, 10, 11)], axis=0),
            jnp.zeros((8, D), F32),
        ],
        axis=0,
    )
    b_up = table[:, 3:7].reshape(1, FF)

    half = ROT // 2
    exponent = jnp.arange(half, dtype=F32) * (2.0 / ROT)
    frequency = jnp.power(ROPE_BASE, -exponent)
    places = first_place - rows + jnp.arange(2 * rows, dtype=jnp.int32)
    angle = places.astype(F32)[None, :] * frequency[:, None]
    cos8, sin8 = jnp.cos(angle), jnp.sin(angle)
    cos_c, sin_c = cos8.T, sin8.T
    ones = jnp.ones((2 * rows, HEAD - ROT), F32)
    none = jnp.zeros((2 * rows, half), F32)
    rest = jnp.zeros((2 * rows, HEAD - ROT), F32)
    cos_t = jnp.concatenate([cos_c, cos_c, ones] * 2, axis=1)
    fwd_t = jnp.concatenate([-sin_c, none, rest] * 2, axis=1)
    back_t = jnp.concatenate([none, sin_c, rest] * 2, axis=1)
    tables = (cos_t, fwd_t, back_t)

    prev_seg = jnp.where(seq_index == 0, -1, prev_seg)
    seg_k = jnp.concatenate([prev_seg, seg_local], axis=1).reshape(2 * rows, 1)

    q, k, v, d_out, m = project(w_rows, w_all, prev_tokens, tokens, cotangent, smalls, tables)
    attn_out, dq, dk, dv, peaks = attend(
        q, k, v, d_out, seg_local, seg_k, cos8[:, rows:], sin8[:, rows:]
    )
    dk_back = passed_along(dk[:rows].astype(BF16), "seq", -1)
    dv_back = passed_along(dv[:rows].astype(BF16), "seq", -1)
    mlp_out, dm, db_up, grads = feed_forward(w_rows, g_rows, w_all, m, cotangent, b_up)
    block_output, input_grad, d_proj, attn_in, sums = finish(
        w_rows, w_all, tokens, cotangent, smalls, attn_out, mlp_out, dm, dq, dk, dv, dk_back, dv_back, tables
    )
    grads = attention_weight_grads(g_rows, grads, attn_in, d_proj, attn_out, cotangent)

    small_terms = jnp.concatenate(
        [
            sums[:3].T,
            db_up.reshape(D, FF // D),
            sums[2:7].T,
        ],
        axis=1,
    ).reshape(SMALL)
    head_peak = jnp.max(peaks.reshape(HEADS // 2, 8, QB)[:, :2, :], axis=-1).reshape(HEADS)
    if ring:
        peak_rows = jnp.zeros((8, BLK), F32).at[:, :HEADS].set(head_peak[None, :])
        extra = jnp.concatenate([small_terms.reshape(SMALL_ROWS, BLK), peak_rows], axis=0)
        tile_grads, extra = sum_gradients(grads, extra)
        tile_grads = tile_grads.reshape(slot_count, BLK, BLK)
        small_grads = lax.dynamic_slice_in_dim(
            extra[:SMALL_ROWS].reshape(SMALL), owner_index * small_count, small_count, 0
        )
        head_peak = extra[SMALL_ROWS, :HEADS]
    else:
        tile_grads = lax.psum_scatter(
            grads.astype(F32).reshape(TILES, BLK, BLK), axes, scatter_dimension=0, tiled=True
        )
        small_grads = lax.psum_scatter(small_terms, axes, scatter_dimension=0, tiled=True)
        head_peak = lax.pmax(head_peak, axes)

    local_ids = lax.dynamic_slice_in_dim(tile_of_slot, owner_index * slot_count, slot_count, 0)
    limit = threshold[0]
    factors = limit / jnp.maximum(head_peak, limit)
    scale = column_scales(local_ids, factors).reshape(slot_count, 1, BLK)
    new_tiles, new_low, new_first, new_second = update_tiles(
        tile_grads, tiles, left_bases, right_bases, first_moments, second_moments, scale
    )
    new_small, new_small_first, new_small_second = small_update(
        small_grads, small_params, small_first, small_second
    )
    return (
        block_output,
        input_grad,
        tile_grads,
        small_grads,
        new_tiles,
        new_low,
        new_first,
        new_second,
        new_small,
        new_small.astype(BF16),
        new_small_first,
        new_small_second,
        factors,
    )


def solution(mesh):
    split = P(("dp", "seq"))
    in_specs = (split, P("dp", "seq"), split, P()) + (split,) * 8 + (P(),)
    out_specs = (split,) * 12 + (P(),)
    ring = (mesh.shape["dp"], mesh.shape["seq"]) == (4, 8)
    return jax.shard_map(
        functools.partial(on_device, ring), mesh=mesh, in_specs=in_specs, out_specs=out_specs, check_vma=False
    )
```

time: 1840 us -> 618 us (0.34); the launches traced: 1810 us -> 616 us
  Pallas kernels: 0 us -> 555 us
  matrix products: 530 us -> 0 us
  local copies, waits for them, and re-layouts: 507 us -> 36.2 us
  waiting for transfers between devices: 356 us -> 0.01 us
  other arithmetic: 229 us -> 17.3 us
  blocking collectives: 121 us -> 0 us
  loops' own time: 41.7 us -> 0 us
    pallas_call x0 -> x8, Pallas kernels: none -> 555 us  [the longest x1 134 us: sum_gradients(): pl.pallas_call(kernel, out_shape=[jax.ShapeDtypeStruct((OWNED, BLK), F32)...]
    dot_general x30 -> x0, matrix products: 530 us -> none  [the longest x4 89.7 us: block_scores(): jnp.einsum('qhd,khd->hqk', query_block, key_block, preferred_element_type...]
    reduce_scatter x1 -> x0, waiting for transfers between devices: 258 us -> none  [on_device(): lax.psum_scatter(slot_grads, ('dp', 'seq'), scatter_dimension=0, tiled=True)]
    dynamic_update_slice x10 -> x0, local copies, waits for them, and re-layouts: 234 us -> none  [the longest x4 83 us: on_device(): lax.scan(backward_block, (zero_heads, zero_heads), (block_starts, log_sums))]
    all_gather x1 -> x0, waiting for transfers between devices: 98.4 us -> none  [collect(): lax.all_gather(tiles_low, ('dp', 'seq'), axis=0, tiled=True)]
    convert_element_type x9 -> x5, other arithmetic: 97.9 us -> 2.54 us  [the longest x1 1.01 us: on_device(): tiles.astype(BF16).reshape(slot_count * BLK, BLK)]
    reshape x11 -> x6, local copies, waits for them, and re-layouts: 81.9 us -> 3.82 us  [the longest x1 1.35 us: on_device(): seg_k = jnp.concatenate([prev_seg, seg_local], axis=1).reshape(2 * rows, 1)]
    gather x2 -> x0, local copies, waits for them, and re-layouts: 62.6 us -> none  [the longest x1 35.3 us: on_device(): slot_grads = grad_by_number[tile_of_slot]]
  transfers between devices with their start and end apart: 7 -> 2, of which waited for: 2 -> 0; matrix products, arithmetic and copies ran while one was open for 16% -> 2% of each run, Pallas kernels for 0% -> 14%
where the time goes in v1:
time: 618 us; the launch traced here: 616 us
  Pallas kernels  555 us (90%)
  local copies, waits for them, and re-layouts  36.2 us (6%)
  other arithmetic  17.3 us (3%)
    pallas_call x1, Pallas kernels, sum_gradients(): pl.pallas_call(kernel, out_shape=[jax.ShapeDtypeStruct((OWNED, BLK), F32)...  134 us
    pallas_call x1, Pallas kernels, attend(): pl.pallas_call(kernel, grid=(pairs, blocks), in_specs=[qblock, kblock, kb...  133 us
    pallas_call x1, Pallas kernels, gather_weights(): pl.pallas_call(kernel, out_shape=[jax.ShapeDtypeStruct((32, rows, BLK), B...  111 us
    pallas_call x1, Pallas kernels, feed_forward(): pl.pallas_call(kernel, grid_spec=pltpu.PrefetchScalarGridSpec(num_scalar_...  86.2 us
    pallas_call x1, Pallas kernels, finish(): pl.pallas_call(kernel, grid_spec=pltpu.PrefetchScalarGridSpec(num_scalar_...  26.4 us
    pallas_call x1, Pallas kernels, project(): pl.pallas_call(kernel, grid_spec=pltpu.PrefetchScalarGridSpec(num_scalar_...  24.6 us
    pallas_call x1, Pallas kernels, update_tiles(): pl.pallas_call(kernel, grid=(count // group,), in_specs=[block] * 6 + [ro...  20.5 us
    pallas_call x1, Pallas kernels, attention_weight_grads(): pl.pallas_call(kernel, grid_spec=pltpu.PrefetchScalarGridSpec(num_scalar_...  19.5 us
  transfers between devices with their start and end apart: 2, of which 0 were waited for; matrix products, arithmetic and copies ran while one was open for 2% of the time, Pallas kernels for 14%

profile of v1, /device:TPU:16, one launch (start us, length us, event | category | flops | bytes accessed | tf_op | source)
XLA Modules:
  0.0 615.5 jit_solution(12463915301387665915)
XLA Ops:
  0.8 5.5 multiply_sine_fusion
  9.1 1.0 broadcast_in_dim.68
  10.1 4.7 concatenate.32.back_ref
  14.9 4.9 concatenate.31.fwd_ref
  21.3 110.5 %gather_weights.1 = (bf16[32,3088,128]{2,1,0:T(8,128)(2,1)}, bf16[1024,1024]{1,0:T(8,128)(2,1)}, s32[8,1024]{1,0:T(8,128)}) custom-call(bf16[3088,128]{1,0:T(8,128)(2,1)} %pad_maximum_fusion.x_ref, bf16[1024,1024]{1,0:T(8,128)(2,1)} %tok_ref.5, s32[8,1024]{1,0:T(8,128)} %broadcast_in_dim.65.seg_ref), custom_call_target="tpu_custom_call" | custom-call | tf_op jit(solution)/shard_map/gather_weights/pallas_call | solution.py:302
  134.1 2.1 slice_reduce_fusion
  136.2 1.3 copy.35.sk_ref
  137.6 3.1 concatenate.30.cos_ref
  140.8 1.3 concatenate.29.small_ref
  142.0 24.6 %project.1 = (bf16[1024,1024]{1,0:T(8,128)(2,1)}, bf16[2048,1024]{1,0:T(8,128)(2,1)}, bf16[2048,1024]{1,0:T(8,128)(2,1)}, bf16[1024,1024]{1,0:T(8,128)(2,1)}, bf16[1024,1024]{1,0:T(8,128)(2,1)}) custom-call(s32[768]{0:T(1024)} %get-tuple-element.114.w_rows_ref, bf16[98816,128]{1,0:T(8,128)(2,1)} %bitcast.29, bf16[1024,1024]{1,0:T(8,128)(2,1)} %get-tuple-element.66.prev_ref, ...), custom_call_target="tpu_custom_call" | custom-call | tf_op jit(solution)/shard_map/project/pallas_call | solution.py:685
  166.6 133.1 %attend.1 = (bf16[1024,1024]{1,0:T(8,128)(2,1)}, bf16[1024,1024]{1,0:T(8,128)(2,1)}, f32[2048,1024]{1,0:T(8,128)}, f32[2048,1024]{1,0:T(8,128)}, f32[64,256]{1,0:T(8,128)}) custom-call(bf16[1024,1024]{1,0:T(8,128)(2,1)} %get-tuple-element.67.q_ref, bf16[2048,1024]{1,0:T(8,128)(2,1)} %get-tuple-element.68.k_ref, bf16[2048,1024]{1,0:T(8,128)(2,1)} %get-tuple-element.69.v_ref, ...), custom_call_target="tpu_custom_call" | custom-call | flops 42949672960 | bytes 33554432 | tf_op jit(solution)/shard_map/attend/pallas_call | solution.py:797
  299.7 3.8 slice.142
  303.5 3.5 collective-permute-start.1
  307.0 3.8 slice.143
  310.9 2.0 collective-permute-start
  314.1 86.2 %feed_forward.1 = (f32[1024,1024]{1,0:T(8,128)}, f32[1024,1024]{1,0:T(8,128)}, f32[1,4096]{1,0:T(1,128)}, bf16[98304,128]{1,0:T(8,128)(2,1)}) custom-call(s32[768]{0:T(1024)} %get-tuple-element.114.w_rows_ref, s32[768]{0:T(1024)} %get-tuple-element.113.g_rows_ref, bf16[98816,128]{1,0:T(8,128)(2,1)} %bitcast.30, bf16[1024,1024]{1,0:T(8,128)(2,1)} %get-tuple-element.73.m_ref, ...), custom_call_target="tpu_custom_call" | custom-call | flops 55834574848 | bytes 50331648 | tf_op jit(solution)/shard_map/feed_forward/pallas_call | solution.py:928
  403.8 1.4 reduce.29
  406.2 1.3 copy-done.3
  407.5 26.4 %finish.1 = (bf16[1024,1024]{1,0:T(8,128)(2,1)}, f32[1024,1024]{1,0:T(8,128)}, bf16[1024,3072]{1,0:T(8,128)(2,1)}, bf16[1024,1024]{1,0:T(8,128)(2,1)}, f32[8,1024]{1,0:T(8,128)}) custom-call(s32[768]{0:T(1024)} %get-tuple-element.114.w_rows_ref, bf16[98816,128]{1,0:T(8,128)(2,1)} %bitcast.31, bf16[1024,1024]{1,0:T(8,128)(2,1)} %tok_ref.5, ...), custom_call_target="tpu_custom_call" | custom-call | tf_op jit(solution)/shard_map/finish/pallas_call | solution.py:1032
  436.7 19.5 %attention_weight_grads.1.g_ref = bf16[98304,128]{1,0:T(8,128)(2,1)} custom-call(s32[768]{0:T(1024)} %get-tuple-element.113.g_rows_ref, bf16[1024,1024]{1,0:T(8,128)(2,1)} %get-tuple-element.81.a_ref, bf16[1024,3072]{1,0:T(8,128)(2,1)} %get-tuple-element.82.dp_ref, bf16[1024,1024]{1,0:T(8,128)(2,1)} %get-tuple-element.72.o_ref, ...), custom_call_target="tpu_custom_call", output_to_operand_aliasing={{}: (5, {})} | custom-call | tf_op jit(solution)/shard_map/attention_weight_grads/pallas_call | solution.py:1116
  456.2 134.2 %sum_gradients.1 = (f32[3072,128]{1,0:T(8,128)}, f32[104,128]{1,0:T(8,128)}) custom-call(bf16[98304,128]{1,0:T(8,128)(2,1)} %attention_weight_grads.1.g_ref, f32[104,128]{1,0:T(8,128)} %pad_maximum_fusion.2.e_ref), custom_call_target="tpu_custom_call" | custom-call | tf_op jit(solution)/shard_map/sum_gradients/pallas_call | solution.py:569
  591.2 1.2 fusion.15
  593.9 20.5 %update_tiles.1 = (f32[24,128,128]{2,1,0:T(8,128)}, bf16[24,128,128]{2,1,0:T(8,128)(2,1)}, f32[24,128,128]{2,1,0:T(8,128)}, f32[24,128,128]{2,1,0:T(8,128)}) custom-call(f32[24,128,128]{2,1,0:T(8,128)} %bitcast.32, f32[24,128,128]{2,1,0:T(8,128)} %w_ref.1, f32[24,128,128]{2,1,0:T(8,128)} %l_ref.1, f32[24,128,128]{2,1,0:T(8,128)} %r_ref.1, ...), custom_call_target="tpu_custom_call" | custom-call | tf_op jit(solution)/shard_map/update_tiles/pallas_call | solution.py:1164
  614.4 1.1 copy.41
  (63 shorter events, 16.7 us)
Async XLA Ops:
  0.6 5.7 copy-start.5
  0.7 5.7 copy-start.7
  0.7 7.3 %copy-start = (f32[24,128,128]{2,1,0:T(8,128)S(1)}, f32[24,128,128]{2,1,0:T(8,128)}, u32[]{:S(2)}) copy-start(f32[24,128,128]{2,1,0:T(8,128)} %w_ref.1) | copy-start | bytes 4718596
  14.9 4.9 copy-start.2
  14.9 5.8 copy-start.4
  303.5 102.6 %collective-permute-start.1 = (bf16[1024,1024]{1,0:T(8,128)(2,1)}, bf16[1024,1024]{1,0:T(8,128)(2,1)S(1)}, u32[]{:S(2)}, u32[]{:S(2)}) collective-permute-start(bf16[1024,1024]{1,0:T(8,128)(2,1)} %slice.142), channel_id=1, source_target_pairs={{1,0},{2,1},{3,2},{4,3},{5,4},{6,5},{7,6},{9,8},{10,9},{11,10},{12... | collective-permute-start | bytes 6291464 | tf_op jit(solution)/shard_map/ppermute | solution.py:1197
  310.9 95.3 %collective-permute-start = (bf16[1024,1024]{1,0:T(8,128)(2,1)}, bf16[1024,1024]{1,0:T(8,128)(2,1)}, u32[]{:S(2)}, u32[]{:S(2)}) collective-permute-start(bf16[1024,1024]{1,0:T(8,128)(2,1)} %slice.143), channel_id=1, source_target_pairs={{1,0},{2,1},{3,2},{4,3},{5,4},{6,5},{7,6},{9,8},{10,9},{11,10},{12... | collective-permute-start | bytes 6291464 | tf_op jit(solution)/shard_map/ppermute | solution.py:1197
  406.2 1.3 copy-start.3
  456.2 137.1 %copy-start.6 = (f32[384]{0:T(512)S(1)}, f32[384]{0:T(512)}, u32[]{:S(2)}) copy-start(f32[384]{0:T(512)} %param.26) | copy-start | bytes 4612
  456.2 137.1 %copy-start.8 = (f32[384]{0:T(512)S(1)}, f32[384]{0:T(512)}, u32[]{:S(2)}) copy-start(f32[384]{0:T(512)} %param.27) | copy-start | bytes 4612
  456.2 137.1 %copy-start.9 = (f32[384]{0:T(512)S(1)}, f32[384]{0:T(512)}, u32[]{:S(2)}) copy-start(f32[384]{0:T(512)} %param.28) | copy-start | bytes 4612
  593.9 20.5 %copy-start.1 = (f32[3072,128]{1,0:T(8,128)S(1)}, f32[3072,128]{1,0:T(8,128)}, u32[]{:S(2)}) copy-start(f32[3072,128]{1,0:T(8,128)} %get-tuple-element.87) | copy-start | bytes 4718596

commit v2 on v1

--- a/solution.py
+++ b/solution.py
@@ -46,6 +46,16 @@
 
 def dot(a, b, dims=NN, precision=None):
     return lax.dot_general(a, b, dims, precision=precision, preferred_element_type=F32)
+
+
+def interleave(*parts):
+    live = list(parts)
+    while live:
+        for part in list(live):
+            try:
+                next(part)
+            except StopIteration:
+                live.remove(part)
 
 
 def params(**kw):
@@ -714,21 +724,39 @@
 SPAN = WINDOW + QB
 
 
+CHUNK = 256
+SAFE_SCORE = 60.0
+
+
 def attend(q, k, v, d_out, seg_q, seg_k, cos8, sin8):
     rows = q.shape[0]
     blocks = rows // QB
     pairs = HEADS // 2
     scale = HEAD ** (-0.5)
     half = ROT // 2
+    n = SPAN // CHUNK
+
+    def heads_apart(x):
+        row = lax.broadcasted_iota(jnp.int32, x.shape, 0)
+        zero = jnp.zeros_like(x)
+        return jnp.concatenate([jnp.where(row < HEAD, x, zero), jnp.where(row < HEAD, zero, x)], axis=1)
+
+    def stacked(x):
+        lane = lax.broadcasted_iota(jnp.int32, x.shape, 1)
+        zero = jnp.zeros_like(x)
+        return jnp.concatenate([jnp.where(lane < HEAD, x, zero), jnp.where(lane < HEAD, zero, x)], axis=0)
+
+    def fold(x, op):
+        return op(x.reshape(x.shape[0] // 8, 8, x.shape[1]), axis=0)
+
+    def two(x):
+        return jnp.concatenate([x, x], axis=1)
 
     def kernel(
         q_ref, k_ref, v_ref, do_ref, sq_ref, sk_ref, cos_ref, sin_ref,
-        o_ref, dq_ref, dk_ref, dv_ref, peak_ref, bias, kt, vt,
+        o_ref, dq_ref, dk_ref, dv_ref, halo_ref, peak_ref, bias, kt, vt, el_ref, ds_ref, dks, dvs,
     ):
         p = pl.program_id(0)
-        i = pl.program_id(1)
-        start = pl.multiple_of(i * QB, QB)
-        span = pl.ds(start, SPAN)
 
         @pl.when(p == 0)
         def _():
@@ -737,86 +765,160 @@
                 + lax.broadcasted_iota(jnp.int32, (SPAN, QB), 1)
                 - lax.broadcasted_iota(jnp.int32, (SPAN, QB), 0)
             )
-            allowed = (gap >= 0) & (gap < WINDOW) & (sk_ref[span, :] == sq_ref[...])
-            bias[i] = jnp.where(allowed, 0.0, MASKED)
-
-        @pl.when(i == 0)
-        def _():
-            kt[...] = k_ref[...].T
-            vt[...] = v_ref[...].T
-            dk_ref[...] = jnp.zeros_like(dk_ref)
-            dv_ref[...] = jnp.zeros_like(dv_ref)
-
-        k_pair = k_ref[span, :]
-        v_pair = v_ref[span, :]
-        lane = lax.broadcasted_iota(jnp.int32, (QB, BLK), 1)
-        q_all = (q_ref[...].astype(F32) * scale).astype(BF16)
-        do_all = do_ref[...]
-        outs, dqs = [], []
-        dk_sum = None
-        for h in range(2):
-            mine = (lane >= h * HEAD) & (lane < (h + 1) * HEAD)
-            q_h = jnp.where(mine, q_all, jnp.zeros_like(q_all))
-            do_h = jnp.where(mine, do_all, jnp.zeros_like(do_all))
-            st = dot(k_pair, q_h, NT) + bias[i]
-            top = jnp.max(st, axis=0, keepdims=True)
-            e = jnp.exp(st - top)
-            prob = e * (1.0 / jnp.sum(e, axis=0, keepdims=True))
-            prob_low = prob.astype(BF16)
-            dpt = dot(v_pair, do_h, NT)
-            mean = jnp.sum(prob * dpt, axis=0, keepdims=True)
-            dst = (prob * (dpt - mean)).astype(BF16)
-            at = pl.ds(h * HEAD, HEAD)
-            outs.append(dot(vt[at, span], prob_low))
-            dq = dot(kt[at, span], dst) * scale
-            a, b = dq[:half], dq[half:ROT]
-            cos_t, sin_t = cos_ref[...], sin_ref[...]
-            dqs += [a * cos_t + b * sin_t, b * cos_t - a * sin_t, dq[ROT:]]
-            dv_h = dot(prob_low, do_h)
-            dk_h = dot(dst, q_h)
-            dk_sum = dk_h if h == 0 else dk_sum + dk_h
-            dv_sum = dv_h if h == 0 else dv_sum + dv_h
-            row = pl.ds(h, 1)
-
-            @pl.when(i == 0)
-            def _():
-                peak_ref[row, :] = top
-
-            @pl.when(i > 0)
-            def _():
-                peak_ref[row, :] = jnp.maximum(peak_ref[row, :], top)
-
-        dk_ref[span, :] += dk_sum
-        dv_ref[span, :] += dv_sum
-        o_ref[...] = jnp.concatenate(outs, axis=0).T.astype(BF16)
-        dq_ref[...] = jnp.concatenate(dqs, axis=0).T.astype(BF16)
-
-    qblock = pl.BlockSpec((QB, BLK), lambda p, i: (i, p))
-    kblock = pl.BlockSpec((2 * rows, BLK), lambda p, i: (0, p))
-    rot = pl.BlockSpec((half, QB), lambda p, i: (0, i))
+            for i in range(blocks):
+                same = sk_ref[i * QB : i * QB + SPAN, :] == sq_ref[:, i * QB : (i + 1) * QB]
+                bias[i] = jnp.where((gap >= 0) & (gap < WINDOW) & same, 0.0, MASKED)
+
+        kt[...] = k_ref[...].T
+        vt[...] = v_ref[...].T
+        k_float = kt[...].astype(F32)
+        q_float = q_ref[...].astype(F32) * scale
+        reach = jnp.max(jnp.sum(k_float * k_float, axis=0)) * jnp.max(jnp.sum(q_float * q_float, axis=1))
+        safe = reach < SAFE_SCORE * SAFE_SCORE
+
+        def keys_at(ref, i, c):
+            return ref[i * QB + c * CHUNK : i * QB + (c + 1) * CHUNK, :]
+
+        def prepare(i):
+            q_all = (q_ref[i * QB : (i + 1) * QB, :].astype(F32) * scale).astype(BF16)
+            return q_all, heads_apart(q_all.T)
+
+        def scores(i, c, q_apart):
+            return dot(keys_at(k_ref, i, c), q_apart) + two(bias[i, c * CHUNK : (c + 1) * CHUNK])
+
+        def forward(i, q_apart, shifted, found):
+            base = None
+            if shifted:
+                for c in range(n):
+                    t = fold(scores(i, c, q_apart), jnp.max)
+                    base = t if c == 0 else jnp.maximum(base, t)
+                base = jnp.max(base, axis=0, keepdims=True)
+            top8 = sum8 = None
+            for c in range(n):
+                st = scores(i, c, q_apart)
+                e = jnp.exp(st - base if shifted else st)
+                el_ref[i % 2, c * CHUNK : (c + 1) * CHUNK] = e.astype(BF16)
+                t, u = fold(st, jnp.max), fold(e, jnp.sum)
+                top8, sum8 = (t, u) if c == 0 else (jnp.maximum(top8, t), sum8 + u)
+                yield
+            found.append(jnp.max(top8, axis=0, keepdims=True))
+            found.append(1.0 / jnp.sum(sum8, axis=0, keepdims=True))
+
+        def per_head(x):
+            return jnp.concatenate(
+                [jnp.broadcast_to(x[:, :QB], (HEAD, QB)), jnp.broadcast_to(x[:, QB:], (HEAD, QB))], axis=0
+            )
+
+        def both(t, x_ref, i):
+            span = slice(i * QB, i * QB + SPAN)
+            return jnp.concatenate(
+                [dot(t[:HEAD, span], x_ref[i % 2, :, :QB]), dot(t[HEAD:, span], x_ref[i % 2, :, QB:])], axis=0
+            )
+
+        def output(i, inv):
+            raw = both(vt, el_ref, i)
+            inv2 = per_head(inv)
+            o_ref[i * QB : (i + 1) * QB, :] = (raw * inv2).T.astype(BF16)
+            do_s = (do_ref[i * QB : (i + 1) * QB, :].astype(F32).T * inv2).astype(BF16)
+            m = do_s.astype(F32) * raw
+            mean = jnp.concatenate(
+                [jnp.sum(m[:HEAD], axis=0, keepdims=True), jnp.sum(m[HEAD:], axis=0, keepdims=True)], axis=1
+            )
+            return do_s, mean * inv
+
+        def score_grads(i, do_s, mean):
+            do_apart = heads_apart(do_s)
+            for c in range(n):
+                w = slice(c * CHUNK, (c + 1) * CHUNK)
+                dpt = dot(keys_at(v_ref, i, c), do_apart)
+                ds_ref[i % 2, w] = (el_ref[i % 2, w].astype(F32) * (dpt - mean)).astype(BF16)
+
+        def input_grads(i, q_all, do_s):
+            do_rows = stacked(do_s.T)
+            q_rows = stacked(q_all)
+            for c in range(n):
+                w = slice(c * CHUNK, (c + 1) * CHUNK)
+                at = slice(i * QB + c * CHUNK, i * QB + (c + 1) * CHUNK)
+                v_part = dot(el_ref[i % 2, w], do_rows)
+                k_part = dot(ds_ref[i % 2, w], q_rows)
+                if i == 0 or c == n - 1:
+                    dvs[at, :] = v_part
+                    dks[at, :] = k_part
+                else:
+                    dvs[at, :] += v_part
+                    dks[at, :] += k_part
+                yield
+            dq = both(kt, ds_ref, i) * scale
+            cos_t, sin_t = cos_ref[:, i * QB : (i + 1) * QB], sin_ref[:, i * QB : (i + 1) * QB]
+            turned = []
+            for h in range(2):
+                f, g = dq[h * HEAD : h * HEAD + half], dq[h * HEAD + half : h * HEAD + ROT]
+                turned += [f * cos_t + g * sin_t, g * cos_t - f * sin_t, dq[h * HEAD + ROT : (h + 1) * HEAD]]
+            dq_ref[i * QB : (i + 1) * QB, :] = jnp.concatenate(turned, axis=0).T.astype(BF16)
+            yield
+
+        def run(shifted):
+            top = held = None
+            for i in range(blocks + 1):
+                parts, found = [], []
+                if held is not None:
+                    parts.append(input_grads(i - 1, *held))
+                if i < blocks:
+                    q_all, q_apart = prepare(i)
+                    parts.append(forward(i, q_apart, shifted, found))
+                interleave(*parts)
+                if i < blocks:
+                    t, inv = found
+                    top = t if top is None else jnp.maximum(top, t)
+                    do_s, mean = output(i, inv)
+                    score_grads(i, do_s, mean)
+                    held = (q_all, do_s)
+            peak_ref[...] = jnp.broadcast_to(top, peak_ref.shape)
+            halo_ref[0] = dks[:rows, :].astype(BF16)
+            halo_ref[1] = dvs[:rows, :].astype(BF16)
+            dk_ref[...] = dks[rows:, :]
+            dv_ref[...] = dvs[rows:, :]
+
+        @pl.when(safe)
+        def _():
+            run(False)
+
+        @pl.when(jnp.logical_not(safe))
+        def _():
+            run(True)
+
+    block = pl.BlockSpec((rows, BLK), lambda p: (0, p))
+    keys = pl.BlockSpec((2 * rows, BLK), lambda p: (0, p))
+    whole = lambda *shape: pl.BlockSpec(shape, lambda p: (0, 0))
     return pl.pallas_call(
         kernel,
-        grid=(pairs, blocks),
+        grid=(pairs,),
         in_specs=[
-            qblock, kblock, kblock, qblock,
-            pl.BlockSpec((1, QB), lambda p, i: (0, i)),
-            pl.BlockSpec((2 * rows, 1), lambda p, i: (0, 0)),
-            rot, rot,
+            block, keys, keys, block, whole(1, rows), whole(2 * rows, 1), whole(half, rows), whole(half, rows),
         ],
-        out_specs=[qblock, qblock, kblock, kblock, pl.BlockSpec((8, QB), lambda p, i: (p, 0))],
+        out_specs=[
+            block, block, block, block,
+            pl.BlockSpec((2, rows, BLK), lambda p: (0, 0, p)),
+            pl.BlockSpec((8, 2 * QB), lambda p: (p, 0)),
+        ],
         out_shape=[
             jax.ShapeDtypeStruct((rows, D), BF16),
             jax.ShapeDtypeStruct((rows, D), BF16),
-            jax.ShapeDtypeStruct((2 * rows, D), F32),
-            jax.ShapeDtypeStruct((2 * rows, D), F32),
-            jax.ShapeDtypeStruct((8 * pairs, QB), F32),
+            jax.ShapeDtypeStruct((rows, D), F32),
+            jax.ShapeDtypeStruct((rows, D), F32),
+            jax.ShapeDtypeStruct((2, rows, D), BF16),
+            jax.ShapeDtypeStruct((8 * pairs, 2 * QB), F32),
         ],
         scratch_shapes=[
             pltpu.VMEM((blocks, SPAN, QB), F32),
             pltpu.VMEM((BLK, 2 * rows), BF16),
             pltpu.VMEM((BLK, 2 * rows), BF16),
+            pltpu.VMEM((2, SPAN, 2 * QB), BF16),
+            pltpu.VMEM((2, SPAN, 2 * QB), BF16),
+            pltpu.VMEM((2 * rows, BLK), F32),
+            pltpu.VMEM((2 * rows, BLK), F32),
         ],
-        compiler_params=params(dimension_semantics=("arbitrary", "arbitrary")),
+        compiler_params=params(dimension_semantics=("arbitrary",)),
         cost_estimate=pl.CostEstimate(flops=40 << 30, bytes_accessed=32 << 20, transcendentals=20 << 20),
         name="attend",
     )(q, k, v, d_out, seg_q, seg_k, cos8, sin8)
@@ -844,7 +946,7 @@
 
     def kernel(
         w_rows_ref, g_rows_ref, w_ref, m_ref, g_ref, b_ref, out_ref, dm_ref, db_ref, gr_ref,
-        mt, wup, wdn, hs, dus, gup, gdn, wsem, gsem,
+        mt, wup, wdn, hs, dus, gup, gdn, u_ref, h_ref, wsem, gsem,
     ):
         f = pl.program_id(0)
         slot = f % 2
@@ -862,30 +964,26 @@
         def down_tile(ff, t):
             return DOWN_BASE + ff * per * 8 + t
 
-        def fetch(ff, sl):
-            def body(t):
-                src = w_ref.at[pl.ds(pl.multiple_of(w_rows_ref[up_tile(ff, t)], 16), BLK)]
-                pltpu.make_async_copy(src, up_at(wup.at[sl], t), wsem.at[0, sl]).start()
-                src = w_ref.at[pl.ds(pl.multiple_of(w_rows_ref[down_tile(ff, t)], 16), BLK)]
-                pltpu.make_async_copy(src, down_at(wdn.at[sl], t), wsem.at[1, sl]).start()
-
-            tile_loop(0, 8 * per, body)
-
-        def store(ff, sl):
-            def body(t):
-                dst = gr_ref.at[pl.ds(pl.multiple_of(g_rows_ref[up_tile(ff, t)], 16), BLK)]
-                pltpu.make_async_copy(up_at(gup.at[sl], t), dst, gsem.at[0, sl]).start()
-                dst = gr_ref.at[pl.ds(pl.multiple_of(g_rows_ref[down_tile(ff, t)], 16), BLK)]
-                pltpu.make_async_copy(down_at(gdn.at[sl], t), dst, gsem.at[1, sl]).start()
-
-            tile_loop(0, 8 * per, body)
+        def fetch_one(ff, sl, t):
+            src = w_ref.at[pl.ds(pl.multiple_of(w_rows_ref[up_tile(ff, t)], 16), BLK)]
+            pltpu.make_async_copy(src, up_at(wup.at[sl], t), wsem.at[0, sl]).start()
+            src = w_ref.at[pl.ds(pl.multiple_of(w_rows_ref[down_tile(ff, t)], 16), BLK)]
+            pltpu.make_async_copy(src, down_at(wdn.at[sl], t), wsem.at[1, sl]).start()
+
+        def store_one(ff, sl, t):
+            dst = gr_ref.at[pl.ds(pl.multiple_of(g_rows_ref[up_tile(ff, t)], 16), BLK)]
+            pltpu.make_async_copy(up_at(gup.at[sl], t), dst, gsem.at[0, sl]).start()
+            dst = gr_ref.at[pl.ds(pl.multiple_of(g_rows_ref[down_tile(ff, t)], 16), BLK)]
+            pltpu.make_async_copy(down_at(gdn.at[sl], t), dst, gsem.at[1, sl]).start()
 
         def whole_wait(buf, sem):
             pltpu.make_async_copy(buf, buf, sem).wait()
 
+        count = 8 * per
+
         @pl.when(f == 0)
         def _():
-            fetch(0, 0)
+            tile_loop(0, count, lambda t: fetch_one(0, 0, t))
             mt[...] = m_ref[...].T
             out_ref[...] = jnp.zeros_like(out_ref)
             dm_ref[...] = jnp.zeros_like(dm_ref)
@@ -893,32 +991,70 @@
         whole_wait(wup.at[slot], wsem.at[0, slot])
         whole_wait(wdn.at[slot], wsem.at[1, slot])
 
-        @pl.when(f + 1 < steps)
-        def _():
-            fetch(f + 1, 1 - slot)
-
         @pl.when(f >= 2)
         def _():
             whole_wait(gup.at[slot], gsem.at[0, slot])
             whole_wait(gdn.at[slot], gsem.at[1, slot])
 
-        w_u = wup[slot]
-        w_d = wdn[slot]
-        u = dot(m_ref[...], w_u) + b_ref[...]
-        dh = dot(g_ref[...], w_d, NT)
-        hidden, slope = gelu_parts(u)
-        hs[...] = hidden.astype(BF16)
-        du = (dh * slope).astype(BF16)
-        dus[...] = du
-        db_ref[...] = jnp.sum(du.astype(F32), axis=0, keepdims=True)
-        out_ref[...] += dot(hs[...], w_d)
-        dm_ref[...] += dot(dus[...], w_u, NT)
+        n = rows // ROWB
+
+        def stage1(c):
+            at = slice(c * ROWB, (c + 1) * ROWB)
+            for k in range(FB // 256):
+                cols = slice(k * 256, (k + 1) * 256)
+                u_ref[c % 2, :, cols] = dot(m_ref[at, :], wup[slot, :, cols]) + b_ref[:, cols]
+                yield
+                h_ref[c % 2, :, cols] = dot(g_ref[at, :], wdn[slot, cols, :], NT)
+                yield
+
+        db = [None]
+
+        def stage2(c):
+            step = ROWB // 8
+            for k in range(8):
+                at = slice(k * step, (k + 1) * step)
+                to = slice(c * ROWB + k * step, c * ROWB + (k + 1) * step)
+                hidden, slope = gelu_parts(u_ref[c % 2, at, :])
+                hs[to, :] = hidden.astype(BF16)
+                du = (h_ref[c % 2, at, :] * slope).astype(BF16)
+                dus[to, :] = du
+                t = jnp.sum(du.astype(F32).reshape(step // 8, 8, FB), axis=0)
+                db[0] = t if db[0] is None else db[0] + t
+                yield
+
+        def stage3(c):
+            at = slice(c * ROWB, (c + 1) * ROWB)
+            for k in range(D // 256):
+                cols = slice(k * 256, (k + 1) * 256)
+                out_ref[at, cols] += dot(hs[at, :], wdn[slot, :, cols])
+                yield
+                dm_ref[at, cols] += dot(dus[at, :], wup[slot, cols, :], NT)
+                yield
+
+        nxt = jnp.minimum(f + 1, steps - 1)
+        for t in range(count):
+            fetch_one(nxt, 1 - slot, t)
+
+        for c in range(n + 2):
+            gens = []
+            if c < n:
+                gens.append(stage1(c))
+            if 0 <= c - 1 < n:
+                gens.append(stage2(c - 1))
+            if 0 <= c - 2 < n:
+                gens.append(stage3(c - 2))
+            interleave(*gens)
+        db_ref[...] = jnp.sum(db[0], axis=0, keepdims=True)
         gdn[slot] = dot(hs[...], g_ref[...], TN).astype(BF16)
         gup[slot] = dot(mt[...], dus[...]).astype(BF16)
-        store(f, slot)
+        for t in range(count):
+            store_one(f, slot, t)
+
 
         @pl.when(f == steps - 1)
         def _():
+            whole_wait(wup.at[1 - slot], wsem.at[0, 1 - slot])
+            whole_wait(wdn.at[1 - slot], wsem.at[1, 1 - slot])
             for sl in range(2):
                 whole_wait(gup.at[sl], gsem.at[0, sl])
                 whole_wait(gdn.at[sl], gsem.at[1, sl])
@@ -940,6 +1076,8 @@
                 pltpu.VMEM((rows, FB), BF16),
                 pltpu.VMEM((2, D, FB), BF16),
                 pltpu.VMEM((2, FB, D), BF16),
+                pltpu.VMEM((2, ROWB, FB), F32),
+                pltpu.VMEM((2, ROWB, FB), F32),
                 pltpu.SemaphoreType.DMA((2, 2)),
                 pltpu.SemaphoreType.DMA((2, 2)),
             ],
@@ -956,13 +1094,13 @@
     )(w_rows, g_rows, w_all, m, cotangent, b_up)
 
 
-def finish(w_rows, w_all, tokens, cotangent, smalls, attn_out, mlp_out, dm, dq, dk, dv, dk_back, dv_back, tables):
+def finish(w_rows, w_all, tokens, cotangent, smalls, attn_out, mlp_out, dm, dq, dk, dv, halo, tables):
     rows = tokens.shape[0]
     steps = rows // ROWB
     cos_t, fwd_t, back_t = tables
 
     def kernel(
-        w_rows_ref, w_ref, tok_ref, g_ref, small_ref, o_ref, mlp_ref, dm_ref, dq_ref, dk_ref, dv_ref, dkb_ref, dvb_ref,
+        w_rows_ref, w_ref, tok_ref, g_ref, small_ref, o_ref, mlp_ref, dm_ref, dq_ref, dk_ref, dv_ref, halo_ref,
         cos_ref, fwd_ref, back_ref,
         out_ref, dx_ref, dp_ref, a_ref, sum_ref, wqkv, wo, sems,
     ):
@@ -993,9 +1131,9 @@
         a_ref[...] = (normed * g1 + small_ref[5:6, :]).astype(BF16)
         attn = dot(o_ref[...], wo[...]) + small_ref[2:3, :]
         out_ref[...] = (x + attn + (mlp_ref[...] + small_ref[3:4, :])).astype(BF16)
-        dk_all = dk_ref[...] + dkb_ref[...].astype(F32)
+        dk_all = dk_ref[...] + halo_ref[0].astype(F32)
         dk_all = rope_rows(dk_all, cos_ref[...], -fwd_ref[...], -back_ref[...])
-        dv_all = dv_ref[...] + dvb_ref[...].astype(F32)
+        dv_all = dv_ref[...] + halo_ref[1].astype(F32)
         dq_low = dq_ref[...]
         dv_low = dv_all.astype(BF16)
         dp_ref[:, :D] = dq_low
@@ -1027,7 +1165,6 @@
     here = lambda i, *_: (i, 0)
     later = lambda i, *_: (i + steps, 0)
     block = pl.BlockSpec((ROWB, D), here)
-    upper = pl.BlockSpec((ROWB, D), later)
     table = pl.BlockSpec((ROWB, BLK), later)
     return pl.pallas_call(
         kernel,
@@ -1036,7 +1173,8 @@
             grid=(steps,),
             in_specs=[
                 ANY, block, block, pl.BlockSpec((16, D), lambda i, *_: (0, 0)),
-                block, block, block, block, upper, upper, block, block, table, table, table,
+                block, block, block, block, block, block,
+                pl.BlockSpec((2, ROWB, D), lambda i, *_: (0, i, 0)), table, table, table,
             ],
             out_specs=[
                 block, block, pl.BlockSpec((ROWB, 3 * D), here), block,
@@ -1057,7 +1195,7 @@
         ],
         compiler_params=params(dimension_semantics=("arbitrary",)),
         name="finish",
-    )(w_rows, w_all, tokens, cotangent, smalls, attn_out, mlp_out, dm, dq, dk, dv, dk_back, dv_back, cos_t, fwd_t, back_t)
+    )(w_rows, w_all, tokens, cotangent, smalls, attn_out, mlp_out, dm, dq, dk, dv, halo, cos_t, fwd_t, back_t)
 
 
 def attention_weight_grads(g_rows, grads, attn_in, d_proj, attn_out, cotangent):
@@ -1276,14 +1414,13 @@
     seg_k = jnp.concatenate([prev_seg, seg_local], axis=1).reshape(2 * rows, 1)
 
     q, k, v, d_out, m = project(w_rows, w_all, prev_tokens, tokens, cotangent, smalls, tables)
-    attn_out, dq, dk, dv, peaks = attend(
+    attn_out, dq, dk, dv, halo, peaks = attend(
         q, k, v, d_out, seg_local, seg_k, cos8[:, rows:], sin8[:, rows:]
     )
-    dk_back = passed_along(dk[:rows].astype(BF16), "seq", -1)
-    dv_back = passed_along(dv[:rows].astype(BF16), "seq", -1)
+    halo = passed_along(halo, "seq", -1)
     mlp_out, dm, db_up, grads = feed_forward(w_rows, g_rows, w_all, m, cotangent, b_up)
     block_output, input_grad, d_proj, attn_in, sums = finish(
-        w_rows, w_all, tokens, cotangent, smalls, attn_out, mlp_out, dm, dq, dk, dv, dk_back, dv_back, tables
+        w_rows, w_all, tokens, cotangent, smalls, attn_out, mlp_out, dm, dq, dk, dv, halo, tables
     )
     grads = attention_weight_grads(g_rows, grads, attn_in, d_proj, attn_out, cotangent)
 
@@ -1295,7 +1432,7 @@
         ],
         axis=1,
     ).reshape(SMALL)
-    head_peak = jnp.max(peaks.reshape(HEADS // 2, 8, QB)[:, :2, :], axis=-1).reshape(HEADS)
+    head_peak = jnp.max(peaks.reshape(HEADS // 2, 8, 2, QB)[:, 0], axis=-1).reshape(HEADS)
     if ring:
         peak_rows = jnp.zeros((8, BLK), F32).at[:, :HEADS].set(head_peak[None, :])
         extra = jnp.concatenate([small_terms.reshape(SMALL_ROWS, BLK), peak_rows], axis=0)

time: 618 us -> 548 us (0.89)
  Pallas kernels: 555 us -> 494 us
  local copies, waits for them, and re-layouts: 36.2 us -> 27.2 us
    pallas_call x1, Pallas kernels: 133 us -> 83.6 us  [attend(): pl.pallas_call(kernel, grid=(pairs,), in_specs=[block, keys, keys, block,...]
    pallas_call x1, Pallas kernels: 86.2 us -> 74.3 us  [feed_forward(): pl.pallas_call(kernel, grid_spec=pltpu.PrefetchScalarGridSpec(num_scalar_...]
    slice x2 -> x0, local copies, waits for them, and re-layouts: 7.67 us -> none  [the longest x1 3.84 us: on_device(): dv_back = passed_along(dv[:rows].astype(BF16), 'seq', -1)]
  transfers between devices with their start and end apart: 2 -> 1, of which waited for: 0 -> 0; matrix products, arithmetic and copies ran while one was open for 2% -> 1% of each run, Pallas kernels for 14% -> 14%
where the time goes in v2:
time: 548 us; the launch traced here: 544 us
  Pallas kernels  494 us (90%)
  local copies, waits for them, and re-layouts  27.2 us (5%)
  other arithmetic  17.4 us (3%)
    pallas_call x1, Pallas kernels, sum_gradients(): pl.pallas_call(kernel, out_shape=[jax.ShapeDtypeStruct((OWNED, BLK), F32)...  135 us
    pallas_call x1, Pallas kernels, gather_weights(): pl.pallas_call(kernel, out_shape=[jax.ShapeDtypeStruct((32, rows, BLK), B...  111 us
    pallas_call x1, Pallas kernels, attend(): pl.pallas_call(kernel, grid=(pairs,), in_specs=[block, keys, keys, block,...  83.6 us
    pallas_call x1, Pallas kernels, feed_forward(): pl.pallas_call(kernel, grid_spec=pltpu.PrefetchScalarGridSpec(num_scalar_...  74.3 us
    pallas_call x1, Pallas kernels, finish(): pl.pallas_call(kernel, grid_spec=pltpu.PrefetchScalarGridSpec(num_scalar_...  26.4 us
    pallas_call x1, Pallas kernels, project(): pl.pallas_call(kernel, grid_spec=pltpu.PrefetchScalarGridSpec(num_scalar_...  24.5 us
    pallas_call x1, Pallas kernels, update_tiles(): pl.pallas_call(kernel, grid=(count // group,), in_specs=[block] * 6 + [ro...  20.5 us
    pallas_call x1, Pallas kernels, attention_weight_grads(): pl.pallas_call(kernel, grid_spec=pltpu.PrefetchScalarGridSpec(num_scalar_...  19.5 us
  transfers between devices with their start and end apart: 1, of which 0 were waited for; matrix products, arithmetic and copies ran while one was open for 1% of the time, Pallas kernels for 14%

profile of v2, /device:TPU:16, one launch (start us, length us, event | category | flops | bytes accessed | tf_op | source)
XLA Modules:
  0.0 544.1 jit_solution(10632074273630132261)
XLA Ops:
  0.8 5.5 %multiply_sine_fusion = (f32[2048,8]{1,0:T(8,128)}, f32[2048,8]{1,0:T(8,128)}, f32[2048,8]{1,0:T(8,128)S(1)}) fusion(f32[2048]{0:T(1024)S(1)} %add_convert_fusion, f32[8]{0:T(128)S(1)} %negate_power_fusion), kind=kLoop, calls=%fused_computation.2 | loop fusion | flops 32768 | bytes 204832 | tf_op jit(solution)/shard_map/sin | solution.py:1403
  8.0 1.0 convert_element_type.23
  9.1 1.0 broadcast_in_dim.68
  10.1 4.9 concatenate.32.back_ref
  15.1 4.8 concatenate.31.fwd_ref
  19.9 0.9 pad_maximum_fusion.x_ref
  21.4 110.5 %gather_weights.1 = (bf16[32,3088,128]{2,1,0:T(8,128)(2,1)}, bf16[1024,1024]{1,0:T(8,128)(2,1)}, s32[8,1024]{1,0:T(8,128)}) custom-call(bf16[3088,128]{1,0:T(8,128)(2,1)} %pad_maximum_fusion.x_ref, bf16[1024,1024]{1,0:T(8,128)(2,1)} %tok_ref.5, s32[8,1024]{1,0:T(8,128)} %broadcast_in_dim.65.seg_ref), custom_call_target="tpu_custom_call" | custom-call | tf_op jit(solution)/shard_map/gather_weights/pallas_call | solution.py:312
  134.2 2.1 slice_reduce_fusion
  136.3 1.3 copy.35.sk_ref
  137.7 3.0 concatenate.30.cos_ref
  140.7 1.3 concatenate.29.small_ref
  142.0 24.5 %project.1 = (bf16[1024,1024]{1,0:T(8,128)(2,1)}, bf16[2048,1024]{1,0:T(8,128)(2,1)}, bf16[2048,1024]{1,0:T(8,128)(2,1)}, bf16[1024,1024]{1,0:T(8,128)(2,1)}, bf16[1024,1024]{1,0:T(8,128)(2,1)}) custom-call(s32[768]{0:T(1024)} %get-tuple-element.116.w_rows_ref, bf16[98816,128]{1,0:T(8,128)(2,1)} %bitcast.29, bf16[1024,1024]{1,0:T(8,128)(2,1)} %get-tuple-element.67.prev_ref, ...), custom_call_target="tpu_custom_call" | custom-call | tf_op jit(solution)/shard_map/project/pallas_call | solution.py:695
  166.5 83.6 %attend.1 = (bf16[1024,1024]{1,0:T(8,128)(2,1)}, bf16[1024,1024]{1,0:T(8,128)(2,1)}, f32[1024,1024]{1,0:T(8,128)}, f32[1024,1024]{1,0:T(8,128)}, bf16[2,1024,1024]{2,1,0:T(8,128)(2,1)}, /*index=5*/f32[64,512]{1,0:T(8,128)}) custom-call(bf16[1024,1024]{1,0:T(8,128)(2,1)} %get-tuple-element.68.q_ref, bf16[2048,1024]{1,0:T(8,128)(2,1)} %get-tuple-element.69.k_ref, ...), custom_call_target="tpu_custom_call" | custom-call | flops 42949672960 | bytes 33554432 | tf_op jit(solution)/shard_map/attend/pallas_call | solution.py:893
  250.1 3.5 collective-permute-start
  255.1 0.9 reshape.234.b_ref
  256.1 1.0 slice_reduce_fusion.8
  257.8 74.3 %feed_forward.1 = (f32[1024,1024]{1,0:T(8,128)}, f32[1024,1024]{1,0:T(8,128)}, f32[1,4096]{1,0:T(1,128)}, bf16[98304,128]{1,0:T(8,128)(2,1)}) custom-call(s32[768]{0:T(1024)} %get-tuple-element.116.w_rows_ref, s32[768]{0:T(1024)} %get-tuple-element.115.g_rows_ref, bf16[98816,128]{1,0:T(8,128)(2,1)} %bitcast.30, bf16[1024,1024]{1,0:T(8,128)(2,1)} %get-tuple-element.74.m_ref, ...), custom_call_target="tpu_custom_call" | custom-call | flops 55834574848 | bytes 50331648 | tf_op jit(solution)/shard_map/feed_forward/pallas_call | solution.py:1064
  332.6 1.4 reduce.30
  335.0 26.4 %finish.1 = (bf16[1024,1024]{1,0:T(8,128)(2,1)}, f32[1024,1024]{1,0:T(8,128)}, bf16[1024,3072]{1,0:T(8,128)(2,1)}, bf16[1024,1024]{1,0:T(8,128)(2,1)}, f32[8,1024]{1,0:T(8,128)}) custom-call(s32[768]{0:T(1024)} %get-tuple-element.116.w_rows_ref, bf16[98816,128]{1,0:T(8,128)(2,1)} %bitcast.31, bf16[1024,1024]{1,0:T(8,128)(2,1)} %tok_ref.5, ...), custom_call_target="tpu_custom_call" | custom-call | tf_op jit(solution)/shard_map/finish/pallas_call | solution.py:1169
  364.3 19.5 %attention_weight_grads.1.g_ref = bf16[98304,128]{1,0:T(8,128)(2,1)} custom-call(s32[768]{0:T(1024)} %get-tuple-element.115.g_rows_ref, bf16[1024,1024]{1,0:T(8,128)(2,1)} %get-tuple-element.83.a_ref, bf16[1024,3072]{1,0:T(8,128)(2,1)} %get-tuple-element.84.dp_ref, bf16[1024,1024]{1,0:T(8,128)(2,1)} %get-tuple-element.73.o_ref, ...), custom_call_target="tpu_custom_call", output_to_operand_aliasing={{}: (5, {})} | custom-call | tf_op jit(solution)/shard_map/attention_weight_grads/pallas_call | solution.py:1254
  383.8 135.0 %sum_gradients.1 = (f32[3072,128]{1,0:T(8,128)}, f32[104,128]{1,0:T(8,128)}) custom-call(bf16[98304,128]{1,0:T(8,128)(2,1)} %attention_weight_grads.1.g_ref, f32[104,128]{1,0:T(8,128)} %pad_maximum_fusion.2.e_ref), custom_call_target="tpu_custom_call" | custom-call | tf_op jit(solution)/shard_map/sum_gradients/pallas_call | solution.py:579
  519.6 1.2 fusion.15
  522.3 20.5 %update_tiles.1 = (f32[24,128,128]{2,1,0:T(8,128)}, bf16[24,128,128]{2,1,0:T(8,128)(2,1)}, f32[24,128,128]{2,1,0:T(8,128)}, f32[24,128,128]{2,1,0:T(8,128)}) custom-call(f32[24,128,128]{2,1,0:T(8,128)} %bitcast.32, f32[24,128,128]{2,1,0:T(8,128)} %w_ref.1, f32[24,128,128]{2,1,0:T(8,128)} %l_ref.1, f32[24,128,128]{2,1,0:T(8,128)} %r_ref.1, ...), custom_call_target="tpu_custom_call" | custom-call | tf_op jit(solution)/shard_map/update_tiles/pallas_call | solution.py:1302
  542.8 1.1 copy.41
  (57 shorter events, 12.9 us)
Async XLA Ops:
  0.6 5.7 %copy-start.4 = (f32[384]{0:T(512)S(1)}, f32[384]{0:T(512)}, u32[]{:S(2)}) copy-start(f32[384]{0:T(512)} %param.26) | copy-start | bytes 4612
  0.7 5.7 %copy-start.6 = (s32[768]{0:T(1024)S(1)}, s32[768]{0:T(1024)}, u32[]{:S(2)}) copy-start(s32[768]{0:T(1024)} %param.20) | copy-start | bytes 9220
  0.7 7.3 %copy-start = (f32[24,128,128]{2,1,0:T(8,128)S(1)}, f32[24,128,128]{2,1,0:T(8,128)}, u32[]{:S(2)}) copy-start(f32[24,128,128]{2,1,0:T(8,128)} %w_ref.1) | copy-start | bytes 4718596
  15.1 4.8 copy-start.2
  15.1 5.8 %copy-start.3 = (s32[1,1024]{1,0:T(1,128)S(1)}, s32[1,1024]{1,0:T(1,128)}, u32[]{:S(2)}) copy-start(s32[1,1024]{1,0:T(1,128)} %sq_ref.1) | copy-start | bytes 12292
  250.1 84.9 %collective-permute-start = (bf16[2,1024,1024]{2,1,0:T(8,128)(2,1)}, bf16[2,1024,1024]{2,1,0:T(8,128)(2,1)}, u32[]{:S(2)}, u32[]{:S(2)}) collective-permute-start(bf16[2,1024,1024]{2,1,0:T(8,128)(2,1)} %get-tuple-element.80), channel_id=1, source_target_pairs={{1,0},{2,1},{3,2},{4,3},{5,4},{6,5},{7,6},{9,8},{10,9},{11,10},{12... | collective-permute-start | bytes 12582920 | tf_op jit(solution)/shard_map/ppermute | solution.py:1335
  383.8 137.9 %copy-start.5 = (f32[384]{0:T(512)S(1)}, f32[384]{0:T(512)}, u32[]{:S(2)}) copy-start(f32[384]{0:T(512)} %param.26) | copy-start | bytes 4612
  383.8 137.9 %copy-start.7 = (f32[384]{0:T(512)S(1)}, f32[384]{0:T(512)}, u32[]{:S(2)}) copy-start(f32[384]{0:T(512)} %param.27) | copy-start | bytes 4612
  383.8 137.9 %copy-start.8 = (f32[384]{0:T(512)S(1)}, f32[384]{0:T(512)}, u32[]{:S(2)}) copy-start(f32[384]{0:T(512)} %param.28) | copy-start | bytes 4612
  522.3 20.5 %copy-start.1 = (f32[3072,128]{1,0:T(8,128)S(1)}, f32[3072,128]{1,0:T(8,128)}, u32[]{:S(2)}) copy-start(f32[3072,128]{1,0:T(8,128)} %get-tuple-element.89) | copy-start | bytes 4718596

commit v3 on v2

--- a/solution.py
+++ b/solution.py
@@ -164,6 +164,12 @@
 
         def from_y(zz):
             return remote(x_ref, place(yn, zz), 3, zz, (yn, s))
+
+        def diag_up(zz):
+            return remote(place(xyn, zz), place(xyn, zz), 10, zz, (d, s + 2))
+
+        def diag_down(zz):
+            return remote(place(xyn, zz), place(xyn, zz), 11, zz, (d, s - 2))
 
         def diag_top(zz):
             return remote(x_ref.at[top], place(xyn, zz).at[top], 4, zz, (yn, s))
@@ -194,6 +200,12 @@
             )
             return tok, seg
 
+        def in_plane(k, body):
+            if k == 0:
+                body()
+            elif k == 3:
+                pl.when((z == 0) | (z == 3))(body)
+
         def launch(k):
             zz = order[k]
             own = k == 0
@@ -231,16 +243,40 @@
         def second(k):
             zz = order[k]
             from_x(zz).wait_recv()
-            on_y(zz).start()
+            in_plane(k, lambda: on_y(zz).start())
             to_sib(xn, zz, 7).start()
             from_y(zz).wait_recv()
-            on_x(zz).start()
+            in_plane(k, lambda: on_x(zz).start())
             to_sib(yn, zz, 8).start()
 
         def third(k):
             zz = order[k]
-            diag_top(zz).wait_recv()
-            diag_low(zz).wait_recv()
+
+            def arrive():
+                diag_top(zz).wait_recv()
+                diag_low(zz).wait_recv()
+
+            in_plane(k, arrive)
+            if k > 0:
+
+                @pl.when((zz < z) & (z - zz <= 2))
+                def _():
+                    diag_up(zz).wait_recv()
+
+                @pl.when((zz > z) & (zz - z <= 2))
+                def _():
+                    diag_down(zz).wait_recv()
+
+            if k < 3:
+
+                @pl.when((zz <= z) & (z - zz <= 1) & (z < 3))
+                def _():
+                    diag_up(zz).start()
+
+                @pl.when((zz >= z) & (zz - z <= 1) & (z > 0))
+                def _():
+                    diag_down(zz).start()
+
             to_sib(xyn, zz, 9).start()
 
         launch(0)
@@ -283,8 +319,21 @@
                 to_sib(dd, zz, kind, own and kind == 6).wait_send()
             to_x(zz, own).wait_send()
             to_y(zz, own).wait_send()
-            on_y(zz).wait_send()
-            on_x(zz).wait_send()
+
+            def halves_sent():
+                on_y(zz).wait_send()
+                on_x(zz).wait_send()
+
+            in_plane(k, halves_sent)
+            if k < 3:
+
+                @pl.when((zz <= z) & (z - zz <= 1) & (z < 3))
+                def _():
+                    diag_up(zz).wait_send()
+
+                @pl.when((zz >= z) & (zz - z <= 1) & (z > 0))
+                def _():
+                    diag_down(zz).wait_send()
 
             @pl.when((zz <= z) & (z < 3))
             def _():
@@ -320,8 +369,8 @@
         out_specs=[ANY, ANY, ANY],
         scratch_shapes=[
             pltpu.SemaphoreType.DMA,
-            pltpu.SemaphoreType.DMA((10, 4)),
-            pltpu.SemaphoreType.DMA((10, 4)),
+            pltpu.SemaphoreType.DMA((12, 4)),
+            pltpu.SemaphoreType.DMA((12, 4)),
             pltpu.SemaphoreType.DMA((2,)),
             pltpu.SemaphoreType.DMA((2,)),
             pltpu.SemaphoreType.DMA((2,)),
@@ -337,20 +386,23 @@
 EXTRA_ROWS = SMALL_ROWS + 8
 
 
-def add_rows(dst, terms, rows, step=256):
+def add_rows(dst, terms, rows, step=512):
     def body(i, carry):
         at = pl.ds(pl.multiple_of(i * step, step), step)
-        total = terms[0][at].astype(F32)
-        for term in terms[1:]:
-            total = total + term[at].astype(F32)
-        dst[at] = total.astype(dst.dtype)
+        if len(terms) == 2 and dst.dtype == BF16:
+            dst[at] = terms[0][at] + terms[1][at]
+        else:
+            total = terms[0][at].astype(F32)
+            for term in terms[1:]:
+                total = total + term[at].astype(F32)
+            dst[at] = total.astype(dst.dtype)
         return carry
 
     lax.fori_loop(0, rows // step, body, 0)
 
 
 def sum_gradients(grads, extra):
-    def kernel(g_ref, e_ref, out_ref, eout_ref, own, crecv, s1a, s1b, s2, zup, zdn, epart, erecv, ls, ss, rs, zss, zrs, es, er):
+    def kernel(g_ref, e_ref, out_ref, eout_ref, own, crecv, s1a, s1b, s2, zup, zdn, gup, gdn, epart, erecv, ls, ss, rs, zss, zrs, es, er):
         d = lax.axis_index("dp")
         s = lax.axis_index("seq")
         z = s // 2
@@ -428,6 +480,73 @@
         def z_dn(zz):
             return remote(own.at[zz, d], zdn.at[zz], zss.at[1, zz], zrs.at[1, zz], (d, s - 2))
 
+        def g_up(zz):
+            return remote(own.at[zz, xyn], gup.at[zz], zss.at[2, zz], zrs.at[2, zz], (d, s + 2))
+
+        def g_dn(zz):
+            return remote(own.at[zz, xyn], gdn.at[zz], zss.at[3, zz], zrs.at[3, zz], (d, s - 2))
+
+        ends = (z == 0) | (z == 3)
+        inner = (z == 1) | (z == 2)
+
+        def in_plane(k, body):
+            if k == 3:
+                body()
+            elif k == 0:
+                pl.when(ends)(body)
+
+        def cross(zz):
+            y_cross(zz).start()
+            x_cross(zz).start()
+
+        def along(zz, act):
+            @pl.when(zz > z)
+            def _():
+                act(g_up(zz))
+
+            @pl.when(zz < z)
+            def _():
+                act(g_dn(zz))
+
+        def outward(k, act):
+            zz = order[k]
+            if k == 0:
+                pl.when(inner)(lambda: along(zz, act))
+            elif k < 3:
+                along(zz, act)
+
+        def diagonal(k):
+            zz = order[k]
+            mine = own.at[zz, xyn]
+            if k < 3:
+
+                @pl.when(inner)
+                def _():
+                    @pl.when(zz > z)
+                    def _():
+                        g_up(zz).wait_recv()
+                        add_rows(mine, [mine, gup.at[zz]], OWNED)
+
+                    @pl.when(zz < z)
+                    def _():
+                        g_dn(zz).wait_recv()
+                        add_rows(mine, [mine, gdn.at[zz]], OWNED)
+
+                    along(zz, lambda cp: cp.start())
+            else:
+
+                @pl.when(z > 0)
+                def _():
+                    g_up(zz).wait_recv()
+                    add_rows(mine, [mine, gup.at[zz]], OWNED)
+
+                @pl.when(z < 3)
+                def _():
+                    g_dn(zz).wait_recv()
+                    add_rows(mine, [mine, gdn.at[zz]], OWNED)
+
+                cross(zz)
+
         def extra_step(i, dev):
             return remote(epart.at[i], erecv.at[i], es.at[i], er.at[i], dev)
 
@@ -445,15 +564,18 @@
             else:
                 eout_ref[...] = total
 
-        for k in range(4):
-            for dd in range(4):
+        def issue(k):
+            for dd in (xyn, yn, xn, d):
                 core(order[k], dd).start()
-            if k == 0:
-                epart[0] = e_ref[...]
-                extra_step(0, extra_devs[0]).start()
+
+        issue(0)
+        epart[0] = e_ref[...]
+        extra_step(0, extra_devs[0]).start()
 
         def first(k):
             zz = order[k]
+            if k < 3:
+                issue(k + 1)
 
             def one(dd, start):
                 load(zz, dd).wait()
@@ -462,20 +584,32 @@
                 for cp in start:
                     cp.start()
 
-            one(xyn, [y_cross(zz), x_cross(zz)])
+            one(xyn, [])
+            if k == 0:
+                pl.when(ends)(lambda: cross(zz))
+                outward(0, lambda cp: cp.start())
+            elif k < 3:
+                pl.when(ends)(lambda: along(zz, lambda cp: cp.start()))
             one(yn, [y_own(zz)])
             one(xn, [x_own(zz)])
             one(d, [])
 
         def second(k):
             zz = order[k]
-            y_cross(zz).wait_recv()
             a = own.at[zz, xn, top]
-            add_rows(a, [a, s1a.at[zz, 1]], HALF)
+            b = own.at[zz, yn, low]
+
+            def crossed():
+                y_cross(zz).wait_recv()
+                add_rows(a, [a, s1a.at[zz, 1]], HALF)
+
+            def crossed_low():
+                x_cross(zz).wait_recv()
+                add_rows(b, [b, s1b.at[zz, 1]], HALF)
+
+            in_plane(k, crossed)
             x_last(zz).start()
-            x_cross(zz).wait_recv()
-            b = own.at[zz, yn, low]
-            add_rows(b, [b, s1b.at[zz, 1]], HALF)
+            in_plane(k, crossed_low)
             y_last(zz).start()
 
         def third(k):
@@ -544,18 +678,21 @@
         first(1)
         extra_add(0)
         second(0)
+        diagonal(1)
         first(2)
+        second(1)
         extra_add(1)
+        first(3)
+        diagonal(2)
+        second(2)
         third(0)
-        second(1)
-        first(3)
         extra_add(2)
+        diagonal(3)
+        extra_add(3)
         third(1)
-        second(2)
-        extra_add(3)
+        extra_add(4)
         third(2)
         second(3)
-        extra_add(4)
         third(3)
 
         for i in range(5):
@@ -564,8 +701,15 @@
             zz = order[k]
             for dd in range(4):
                 core(zz, dd).wait_send()
-            for cp in (y_own(zz), y_cross(zz), x_own(zz), x_cross(zz), x_last(zz), y_last(zz)):
+            for cp in (y_own(zz), x_own(zz), x_last(zz), y_last(zz)):
                 cp.wait_send()
+
+            def crosses_sent():
+                y_cross(zz).wait_send()
+                x_cross(zz).wait_send()
+
+            in_plane(k, crosses_sent)
+            outward(k, lambda cp: cp.wait_send())
             if k < 3:
 
                 @pl.when(zz > z)
@@ -592,13 +736,15 @@
             pltpu.VMEM((4, OWNED, BLK), BF16),
             pltpu.VMEM((4, OWNED, BLK), BF16),
             pltpu.VMEM((4, OWNED, BLK), BF16),
+            pltpu.VMEM((4, OWNED, BLK), BF16),
+            pltpu.VMEM((4, OWNED, BLK), BF16),
             pltpu.VMEM((5, EXTRA_ROWS, BLK), F32),
             pltpu.VMEM((5, EXTRA_ROWS, BLK), F32),
             pltpu.SemaphoreType.DMA((4, 4)),
             pltpu.SemaphoreType.DMA((4, 10)),
             pltpu.SemaphoreType.DMA((4, 10)),
-            pltpu.SemaphoreType.DMA((2, 4)),
-            pltpu.SemaphoreType.DMA((2, 4)),
+            pltpu.SemaphoreType.DMA((4, 4)),
+            pltpu.SemaphoreType.DMA((4, 4)),
             pltpu.SemaphoreType.DMA((5,)),
             pltpu.SemaphoreType.DMA((5,)),
         ],
@@ -620,13 +766,22 @@
     return jnp.concatenate(pieces, axis=1)
 
 
+def spread_tables(cos8, sin8):
+    none = jnp.zeros_like(cos8)
+    rest = (HEAD - ROT) // none.shape[0]
+    cos_t = [cos8, cos8] + [none + 1.0] * rest
+    fwd_t = [-sin8, none] + [none] * rest
+    back_t = [none, sin8] + [none] * rest
+    return [jnp.concatenate(t * 2, axis=0).T for t in (cos_t, fwd_t, back_t)]
+
+
 def project(w_rows, w_all, prev_tokens, tokens, cotangent, smalls, tables):
     rows = tokens.shape[0]
     steps = rows // ROWB
-    cos_t, fwd_t, back_t = tables
+    cos8, sin8 = tables
 
     def kernel(
-        w_rows_ref, w_ref, prev_ref, tok_ref, g_ref, small_ref, cos_ref, fwd_ref, back_ref,
+        w_rows_ref, w_ref, prev_ref, tok_ref, g_ref, small_ref, cos_ref, sin_ref,
         q_ref, k_ref, v_ref, do_ref, m_ref, wqkv, wo, sems,
     ):
         i = pl.program_id(0)
@@ -665,12 +820,14 @@
             third_wait(0)
             pltpu.make_async_copy(wo, wo, sems.at[3]).wait()
 
+        spread = spread_tables(cos_ref[...], sin_ref[...])
+
         def keys(x):
             normed, _ = norm_rows(x)
             attn_in = (normed * small_ref[4:5, :] + small_ref[5:6, :]).astype(BF16)
             k = dot(attn_in, wqkv[:, D : 2 * D])
             v = dot(attn_in, wqkv[:, 2 * D :]) + small_ref[1:2, :]
-            k_ref[...] = rope_rows(k, cos_ref[...], fwd_ref[...], back_ref[...]).astype(BF16)
+            k_ref[...] = rope_rows(k, *spread).astype(BF16)
             v_ref[...] = v.astype(BF16)
             return normed, attn_in
 
@@ -683,7 +840,7 @@
             normed, attn_in = keys(tok_ref[...].astype(F32))
             m_ref[...] = (normed * small_ref[6:7, :] + small_ref[7:8, :]).astype(BF16)
             q = dot(attn_in, wqkv[:, :D]) + small_ref[0:1, :]
-            q = rope_rows(q, cos_ref[...], fwd_ref[...], back_ref[...])
+            q = rope_rows(q, *spread)
             q_ref[...] = q.astype(BF16)
             do_ref[...] = dot(g_ref[...], wo[...], NT).astype(BF16)
 
@@ -691,7 +848,7 @@
     prev = lambda i, *_: (jnp.minimum(i, steps - 1), 0)
     here = lambda i, *_: (i, 0)
     block = lambda m: pl.BlockSpec((ROWB, D), m)
-    table = pl.BlockSpec((ROWB, BLK), here)
+    table = pl.BlockSpec((ROT // 2, ROWB), lambda i, *_: (0, i))
     return pl.pallas_call(
         kernel,
         grid_spec=pltpu.PrefetchScalarGridSpec(
@@ -699,7 +856,7 @@
             grid=(2 * steps,),
             in_specs=[
                 ANY, block(prev), block(own), block(own),
-                pl.BlockSpec((16, D), lambda i, *_: (0, 0)), table, table, table,
+                pl.BlockSpec((16, D), lambda i, *_: (0, 0)), table, table,
             ],
             out_specs=[block(own), block(here), block(here), block(own), block(own)],
             scratch_shapes=[
@@ -717,7 +874,7 @@
         ],
         compiler_params=params(dimension_semantics=("arbitrary",)),
         name="project",
-    )(w_rows, w_all, prev_tokens, tokens, cotangent, smalls, cos_t, fwd_t, back_t)
+    )(w_rows, w_all, prev_tokens, tokens, cotangent, smalls, cos8, sin8)
 
 
 QB = 256
@@ -1097,11 +1254,11 @@
 def finish(w_rows, w_all, tokens, cotangent, smalls, attn_out, mlp_out, dm, dq, dk, dv, halo, tables):
     rows = tokens.shape[0]
     steps = rows // ROWB
-    cos_t, fwd_t, back_t = tables
+    cos8, sin8 = tables
 
     def kernel(
         w_rows_ref, w_ref, tok_ref, g_ref, small_ref, o_ref, mlp_ref, dm_ref, dq_ref, dk_ref, dv_ref, halo_ref,
-        cos_ref, fwd_ref, back_ref,
+        cos_ref, sin_ref,
         out_ref, dx_ref, dp_ref, a_ref, sum_ref, wqkv, wo, sems,
     ):
         i = pl.program_id(0)
@@ -1132,7 +1289,7 @@
         attn = dot(o_ref[...], wo[...]) + small_ref[2:3, :]
         out_ref[...] = (x + attn + (mlp_ref[...] + small_ref[3:4, :])).astype(BF16)
         dk_all = dk_ref[...] + halo_ref[0].astype(F32)
-        dk_all = rope_rows(dk_all, cos_ref[...], -fwd_ref[...], -back_ref[...])
+        dk_all = rope_rows(dk_all, *spread_tables(cos_ref[...], -sin_ref[...]))
         dv_all = dv_ref[...] + halo_ref[1].astype(F32)
         dq_low = dq_ref[...]
         dv_low = dv_all.astype(BF16)
@@ -1163,9 +1320,8 @@
         add(6, dmv)
 
     here = lambda i, *_: (i, 0)
-    later = lambda i, *_: (i + steps, 0)
     block = pl.BlockSpec((ROWB, D), here)
-    table = pl.BlockSpec((ROWB, BLK), later)
+    table = pl.BlockSpec((ROT // 2, ROWB), lambda i, *_: (0, i + steps))
     return pl.pallas_call(
         kernel,
         grid_spec=pltpu.PrefetchScalarGridSpec(
@@ -1174,7 +1330,7 @@
             in_specs=[
                 ANY, block, block, pl.BlockSpec((16, D), lambda i, *_: (0, 0)),
                 block, block, block, block, block, block,
-                pl.BlockSpec((2, ROWB, D), lambda i, *_: (0, i, 0)), table, table, table,
+                pl.BlockSpec((2, ROWB, D), lambda i, *_: (0, i, 0)), table, table,
             ],
             out_specs=[
                 block, block, pl.BlockSpec((ROWB, 3 * D), here), block,
@@ -1195,7 +1351,7 @@
         ],
         compiler_params=params(dimension_semantics=("arbitrary",)),
         name="finish",
-    )(w_rows, w_all, tokens, cotangent, smalls, attn_out, mlp_out, dm, dq, dk, dv, halo, cos_t, fwd_t, back_t)
+    )(w_rows, w_all, tokens, cotangent, smalls, attn_out, mlp_out, dm, dq, dk, dv, halo, cos8, sin8)
 
 
 def attention_weight_grads(g_rows, grads, attn_in, d_proj, attn_out, cotangent):
@@ -1278,18 +1434,30 @@
     )(g_rows, attn_in, d_proj, attn_out, cotangent, grads)
 
 
+def halves(x):
+    high = x.astype(BF16)
+    return high, (x - high.astype(F32)).astype(BF16)
+
+
+def dot3(a, b, dims=NN):
+    return dot(a[0], b[0], dims) + (dot(a[0], b[1], dims) + dot(a[1], b[0], dims))
+
+
 def update_tiles(grads, tiles, left, right, first, second, scale):
     count = tiles.shape[0]
-    group = max(g for g in (1, 2, 3, 4) if count % g == 0)
+    group = max(g for g in (1, 2, 3, 4, 6, 8) if count % g == 0)
 
     def kernel(g_ref, w_ref, l_ref, r_ref, m_ref, v_ref, s_ref, w_out, low_out, m_out, v_out):
+        turned = []
         for t in range(group):
-            l, r = l_ref[t], r_ref[t]
-            turned = dot(dot(l, g_ref[t], TN, HIGH), r, NN, HIGH)
-            m_new = BETA * m_ref[t] + (1.0 - BETA) * turned
-            v_new = BETA * v_ref[t] + (1.0 - BETA) * turned * turned
+            l, r = halves(l_ref[t]), halves(r_ref[t])
+            turned.append(dot3(halves(dot3(l, halves(g_ref[t]), TN)), r))
+        for t in range(group):
+            l, r = halves(l_ref[t]), halves(r_ref[t])
+            m_new = BETA * m_ref[t] + (1.0 - BETA) * turned[t]
+            v_new = BETA * v_ref[t] + (1.0 - BETA) * turned[t] * turned[t]
             ratio = m_new / (jnp.sqrt(v_new) + ADAM_EPS)
-            back = dot(dot(l, ratio, NN, HIGH), r, NT, HIGH)
+            back = dot3(halves(dot3(l, halves(ratio))), r, NT)
             w_new = (w_ref[t] - LEARN * back) * s_ref[t]
             w_out[t] = w_new
             low_out[t] = w_new.astype(BF16)
@@ -1401,14 +1569,7 @@
     places = first_place - rows + jnp.arange(2 * rows, dtype=jnp.int32)
     angle = places.astype(F32)[None, :] * frequency[:, None]
     cos8, sin8 = jnp.cos(angle), jnp.sin(angle)
-    cos_c, sin_c = cos8.T, sin8.T
-    ones = jnp.ones((2 * rows, HEAD - ROT), F32)
-    none = jnp.zeros((2 * rows, half), F32)
-    rest = jnp.zeros((2 * rows, HEAD - ROT), F32)
-    cos_t = jnp.concatenate([cos_c, cos_c, ones] * 2, axis=1)
-    fwd_t = jnp.concatenate([-sin_c, none, rest] * 2, axis=1)
-    back_t = jnp.concatenate([none, sin_c, rest] * 2, axis=1)
-    tables = (cos_t, fwd_t, back_t)
+    tables = (cos8, sin8)
 
     prev_seg = jnp.where(seq_index == 0, -1, prev_seg)
     seg_k = jnp.concatenate([prev_seg, seg_local], axis=1).reshape(2 * rows, 1)

time: 548 us -> 509 us (0.929)
  Pallas kernels: 494 us -> 468 us
  local copies, waits for them, and re-layouts: 27.2 us -> 13.7 us
    concatenate x3 -> x0, local copies, waits for them, and re-layouts: 12.7 us -> none  [the longest x1 4.94 us: on_device(): back_t = jnp.concatenate([none, sin_c, rest] * 2, axis=1)]
    pallas_call x1, Pallas kernels: 20.5 us -> 9.01 us  [update_tiles(): pl.pallas_call(kernel, grid=(count // group,), in_specs=[block] * 6 + [ro...]
    pallas_call x1, Pallas kernels: 135 us -> 125 us  [sum_gradients(): pl.pallas_call(kernel, out_shape=[jax.ShapeDtypeStruct((OWNED, BLK), F32)...]
    pallas_call x1, Pallas kernels: 111 us -> 104 us  [gather_weights(): pl.pallas_call(kernel, out_shape=[jax.ShapeDtypeStruct((32, rows, BLK), B...]
  transfers between devices with their start and end apart: 1 -> 1, of which waited for: 0 -> 0; matrix products, arithmetic and copies ran while one was open for 1% -> 2% of each run, Pallas kernels for 14% -> 15%
where the time goes in v3:
time: 509 us; the launch traced here: 500 us
  Pallas kernels  468 us (92%)
  other arithmetic  15.4 us (3%)
  local copies, waits for them, and re-layouts  13.7 us (3%)
    pallas_call x1, Pallas kernels, sum_gradients(): pl.pallas_call(kernel, out_shape=[jax.ShapeDtypeStruct((OWNED, BLK), F32)...  125 us
    pallas_call x1, Pallas kernels, gather_weights(): pl.pallas_call(kernel, out_shape=[jax.ShapeDtypeStruct((32, rows, BLK), B...  104 us
    pallas_call x1, Pallas kernels, attend(): pl.pallas_call(kernel, grid=(pairs,), in_specs=[block, keys, keys, block,...  83.6 us
    pallas_call x1, Pallas kernels, feed_forward(): pl.pallas_call(kernel, grid_spec=pltpu.PrefetchScalarGridSpec(num_scalar_...  74.3 us
    pallas_call x1, Pallas kernels, finish(): pl.pallas_call(kernel, grid_spec=pltpu.PrefetchScalarGridSpec(num_scalar_...  26.3 us
    pallas_call x1, Pallas kernels, project(): pl.pallas_call(kernel, grid_spec=pltpu.PrefetchScalarGridSpec(num_scalar_...  25.7 us
    pallas_call x1, Pallas kernels, attention_weight_grads(): pl.pallas_call(kernel, grid_spec=pltpu.PrefetchScalarGridSpec(num_scalar_...  19.5 us
  transfers between devices with their start and end apart: 1, of which 0 were waited for; matrix products, arithmetic and copies ran while one was open for 2% of the time, Pallas kernels for 15%

profile of v3, /device:TPU:16, one launch (start us, length us, event | category | flops | bytes accessed | tf_op | source)
XLA Modules:
  0.0 500.4 jit_solution(2311693900110756919)
XLA Ops:
  1.4 1.0 select_reduce_fusion
  4.5 1.5 convert_element_type.23
  6.1 0.9 pad_maximum_fusion.x_ref
  7.6 103.9 %gather_weights.1 = (bf16[32,3088,128]{2,1,0:T(8,128)(2,1)}, bf16[1024,1024]{1,0:T(8,128)(2,1)}, s32[8,1024]{1,0:T(8,128)}) custom-call(bf16[3088,128]{1,0:T(8,128)(2,1)} %pad_maximum_fusion.x_ref, bf16[1024,1024]{1,0:T(8,128)(2,1)} %tok_ref.5, s32[8,1024]{1,0:T(8,128)} %broadcast_in_dim.56.seg_ref), custom_call_target="tpu_custom_call" | custom-call | tf_op jit(solution)/shard_map/gather_weights/pallas_call | solution.py:361
  111.6 0.8 broadcast_select_fusion
  112.4 0.8 slice_convert_fusion
  113.8 2.1 slice_reduce_fusion
  115.9 1.3 copy.31.sk_ref
  117.3 1.3 concatenate.20.small_ref
  118.6 25.7 %project.1 = (bf16[1024,1024]{1,0:T(8,128)(2,1)}, bf16[2048,1024]{1,0:T(8,128)(2,1)}, bf16[2048,1024]{1,0:T(8,128)(2,1)}, bf16[1024,1024]{1,0:T(8,128)(2,1)}, bf16[1024,1024]{1,0:T(8,128)(2,1)}) custom-call(s32[768]{0:T(1024)} %get-tuple-element.113.w_rows_ref, bf16[98816,128]{1,0:T(8,128)(2,1)} %bitcast.29, bf16[1024,1024]{1,0:T(8,128)(2,1)} %get-tuple-element.67.prev_ref, ...), custom_call_target="tpu_custom_call" | custom-call | tf_op jit(solution)/shard_map/project/pallas_call | solution.py:852
  144.3 83.6 %attend.1 = (bf16[1024,1024]{1,0:T(8,128)(2,1)}, bf16[1024,1024]{1,0:T(8,128)(2,1)}, f32[1024,1024]{1,0:T(8,128)}, f32[1024,1024]{1,0:T(8,128)}, bf16[2,1024,1024]{2,1,0:T(8,128)(2,1)}, /*index=5*/f32[64,512]{1,0:T(8,128)}) custom-call(bf16[1024,1024]{1,0:T(8,128)(2,1)} %get-tuple-element.68.q_ref, bf16[2048,1024]{1,0:T(8,128)(2,1)} %get-tuple-element.69.k_ref, ...), custom_call_target="tpu_custom_call" | custom-call | flops 42949672960 | bytes 33554432 | tf_op jit(solution)/shard_map/attend/pallas_call | solution.py:1050
  227.9 1.9 collective-permute-start
  231.3 0.9 reshape.234.b_ref
  232.3 1.0 slice_reduce_fusion.8
  234.0 74.3 %feed_forward.1 = (f32[1024,1024]{1,0:T(8,128)}, f32[1024,1024]{1,0:T(8,128)}, f32[1,4096]{1,0:T(1,128)}, bf16[98304,128]{1,0:T(8,128)(2,1)}) custom-call(s32[768]{0:T(1024)} %get-tuple-element.113.w_rows_ref, s32[768]{0:T(1024)} %get-tuple-element.112.g_rows_ref, bf16[98816,128]{1,0:T(8,128)(2,1)} %bitcast.30, bf16[1024,1024]{1,0:T(8,128)(2,1)} %get-tuple-element.74.m_ref, ...), custom_call_target="tpu_custom_call" | custom-call | flops 55834574848 | bytes 50331648 | tf_op jit(solution)/shard_map/feed_forward/pallas_call | solution.py:1221
  308.8 1.4 reduce.30
  311.0 0.8 fusion.11
  312.6 26.3 %finish.1 = (bf16[1024,1024]{1,0:T(8,128)(2,1)}, f32[1024,1024]{1,0:T(8,128)}, bf16[1024,3072]{1,0:T(8,128)(2,1)}, bf16[1024,1024]{1,0:T(8,128)(2,1)}, f32[8,1024]{1,0:T(8,128)}) custom-call(s32[768]{0:T(1024)} %get-tuple-element.113.w_rows_ref, bf16[98816,128]{1,0:T(8,128)(2,1)} %bitcast.31, bf16[1024,1024]{1,0:T(8,128)(2,1)} %tok_ref.5, ...), custom_call_target="tpu_custom_call" | custom-call | tf_op jit(solution)/shard_map/finish/pallas_call | solution.py:1325
  341.7 19.5 %attention_weight_grads.1.g_ref = bf16[98304,128]{1,0:T(8,128)(2,1)} custom-call(s32[768]{0:T(1024)} %get-tuple-element.112.g_rows_ref, bf16[1024,1024]{1,0:T(8,128)(2,1)} %get-tuple-element.83.a_ref, bf16[1024,3072]{1,0:T(8,128)(2,1)} %get-tuple-element.84.dp_ref, bf16[1024,1024]{1,0:T(8,128)(2,1)} %get-tuple-element.73.o_ref, ...), custom_call_target="tpu_custom_call", output_to_operand_aliasing={{}: (5, {})} | custom-call | tf_op jit(solution)/shard_map/attention_weight_grads/pallas_call | solution.py:1410
  361.3 125.2 %sum_gradients.1 = (f32[3072,128]{1,0:T(8,128)}, f32[104,128]{1,0:T(8,128)}) custom-call(bf16[98304,128]{1,0:T(8,128)(2,1)} %attention_weight_grads.1.g_ref, f32[104,128]{1,0:T(8,128)} %pad_maximum_fusion.2.e_ref), custom_call_target="tpu_custom_call" | custom-call | tf_op jit(solution)/shard_map/sum_gradients/pallas_call | solution.py:723
  486.5 0.8 slice_bitcast_fusion
  487.3 1.2 fusion.14
  490.1 9.0 %update_tiles.1 = (f32[24,128,128]{2,1,0:T(8,128)}, bf16[24,128,128]{2,1,0:T(8,128)(2,1)}, f32[24,128,128]{2,1,0:T(8,128)}, f32[24,128,128]{2,1,0:T(8,128)}) custom-call(f32[24,128,128]{2,1,0:T(8,128)} %bitcast.32, f32[24,128,128]{2,1,0:T(8,128)} %w_ref.1, f32[24,128,128]{2,1,0:T(8,128)} %l_ref.1, f32[24,128,128]{2,1,0:T(8,128)} %r_ref.1, ...), custom_call_target="tpu_custom_call" | custom-call | tf_op jit(solution)/shard_map/update_tiles/pallas_call | solution.py:1470
  499.1 1.1 copy.37
  (47 shorter events, 12.0 us)
Async XLA Ops:
  3.0 4.0 copy-start.3
  3.3 108.3 %copy-start.1 = (f32[8,2048]{1,0:T(8,128)}, f32[8,2048]{1,0:T(8,128)S(1)}, u32[]{:S(2)}) copy-start(f32[8,2048]{1,0:T(8,128)S(1)} %get-tuple-element.110.sin_ref) | copy-start | bytes 196612
  3.3 108.3 %copy-start.2 = (f32[8,2048]{1,0:T(8,128)}, f32[8,2048]{1,0:T(8,128)S(1)}, u32[]{:S(2)}) copy-start(f32[8,2048]{1,0:T(8,128)S(1)} %get-tuple-element.111.cos_ref) | copy-start | bytes 196612
  227.9 84.7 %collective-permute-start = (bf16[2,1024,1024]{2,1,0:T(8,128)(2,1)}, bf16[2,1024,1024]{2,1,0:T(8,128)(2,1)}, u32[]{:S(2)}, u32[]{:S(2)}) collective-permute-start(bf16[2,1024,1024]{2,1,0:T(8,128)(2,1)} %get-tuple-element.80), channel_id=1, source_target_pairs={{1,0},{2,1},{3,2},{4,3},{5,4},{6,5},{7,6},{9,8},{10,9},{11,10},{12... | collective-permute-start | bytes 12582920 | tf_op jit(solution)/shard_map/ppermute | solution.py:1503
  361.3 128.1 %copy-start.4 = (f32[384]{0:T(512)S(1)}, f32[384]{0:T(512)}, u32[]{:S(2)}) copy-start(f32[384]{0:T(512)} %param.26) | copy-start | bytes 4612
  361.3 128.1 %copy-start.5 = (f32[384]{0:T(512)S(1)}, f32[384]{0:T(512)}, u32[]{:S(2)}) copy-start(f32[384]{0:T(512)} %param.27) | copy-start | bytes 4612
  361.3 128.1 %copy-start.6 = (f32[384]{0:T(512)S(1)}, f32[384]{0:T(512)}, u32[]{:S(2)}) copy-start(f32[384]{0:T(512)} %param.28) | copy-start | bytes 4612
  490.1 9.0 %copy-start = (f32[3072,128]{1,0:T(8,128)S(1)}, f32[3072,128]{1,0:T(8,128)}, u32[]{:S(2)}) copy-start(f32[3072,128]{1,0:T(8,128)} %get-tuple-element.89) | copy-start | bytes 4718596

commit v4 on v3

--- a/solution.py
+++ b/solution.py
@@ -203,8 +203,11 @@
         def in_plane(k, body):
             if k == 0:
                 body()
-            elif k == 3:
-                pl.when((z == 0) | (z == 3))(body)
+            else:
+                pl.when((z - order[k] >= 2) | (order[k] - z >= 3))(body)
+
+        def on_line(k, body):
+            pl.when((z - order[k] < 2) & (order[k] - z < 3))(body)
 
         def launch(k):
             zz = order[k]
@@ -242,12 +245,27 @@
 
         def second(k):
             zz = order[k]
-            from_x(zz).wait_recv()
-            in_plane(k, lambda: on_y(zz).start())
-            to_sib(xn, zz, 7).start()
-            from_y(zz).wait_recv()
-            in_plane(k, lambda: on_x(zz).start())
-            to_sib(yn, zz, 8).start()
+
+            def pass_on():
+                from_x(zz).wait_recv()
+                on_y(zz).start()
+                to_sib(xn, zz, 7).start()
+                from_y(zz).wait_recv()
+                on_x(zz).start()
+                to_sib(yn, zz, 8).start()
+
+            in_plane(k, pass_on)
+
+        def rest(k):
+            zz = order[k]
+
+            def share():
+                from_x(zz).wait_recv()
+                to_sib(xn, zz, 7).start()
+                from_y(zz).wait_recv()
+                to_sib(yn, zz, 8).start()
+
+            on_line(k, share)
 
         def third(k):
             zz = order[k]
@@ -259,7 +277,7 @@
             in_plane(k, arrive)
             if k > 0:
 
-                @pl.when((zz < z) & (z - zz <= 2))
+                @pl.when((zz < z) & (z - zz <= 1))
                 def _():
                     diag_up(zz).wait_recv()
 
@@ -269,7 +287,7 @@
 
             if k < 3:
 
-                @pl.when((zz <= z) & (z - zz <= 1) & (z < 3))
+                @pl.when((zz == z) & (z < 3))
                 def _():
                     diag_up(zz).start()
 
@@ -279,29 +297,34 @@
 
             to_sib(xyn, zz, 9).start()
 
-        launch(0)
         own_tok = pltpu.make_async_copy(tok_ref, ptok_ref, hls.at[0])
         own_seg = pltpu.make_async_copy(seg_ref, pseg_ref, hls.at[1])
 
-        @pl.when(s < 7)
-        def _():
-            for cp in halo_copies((d, s + 1)):
-                cp.start()
 
         @pl.when(s == 0)
         def _():
             own_tok.start()
             own_seg.start()
 
+        launch(0)
         launch(1)
         second(0)
         launch(2)
+        launch(3)
+        third(0)
         second(1)
-        third(0)
-        launch(3)
+        third(1)
         second(2)
-        third(1)
+
+        @pl.when(s < 7)
+        def _():
+            for cp in halo_copies((d, s + 1)):
+                cp.start()
+
         second(3)
+        rest(1)
+        rest(2)
+        rest(3)
         third(2)
         third(3)
 
@@ -327,7 +350,7 @@
             in_plane(k, halves_sent)
             if k < 3:
 
-                @pl.when((zz <= z) & (z - zz <= 1) & (z < 3))
+                @pl.when((zz == z) & (z < 3))
                 def _():
                     diag_up(zz).wait_send()
 
@@ -777,7 +800,6 @@
 
 def project(w_rows, w_all, prev_tokens, tokens, cotangent, smalls, tables):
     rows = tokens.shape[0]
-    steps = rows // ROWB
     cos8, sin8 = tables
 
     def kernel(
@@ -815,50 +837,78 @@
             third_wait(1)
             third_wait(2)
 
-        @pl.when(i == steps)
+        @pl.when(i == 1)
         def _():
             third_wait(0)
             pltpu.make_async_copy(wo, wo, sems.at[3]).wait()
 
-        spread = spread_tables(cos_ref[...], sin_ref[...])
-
-        def keys(x):
-            normed, _ = norm_rows(x)
-            attn_in = (normed * small_ref[4:5, :] + small_ref[5:6, :]).astype(BF16)
-            k = dot(attn_in, wqkv[:, D : 2 * D])
-            v = dot(attn_in, wqkv[:, 2 * D :]) + small_ref[1:2, :]
-            k_ref[...] = rope_rows(k, *spread).astype(BF16)
-            v_ref[...] = v.astype(BF16)
-            return normed, attn_in
-
-        @pl.when(i < steps)
-        def _():
-            keys(prev_ref[...].astype(F32))
-
-        @pl.when(i >= steps)
-        def _():
-            normed, attn_in = keys(tok_ref[...].astype(F32))
-            m_ref[...] = (normed * small_ref[6:7, :] + small_ref[7:8, :]).astype(BF16)
-            q = dot(attn_in, wqkv[:, :D]) + small_ref[0:1, :]
-            q = rope_rows(q, *spread)
-            q_ref[...] = q.astype(BF16)
-            do_ref[...] = dot(g_ref[...], wo[...], NT).astype(BF16)
-
-    own = lambda i, *_: (jnp.maximum(i - steps, 0), 0)
-    prev = lambda i, *_: (jnp.minimum(i, steps - 1), 0)
-    here = lambda i, *_: (i, 0)
-    block = lambda m: pl.BlockSpec((ROWB, D), m)
-    table = pl.BlockSpec((ROT // 2, ROWB), lambda i, *_: (0, i))
+        n = rows // ROWB
+
+        def run(own):
+            x_ref = tok_ref if own else prev_ref
+            ins, tabs, raw = {}, {}, {}
+
+            def prepare(c):
+                at = slice(c * ROWB, (c + 1) * ROWB)
+                normed, _ = norm_rows(x_ref[at, :].astype(F32))
+                ins[c] = (normed * small_ref[4:5, :] + small_ref[5:6, :]).astype(BF16)
+                if own:
+                    m_ref[at, :] = (normed * small_ref[6:7, :] + small_ref[7:8, :]).astype(BF16)
+                yield
+                tabs[c] = spread_tables(cos_ref[:, at], sin_ref[:, at])
+                yield
+
+            def multiply(c):
+                at = slice(c * ROWB, (c + 1) * ROWB)
+                raw[c] = [dot(ins[c], wqkv[:, D : 2 * D])]
+                yield
+                v_ref[at, :] = (dot(ins[c], wqkv[:, 2 * D :]) + small_ref[1:2, :]).astype(BF16)
+                yield
+                if own:
+                    raw[c].append(dot(ins[c], wqkv[:, :D]) + small_ref[0:1, :])
+                    yield
+                    do_ref[at, :] = dot(g_ref[at, :], wo[...], NT).astype(BF16)
+                    yield
+
+            def turn(c):
+                at = slice(c * ROWB, (c + 1) * ROWB)
+                k_ref[at, :] = rope_rows(raw[c][0], *tabs[c]).astype(BF16)
+                yield
+                if own:
+                    q_ref[at, :] = rope_rows(raw[c][1], *tabs[c]).astype(BF16)
+                    yield
+
+            for c in range(n + 2):
+                parts = []
+                if 0 <= c - 1 < n:
+                    parts.append(multiply(c - 1))
+                if c < n:
+                    parts.append(prepare(c))
+                if 0 <= c - 2 < n:
+                    parts.append(turn(c - 2))
+                interleave(*parts)
+
+        @pl.when(i == 0)
+        def _():
+            run(False)
+
+        @pl.when(i == 1)
+        def _():
+            run(True)
+
+    block = pl.BlockSpec((rows, D), lambda i, *_: (0, 0))
+    here = pl.BlockSpec((rows, D), lambda i, *_: (i, 0))
+    table = pl.BlockSpec((ROT // 2, rows), lambda i, *_: (0, i))
     return pl.pallas_call(
         kernel,
         grid_spec=pltpu.PrefetchScalarGridSpec(
             num_scalar_prefetch=1,
-            grid=(2 * steps,),
+            grid=(2,),
             in_specs=[
-                ANY, block(prev), block(own), block(own),
+                ANY, block, block, block,
                 pl.BlockSpec((16, D), lambda i, *_: (0, 0)), table, table,
             ],
-            out_specs=[block(own), block(here), block(here), block(own), block(own)],
+            out_specs=[block, here, here, block, block],
             scratch_shapes=[
                 pltpu.VMEM((D, 3 * D), BF16),
                 pltpu.VMEM((D, D), BF16),
@@ -1251,187 +1301,147 @@
     )(w_rows, g_rows, w_all, m, cotangent, b_up)
 
 
-def finish(w_rows, w_all, tokens, cotangent, smalls, attn_out, mlp_out, dm, dq, dk, dv, halo, tables):
+def finish(
+    w_rows, g_rows, w_all, tokens, cotangent, smalls, attn_out, mlp_out, dm, dq, dk, dv, halo, tables, grads
+):
     rows = tokens.shape[0]
     steps = rows // ROWB
+    q_cols = 3 * D // FB
+    o_cols = D // FB
+    per = FB // BLK
+    last = steps + q_cols + o_cols
     cos8, sin8 = tables
 
     def kernel(
-        w_rows_ref, w_ref, tok_ref, g_ref, small_ref, o_ref, mlp_ref, dm_ref, dq_ref, dk_ref, dv_ref, halo_ref,
-        cos_ref, sin_ref,
-        out_ref, dx_ref, dp_ref, a_ref, sum_ref, wqkv, wo, sems,
+        w_rows_ref, g_rows_ref, w_ref, tok_ref, g_ref, small_ref, o_ref, mlp_ref, dm_ref, dq_ref, dk_ref, dv_ref,
+        halo_ref, cos_ref, sin_ref, _,
+        out_ref, dx_ref, sum_ref, gr_ref, wqkv, wo, at, dp, stage, sems, gsem,
     ):
         i = pl.program_id(0)
 
+        def fetch(first, count, width, dst, sem):
+            def body(t):
+                src = w_ref.at[pl.ds(pl.multiple_of(w_rows_ref[first + t], 16), BLK)]
+                r, c = t // width, t % width
+                to = dst.at[pl.ds(pl.multiple_of(r * BLK, BLK), BLK), pl.ds(pl.multiple_of(c * BLK, BLK), BLK)]
+                pltpu.make_async_copy(src, to, sem).start()
+
+            tile_loop(0, count, body)
+
         @pl.when(i == 0)
         def _():
-            def body(t):
-                src = w_ref.at[pl.ds(pl.multiple_of(w_rows_ref[OUT_BASE + t], 16), BLK)]
-                dst = wo.at[pl.ds(pl.multiple_of((t // 8) * BLK, BLK), BLK), pl.ds(pl.multiple_of((t % 8) * BLK, BLK), BLK)]
-                pltpu.make_async_copy(src, dst, sems.at[0]).start()
-
-            tile_loop(0, 64, body)
-
-            def body(t):
-                src = w_ref.at[pl.ds(pl.multiple_of(w_rows_ref[t], 16), BLK)]
-                dst = wqkv.at[pl.ds(pl.multiple_of((t // 24) * BLK, BLK), BLK), pl.ds(pl.multiple_of((t % 24) * BLK, BLK), BLK)]
-                pltpu.make_async_copy(src, dst, sems.at[1]).start()
-
-            tile_loop(0, 192, body)
+            fetch(OUT_BASE, OUT_TILES, D // BLK, wo, sems.at[0])
+            fetch(0, QKV_TILES, 3 * D // BLK, wqkv, sems.at[1])
+            sum_ref[...] = jnp.zeros_like(sum_ref)
             pltpu.make_async_copy(wo, wo, sems.at[0]).wait()
-            sum_ref[...] = jnp.zeros_like(sum_ref)
-
-        x = tok_ref[...].astype(F32)
-        grad = g_ref[...].astype(F32)
-        normed, inv = norm_rows(x)
-        g1, g2 = small_ref[4:5, :], small_ref[6:7, :]
-        a_ref[...] = (normed * g1 + small_ref[5:6, :]).astype(BF16)
-        attn = dot(o_ref[...], wo[...]) + small_ref[2:3, :]
-        out_ref[...] = (x + attn + (mlp_ref[...] + small_ref[3:4, :])).astype(BF16)
-        dk_all = dk_ref[...] + halo_ref[0].astype(F32)
-        dk_all = rope_rows(dk_all, *spread_tables(cos_ref[...], -sin_ref[...]))
-        dv_all = dv_ref[...] + halo_ref[1].astype(F32)
-        dq_low = dq_ref[...]
-        dv_low = dv_all.astype(BF16)
-        dp_ref[:, :D] = dq_low
-        dp_ref[:, D : 2 * D] = dk_all.astype(BF16)
-        dp_ref[:, 2 * D :] = dv_low
-
-        @pl.when(i == 0)
-        def _():
-            pltpu.make_async_copy(wqkv, wqkv, sems.at[1]).wait()
-
-        da = dot(dp_ref[...], wqkv[...], NT)
-        dmv = dm_ref[...]
-        dn = da * g1 + dmv * g2
-        mean_dn = jnp.mean(dn, axis=-1, keepdims=True)
-        mean_dnn = jnp.mean(dn * normed, axis=-1, keepdims=True)
-        dx_ref[...] = grad + inv * (dn - mean_dn - normed * mean_dnn)
-
-        def add(row, value):
-            sum_ref[row : row + 1, :] += jnp.sum(value, axis=0, keepdims=True)
-
-        add(0, dq_low.astype(F32))
-        add(1, dv_low.astype(F32))
-        add(2, grad)
-        add(3, da * normed)
-        add(4, da)
-        add(5, dmv * normed)
-        add(6, dmv)
-
-    here = lambda i, *_: (i, 0)
+
+        @pl.when(i < steps)
+        def _():
+            here = pl.ds(pl.multiple_of(i * ROWB, ROWB), ROWB)
+            x = tok_ref[...].astype(F32)
+            grad = g_ref[here, :].astype(F32)
+            normed, inv = norm_rows(x)
+            g1, g2 = small_ref[4:5, :], small_ref[6:7, :]
+            attn = dot(o_ref[here, :], wo[...]) + small_ref[2:3, :]
+            out_ref[...] = (x + attn + (mlp_ref[...] + small_ref[3:4, :])).astype(BF16)
+            dk_all = dk_ref[...].astype(F32) + halo_ref[0].astype(F32)
+            dk_all = rope_rows(dk_all, *spread_tables(cos_ref[...], -sin_ref[...]))
+            dv_low = (dv_ref[...].astype(F32) + halo_ref[1].astype(F32)).astype(BF16)
+            dq_low = dq_ref[...]
+            dp[here, :D] = dq_low
+            dp[here, D : 2 * D] = dk_all.astype(BF16)
+            dp[here, 2 * D :] = dv_low
+
+            @pl.when(i == 0)
+            def _():
+                pltpu.make_async_copy(wqkv, wqkv, sems.at[1]).wait()
+
+            da = dot(dp[here, :], wqkv[...], NT)
+            at[:, here] = (normed * g1 + small_ref[5:6, :]).astype(BF16).T
+            dmv = dm_ref[...]
+            dn = da * g1 + dmv * g2
+            mean_dn = jnp.mean(dn, axis=-1, keepdims=True)
+            mean_dnn = jnp.mean(dn * normed, axis=-1, keepdims=True)
+            dx_ref[...] = grad + inv * (dn - mean_dn - normed * mean_dnn)
+
+            def add(row, value):
+                sum_ref[row : row + 1, :] += jnp.sum(value, axis=0, keepdims=True)
+
+            add(0, dq_low.astype(F32))
+            add(1, dv_low.astype(F32))
+            add(2, grad)
+            add(3, da * normed)
+            add(4, da)
+            add(5, dmv * normed)
+            add(6, dmv)
+
+        slot = i % 2
+
+        def drain(sl):
+            pltpu.make_async_copy(stage.at[sl], stage.at[sl], gsem.at[sl]).wait()
+
+        def send(first, width, c):
+            for t in range(8 * per):
+                tile = first + (t // per) * width + c * per + t % per
+                dst = gr_ref.at[pl.ds(pl.multiple_of(g_rows_ref[tile], 16), BLK)]
+                r, k = t // per * BLK, t % per * BLK
+                pltpu.make_async_copy(stage.at[slot, r : r + BLK, k : k + BLK], dst, gsem.at[slot]).start()
+
+        @pl.when(i >= steps + 2)
+        def _():
+            drain(slot)
+
+        @pl.when((i >= steps) & (i < steps + q_cols))
+        def _():
+            c = i - steps
+            stage[slot] = dot(at[...], dp[:, pl.ds(pl.multiple_of(c * FB, FB), FB)]).astype(BF16)
+            send(0, 3 * D // BLK, c)
+
+        @pl.when(i >= steps + q_cols)
+        def _():
+            c = i - steps - q_cols
+            stage[slot] = dot(o_ref[...], g_ref[:, pl.ds(pl.multiple_of(c * FB, FB), FB)], TN).astype(BF16)
+            send(OUT_BASE, D // BLK, c)
+
+        @pl.when(i == last - 1)
+        def _():
+            drain(0)
+            drain(1)
+
+    here = lambda i, *_: (jnp.minimum(i, steps - 1), 0)
+    whole = lambda *shape: pl.BlockSpec(shape, lambda i, *_: (0, 0))
     block = pl.BlockSpec((ROWB, D), here)
-    table = pl.BlockSpec((ROT // 2, ROWB), lambda i, *_: (0, i + steps))
+    table = pl.BlockSpec((ROT // 2, ROWB), lambda i, *_: (0, steps + jnp.minimum(i, steps - 1)))
     return pl.pallas_call(
         kernel,
         grid_spec=pltpu.PrefetchScalarGridSpec(
-            num_scalar_prefetch=1,
-            grid=(steps,),
+            num_scalar_prefetch=2,
+            grid=(last,),
             in_specs=[
-                ANY, block, block, pl.BlockSpec((16, D), lambda i, *_: (0, 0)),
-                block, block, block, block, block, block,
-                pl.BlockSpec((2, ROWB, D), lambda i, *_: (0, i, 0)), table, table,
+                ANY, block, whole(rows, D), whole(16, D), whole(rows, D), block, block, block, block, block,
+                pl.BlockSpec((2, ROWB, D), lambda i, *_: (0, jnp.minimum(i, steps - 1), 0)), table, table, ANY,
             ],
-            out_specs=[
-                block, block, pl.BlockSpec((ROWB, 3 * D), here), block,
-                pl.BlockSpec((8, D), lambda i, *_: (0, 0)),
-            ],
+            out_specs=[block, block, whole(8, D), ANY],
             scratch_shapes=[
                 pltpu.VMEM((D, 3 * D), BF16),
                 pltpu.VMEM((D, D), BF16),
+                pltpu.VMEM((D, rows), BF16),
+                pltpu.VMEM((rows, 3 * D), BF16),
+                pltpu.VMEM((2, D, FB), BF16),
+                pltpu.SemaphoreType.DMA((2,)),
                 pltpu.SemaphoreType.DMA((2,)),
             ],
         ),
         out_shape=[
             jax.ShapeDtypeStruct((rows, D), BF16),
             jax.ShapeDtypeStruct((rows, D), F32),
-            jax.ShapeDtypeStruct((rows, 3 * D), BF16),
-            jax.ShapeDtypeStruct((rows, D), BF16),
             jax.ShapeDtypeStruct((8, D), F32),
+            jax.ShapeDtypeStruct(grads.shape, BF16),
         ],
+        input_output_aliases={15: 3},
         compiler_params=params(dimension_semantics=("arbitrary",)),
         name="finish",
-    )(w_rows, w_all, tokens, cotangent, smalls, attn_out, mlp_out, dm, dq, dk, dv, halo, cos8, sin8)
-
-
-def attention_weight_grads(g_rows, grads, attn_in, d_proj, attn_out, cotangent):
-    rows = attn_in.shape[0]
-    steps = 4 * D // FB
-
-    def kernel(g_rows_ref, a_ref, dp_ref, o_ref, g_ref, _, gr_ref, at, ot, stage, sem):
-        i = pl.program_id(0)
-        slot = i % 2
-        per = FB // BLK
-
-        @pl.when(i == 0)
-        def _():
-            at[...] = a_ref[...].T
-
-        @pl.when(i == 3 * D // FB)
-        def _():
-            ot[...] = o_ref[...].T
-
-        @pl.when(i >= 2)
-        def _():
-            pltpu.make_async_copy(stage.at[slot], stage.at[slot], sem.at[slot]).wait()
-
-        def piece(buf, t):
-            return buf.at[pl.ds(pl.multiple_of((t // per) * BLK, BLK), BLK), pl.ds(pl.multiple_of((t % per) * BLK, BLK), BLK)]
-
-        @pl.when(i < 3 * D // FB)
-        def _():
-            stage[slot] = dot(at[...], dp_ref[...]).astype(BF16)
-
-            def body(t):
-                tile = (t // per) * 24 + i * per + t % per
-                dst = gr_ref.at[pl.ds(pl.multiple_of(g_rows_ref[tile], 16), BLK)]
-                pltpu.make_async_copy(piece(stage.at[slot], t), dst, sem.at[slot]).start()
-
-            tile_loop(0, 8 * per, body)
-
-        @pl.when(i >= 3 * D // FB)
-        def _():
-            stage[slot] = dot(ot[...], g_ref[...]).astype(BF16)
-
-            def body(t):
-                tile = OUT_BASE + (t // per) * 8 + (i - 3 * D // FB) * per + t % per
-                dst = gr_ref.at[pl.ds(pl.multiple_of(g_rows_ref[tile], 16), BLK)]
-                pltpu.make_async_copy(piece(stage.at[slot], t), dst, sem.at[slot]).start()
-
-            tile_loop(0, 8 * per, body)
-
-        @pl.when(i == steps - 1)
-        def _():
-            for sl in range(2):
-                pltpu.make_async_copy(stage.at[sl], stage.at[sl], sem.at[sl]).wait()
-
-    full = pl.BlockSpec((rows, D), lambda i, *_: (0, 0))
-    last = 3 * D // FB - 1
-    return pl.pallas_call(
-        kernel,
-        grid_spec=pltpu.PrefetchScalarGridSpec(
-            num_scalar_prefetch=1,
-            grid=(steps,),
-            in_specs=[
-                full,
-                pl.BlockSpec((rows, FB), lambda i, *_: (0, jnp.minimum(i, last))),
-                full,
-                pl.BlockSpec((rows, FB), lambda i, *_: (0, jnp.maximum(i - last - 1, 0))),
-                ANY,
-            ],
-            out_specs=ANY,
-            scratch_shapes=[
-                pltpu.VMEM((D, rows), BF16),
-                pltpu.VMEM((D, rows), BF16),
-                pltpu.VMEM((2, D, FB), BF16),
-                pltpu.SemaphoreType.DMA((2,)),
-            ],
-        ),
-        out_shape=jax.ShapeDtypeStruct(grads.shape, BF16),
-        input_output_aliases={5: 0},
-        compiler_params=params(dimension_semantics=("arbitrary",)),
-        name="attention_weight_grads",
-    )(g_rows, attn_in, d_proj, attn_out, cotangent, grads)
+    )(w_rows, g_rows, w_all, tokens, cotangent, smalls, attn_out, mlp_out, dm, dq, dk, dv, halo, cos8, sin8, grads)
 
 
 def halves(x):
@@ -1580,10 +1590,9 @@
     )
     halo = passed_along(halo, "seq", -1)
     mlp_out, dm, db_up, grads = feed_forward(w_rows, g_rows, w_all, m, cotangent, b_up)
-    block_output, input_grad, d_proj, attn_in, sums = finish(
-        w_rows, w_all, tokens, cotangent, smalls, attn_out, mlp_out, dm, dq, dk, dv, halo, tables
+    block_output, input_grad, sums, grads = finish(
+        w_rows, g_rows, w_all, tokens, cotangent, smalls, attn_out, mlp_out, dm, dq, dk, dv, halo, tables, grads
     )
-    grads = attention_weight_grads(g_rows, grads, attn_in, d_proj, attn_out, cotangent)
 
     small_terms = jnp.concatenate(
         [

time: 509 us -> 480 us (0.943)
  Pallas kernels: 468 us -> 438 us
    pallas_call x1 -> x0, Pallas kernels: 19.5 us -> none  [attention_weight_grads(): pl.pallas_call(kernel, grid_spec=pltpu.PrefetchScalarGridSpec(num_scalar_...]
    pallas_call x1, Pallas kernels: 125 us -> 106 us  [sum_gradients(): pl.pallas_call(kernel, out_shape=[jax.ShapeDtypeStruct((OWNED, BLK), F32)...]
    pallas_call x1, Pallas kernels: 26.3 us -> 39.1 us  [finish(): pl.pallas_call(kernel, grid_spec=pltpu.PrefetchScalarGridSpec(num_scalar_...]
  transfers between devices with their start and end apart: 1 -> 1, of which waited for: 0 -> 0; matrix products, arithmetic and copies ran while one was open for 2% -> 2% of each run, Pallas kernels for 15% -> 16%
where the time goes in v4:
time: 480 us; the launch traced here: 476 us
  Pallas kernels  438 us (91%)
  other arithmetic  15.4 us (3%)
  local copies, waits for them, and re-layouts  13.7 us (3%)
  starting transfers between devices  6.61 us (1%)
    pallas_call x1, Pallas kernels, sum_gradients(): pl.pallas_call(kernel, out_shape=[jax.ShapeDtypeStruct((OWNED, BLK), F32)...  106 us
    pallas_call x1, Pallas kernels, gather_weights(): pl.pallas_call(kernel, out_shape=[jax.ShapeDtypeStruct((32, rows, BLK), B...  99.7 us
    pallas_call x1, Pallas kernels, attend(): pl.pallas_call(kernel, grid=(pairs,), in_specs=[block, keys, keys, block,...  83.6 us
    pallas_call x1, Pallas kernels, feed_forward(): pl.pallas_call(kernel, grid_spec=pltpu.PrefetchScalarGridSpec(num_scalar_...  74.2 us
    pallas_call x1, Pallas kernels, finish(): pl.pallas_call(kernel, grid_spec=pltpu.PrefetchScalarGridSpec(num_scalar_...  39.1 us
    pallas_call x1, Pallas kernels, project(): pl.pallas_call(kernel, grid_spec=pltpu.PrefetchScalarGridSpec(num_scalar_...  26.8 us
  transfers between devices with their start and end apart: 1, of which 0 were waited for; matrix products, arithmetic and copies ran while one was open for 2% of the time, Pallas kernels for 16%

profile of v4, /device:TPU:16, one launch (start us, length us, event | category | flops | bytes accessed | tf_op | source)
XLA Modules:
  0.0 475.9 jit_solution(10240279670006822518)
XLA Ops:
  1.4 1.0 select_reduce_fusion
  4.5 1.5 convert_element_type.23
  6.1 0.9 pad_maximum_fusion.x_ref
  7.6 99.7 %gather_weights.1 = (bf16[32,3088,128]{2,1,0:T(8,128)(2,1)}, bf16[1024,1024]{1,0:T(8,128)(2,1)}, s32[8,1024]{1,0:T(8,128)}) custom-call(bf16[3088,128]{1,0:T(8,128)(2,1)} %pad_maximum_fusion.x_ref, bf16[1024,1024]{1,0:T(8,128)(2,1)} %tok_ref.5, s32[8,1024]{1,0:T(8,128)} %broadcast_in_dim.56.seg_ref), custom_call_target="tpu_custom_call" | custom-call | tf_op jit(solution)/shard_map/gather_weights/pallas_call | solution.py:384
  107.3 0.8 broadcast_select_fusion
  108.1 0.8 slice_convert_fusion
  109.5 2.1 slice_reduce_fusion
  111.7 1.3 copy.31.sk_ref
  113.0 1.3 concatenate.20.small_ref
  114.3 26.8 %project.1 = (bf16[1024,1024]{1,0:T(8,128)(2,1)}, bf16[2048,1024]{1,0:T(8,128)(2,1)}, bf16[2048,1024]{1,0:T(8,128)(2,1)}, bf16[1024,1024]{1,0:T(8,128)(2,1)}, bf16[1024,1024]{1,0:T(8,128)(2,1)}) custom-call(s32[768]{0:T(1024)} %get-tuple-element.111.w_rows_ref, bf16[98816,128]{1,0:T(8,128)(2,1)} %bitcast.29, bf16[1024,1024]{1,0:T(8,128)(2,1)} %get-tuple-element.66.prev_ref, ...), custom_call_target="tpu_custom_call" | custom-call | tf_op jit(solution)/shard_map/project/pallas_call | solution.py:902
  141.1 83.6 %attend.1 = (bf16[1024,1024]{1,0:T(8,128)(2,1)}, bf16[1024,1024]{1,0:T(8,128)(2,1)}, f32[1024,1024]{1,0:T(8,128)}, f32[1024,1024]{1,0:T(8,128)}, bf16[2,1024,1024]{2,1,0:T(8,128)(2,1)}, /*index=5*/f32[64,512]{1,0:T(8,128)}) custom-call(bf16[1024,1024]{1,0:T(8,128)(2,1)} %get-tuple-element.67.q_ref, bf16[2048,1024]{1,0:T(8,128)(2,1)} %get-tuple-element.68.k_ref, ...), custom_call_target="tpu_custom_call" | custom-call | flops 42949672960 | bytes 33554432 | tf_op jit(solution)/shard_map/attend/pallas_call | solution.py:1100
  224.7 6.6 %collective-permute-start = (bf16[2,1024,1024]{2,1,0:T(8,128)(2,1)}, bf16[2,1024,1024]{2,1,0:T(8,128)(2,1)}, u32[]{:S(2)}, u32[]{:S(2)}) collective-permute-start(bf16[2,1024,1024]{2,1,0:T(8,128)(2,1)} %get-tuple-element.79), channel_id=1, source_target_pairs={{1,0},{2,1},{3,2},{4,3},{5,4},{6,5},{7,6},{9,8},{10,9},{11,10},{12... | collective-permute-start | bytes 12582920 | tf_op jit(solution)/shard_map/ppermute | solution.py:1513
  232.8 0.9 reshape.234.b_ref
  233.8 1.0 slice_reduce_fusion.8
  235.5 74.2 %feed_forward.1 = (f32[1024,1024]{1,0:T(8,128)}, f32[1024,1024]{1,0:T(8,128)}, f32[1,4096]{1,0:T(1,128)}, bf16[98304,128]{1,0:T(8,128)(2,1)}) custom-call(s32[768]{0:T(1024)} %get-tuple-element.111.w_rows_ref, s32[768]{0:T(1024)} %get-tuple-element.110.g_rows_ref, bf16[98816,128]{1,0:T(8,128)(2,1)} %bitcast.30, bf16[1024,1024]{1,0:T(8,128)(2,1)} %get-tuple-element.73.m_ref, ...), custom_call_target="tpu_custom_call" | custom-call | flops 55834574848 | bytes 50331648 | tf_op jit(solution)/shard_map/feed_forward/pallas_call | solution.py:1271
  310.3 1.4 reduce.30
  312.4 0.8 fusion.11
  314.1 39.1 %finish.1 = (bf16[1024,1024]{1,0:T(8,128)(2,1)}, f32[1024,1024]{1,0:T(8,128)}, f32[8,1024]{1,0:T(8,128)}, bf16[98304,128]{1,0:T(8,128)(2,1)}) custom-call(s32[768]{0:T(1024)} %get-tuple-element.111.w_rows_ref, s32[768]{0:T(1024)} %get-tuple-element.110.g_rows_ref, bf16[98816,128]{1,0:T(8,128)(2,1)} %bitcast.31, ...), custom_call_target="tpu_custom_call", output_to_operand_aliasing={{3}: (15, {})} | custom-call | tf_op jit(solution)/shard_map/finish/pallas_call | solution.py:1415
  353.2 0.8 slice_bitcast_fusion.2
  355.9 106.1 %sum_gradients.1 = (f32[3072,128]{1,0:T(8,128)}, f32[104,128]{1,0:T(8,128)}) custom-call(bf16[98304,128]{1,0:T(8,128)(2,1)} %get-tuple-element.83.g_ref, f32[104,128]{1,0:T(8,128)} %pad_maximum_fusion.2.e_ref), custom_call_target="tpu_custom_call" | custom-call | tf_op jit(solution)/shard_map/sum_gradients/pallas_call | solution.py:746
  462.0 0.8 slice_bitcast_fusion
  462.8 1.2 fusion.14
  465.5 9.0 %update_tiles.1 = (f32[24,128,128]{2,1,0:T(8,128)}, bf16[24,128,128]{2,1,0:T(8,128)(2,1)}, f32[24,128,128]{2,1,0:T(8,128)}, f32[24,128,128]{2,1,0:T(8,128)}) custom-call(f32[24,128,128]{2,1,0:T(8,128)} %bitcast.32, f32[24,128,128]{2,1,0:T(8,128)} %w_ref.1, f32[24,128,128]{2,1,0:T(8,128)} %l_ref.1, f32[24,128,128]{2,1,0:T(8,128)} %r_ref.1, ...), custom_call_target="tpu_custom_call" | custom-call | tf_op jit(solution)/shard_map/update_tiles/pallas_call | solution.py:1480
  474.6 1.1 copy.37
  (46 shorter events, 11.3 us)
Async XLA Ops:
  3.0 4.0 copy-start.3
  3.3 104.0 %copy-start.1 = (f32[8,2048]{1,0:T(8,128)}, f32[8,2048]{1,0:T(8,128)S(1)}, u32[]{:S(2)}) copy-start(f32[8,2048]{1,0:T(8,128)S(1)} %get-tuple-element.108.sin_ref) | copy-start | bytes 196612
  3.3 104.0 %copy-start.2 = (f32[8,2048]{1,0:T(8,128)}, f32[8,2048]{1,0:T(8,128)S(1)}, u32[]{:S(2)}) copy-start(f32[8,2048]{1,0:T(8,128)S(1)} %get-tuple-element.109.cos_ref) | copy-start | bytes 196612
  224.7 89.3 %collective-permute-start = (bf16[2,1024,1024]{2,1,0:T(8,128)(2,1)}, bf16[2,1024,1024]{2,1,0:T(8,128)(2,1)}, u32[]{:S(2)}, u32[]{:S(2)}) collective-permute-start(bf16[2,1024,1024]{2,1,0:T(8,128)(2,1)} %get-tuple-element.79), channel_id=1, source_target_pairs={{1,0},{2,1},{3,2},{4,3},{5,4},{6,5},{7,6},{9,8},{10,9},{11,10},{12... | collective-permute-start | bytes 12582920 | tf_op jit(solution)/shard_map/ppermute | solution.py:1513
  355.9 108.9 %copy-start.4 = (f32[384]{0:T(512)S(1)}, f32[384]{0:T(512)}, u32[]{:S(2)}) copy-start(f32[384]{0:T(512)} %param.26) | copy-start | bytes 4612
  355.9 108.9 %copy-start.5 = (f32[384]{0:T(512)S(1)}, f32[384]{0:T(512)}, u32[]{:S(2)}) copy-start(f32[384]{0:T(512)} %param.27) | copy-start | bytes 4612
  355.9 108.9 %copy-start.6 = (f32[384]{0:T(512)S(1)}, f32[384]{0:T(512)}, u32[]{:S(2)}) copy-start(f32[384]{0:T(512)} %param.28) | copy-start | bytes 4612
  465.5 9.0 %copy-start = (f32[3072,128]{1,0:T(8,128)S(1)}, f32[3072,128]{1,0:T(8,128)}, u32[]{:S(2)}) copy-start(f32[3072,128]{1,0:T(8,128)} %get-tuple-element.87) | copy-start | bytes 4718596

commit v5 on v4

--- a/solution.py
+++ b/solution.py
@@ -779,14 +779,19 @@
 ROWB = 256
 
 
-def rope_rows(value, cos_t, fwd_t, back_t):
-    pieces = []
-    for j in range(value.shape[1] // BLK):
-        p = value[:, j * BLK : (j + 1) * BLK]
-        pieces.append(
-            p * cos_t + pltpu.roll(p, BLK - ROT // 2, 1) * fwd_t + pltpu.roll(p, ROT // 2, 1) * back_t
-        )
-    return jnp.concatenate(pieces, axis=1)
+PAIRS = HEADS // 2
+
+
+def rope(p, cos_t, fwd_t, back_t):
+    return p * cos_t + pltpu.roll(p, BLK - ROT // 2, 1) * fwd_t + pltpu.roll(p, ROT // 2, 1) * back_t
+
+
+def by_pair(value):
+    return [value[:, j * BLK : (j + 1) * BLK] for j in range(PAIRS)]
+
+
+def side_by_side(ref, at=slice(None)):
+    return jnp.concatenate([ref[j, at, :] for j in range(PAIRS)], axis=1)
 
 
 def spread_tables(cos8, sin8):
@@ -843,6 +848,10 @@
             pltpu.make_async_copy(wo, wo, sems.at[3]).wait()
 
         n = rows // ROWB
+
+        def put(ref, at, pieces):
+            for j in range(PAIRS):
+                ref[j, at, :] = pieces[j].astype(BF16)
 
         def run(own):
             x_ref = tok_ref if own else prev_ref
@@ -862,20 +871,20 @@
                 at = slice(c * ROWB, (c + 1) * ROWB)
                 raw[c] = [dot(ins[c], wqkv[:, D : 2 * D])]
                 yield
-                v_ref[at, :] = (dot(ins[c], wqkv[:, 2 * D :]) + small_ref[1:2, :]).astype(BF16)
+                put(v_ref, at, by_pair(dot(ins[c], wqkv[:, 2 * D :]) + small_ref[1:2, :]))
                 yield
                 if own:
                     raw[c].append(dot(ins[c], wqkv[:, :D]) + small_ref[0:1, :])
                     yield
-                    do_ref[at, :] = dot(g_ref[at, :], wo[...], NT).astype(BF16)
+                    put(do_ref, at, by_pair(dot(g_ref[at, :], wo[...], NT)))
                     yield
 
             def turn(c):
                 at = slice(c * ROWB, (c + 1) * ROWB)
-                k_ref[at, :] = rope_rows(raw[c][0], *tabs[c]).astype(BF16)
+                put(k_ref, at, [rope(p, *tabs[c]) for p in by_pair(raw[c][0])])
                 yield
                 if own:
-                    q_ref[at, :] = rope_rows(raw[c][1], *tabs[c]).astype(BF16)
+                    put(q_ref, at, [rope(p, *tabs[c]) for p in by_pair(raw[c][1])])
                     yield
 
             for c in range(n + 2):
@@ -897,7 +906,8 @@
             run(True)
 
     block = pl.BlockSpec((rows, D), lambda i, *_: (0, 0))
-    here = pl.BlockSpec((rows, D), lambda i, *_: (i, 0))
+    here = pl.BlockSpec((PAIRS, rows, BLK), lambda i, *_: (0, i, 0))
+    own = pl.BlockSpec((PAIRS, rows, BLK), lambda i, *_: (0, 0, 0))
     table = pl.BlockSpec((ROT // 2, rows), lambda i, *_: (0, i))
     return pl.pallas_call(
         kernel,
@@ -908,7 +918,7 @@
                 ANY, block, block, block,
                 pl.BlockSpec((16, D), lambda i, *_: (0, 0)), table, table,
             ],
-            out_specs=[block, here, here, block, block],
+            out_specs=[own, here, here, own, block],
             scratch_shapes=[
                 pltpu.VMEM((D, 3 * D), BF16),
                 pltpu.VMEM((D, D), BF16),
@@ -916,10 +926,10 @@
             ],
         ),
         out_shape=[
-            jax.ShapeDtypeStruct((rows, D), BF16),
-            jax.ShapeDtypeStruct((2 * rows, D), BF16),
-            jax.ShapeDtypeStruct((2 * rows, D), BF16),
-            jax.ShapeDtypeStruct((rows, D), BF16),
+            jax.ShapeDtypeStruct((PAIRS, rows, BLK), BF16),
+            jax.ShapeDtypeStruct((PAIRS, 2 * rows, BLK), BF16),
+            jax.ShapeDtypeStruct((PAIRS, 2 * rows, BLK), BF16),
+            jax.ShapeDtypeStruct((PAIRS, rows, BLK), BF16),
             jax.ShapeDtypeStruct((rows, D), BF16),
         ],
         compiler_params=params(dimension_semantics=("arbitrary",)),
@@ -936,9 +946,8 @@
 
 
 def attend(q, k, v, d_out, seg_q, seg_k, cos8, sin8):
-    rows = q.shape[0]
+    rows = q.shape[1]
     blocks = rows // QB
-    pairs = HEADS // 2
     scale = HEAD ** (-0.5)
     half = ROT // 2
     n = SPAN // CHUNK
@@ -961,7 +970,7 @@
 
     def kernel(
         q_ref, k_ref, v_ref, do_ref, sq_ref, sk_ref, cos_ref, sin_ref,
-        o_ref, dq_ref, dk_ref, dv_ref, halo_ref, peak_ref, bias, kt, vt, el_ref, ds_ref, dks, dvs,
+        o_ref, dq_ref, dk_ref, dv_ref, halo_ref, peak_ref, bias, kt, vt, el_ref, ds_ref, dks, dvs, base,
     ):
         p = pl.program_id(0)
 
@@ -993,17 +1002,19 @@
         def scores(i, c, q_apart):
             return dot(keys_at(k_ref, i, c), q_apart) + two(bias[i, c * CHUNK : (c + 1) * CHUNK])
 
-        def forward(i, q_apart, shifted, found):
-            base = None
-            if shifted:
-                for c in range(n):
-                    t = fold(scores(i, c, q_apart), jnp.max)
-                    base = t if c == 0 else jnp.maximum(base, t)
-                base = jnp.max(base, axis=0, keepdims=True)
+        def row_tops(i):
+            q_apart = prepare(i)[1]
+            for c in range(n):
+                t = fold(scores(i, c, q_apart), jnp.max)
+                most = t if c == 0 else jnp.maximum(most, t)
+            base[i] = jnp.max(most, axis=0, keepdims=True)
+
+        def forward(i, q_apart, found):
+            low = base[i]
             top8 = sum8 = None
             for c in range(n):
                 st = scores(i, c, q_apart)
-                e = jnp.exp(st - base if shifted else st)
+                e = jnp.exp(st - low)
                 el_ref[i % 2, c * CHUNK : (c + 1) * CHUNK] = e.astype(BF16)
                 t, u = fold(st, jnp.max), fold(e, jnp.sum)
                 top8, sum8 = (t, u) if c == 0 else (jnp.maximum(top8, t), sum8 + u)
@@ -1064,7 +1075,7 @@
             dq_ref[i * QB : (i + 1) * QB, :] = jnp.concatenate(turned, axis=0).T.astype(BF16)
             yield
 
-        def run(shifted):
+        def run():
             top = held = None
             for i in range(blocks + 1):
                 parts, found = [], []
@@ -1072,7 +1083,7 @@
                     parts.append(input_grads(i - 1, *held))
                 if i < blocks:
                     q_all, q_apart = prepare(i)
-                    parts.append(forward(i, q_apart, shifted, found))
+                    parts.append(forward(i, q_apart, found))
                 interleave(*parts)
                 if i < blocks:
                     t, inv = found
@@ -1086,35 +1097,36 @@
             dk_ref[...] = dks[rows:, :]
             dv_ref[...] = dvs[rows:, :]
 
-        @pl.when(safe)
-        def _():
-            run(False)
+        base[...] = jnp.zeros_like(base)
 
         @pl.when(jnp.logical_not(safe))
         def _():
-            run(True)
-
-    block = pl.BlockSpec((rows, BLK), lambda p: (0, p))
-    keys = pl.BlockSpec((2 * rows, BLK), lambda p: (0, p))
+            for i in range(blocks):
+                row_tops(i)
+
+        run()
+
+    block = pl.BlockSpec((None, rows, BLK), lambda p: (p, 0, 0))
+    keys = pl.BlockSpec((None, 2 * rows, BLK), lambda p: (p, 0, 0))
     whole = lambda *shape: pl.BlockSpec(shape, lambda p: (0, 0))
     return pl.pallas_call(
         kernel,
-        grid=(pairs,),
+        grid=(PAIRS,),
         in_specs=[
             block, keys, keys, block, whole(1, rows), whole(2 * rows, 1), whole(half, rows), whole(half, rows),
         ],
         out_specs=[
             block, block, block, block,
-            pl.BlockSpec((2, rows, BLK), lambda p: (0, 0, p)),
+            pl.BlockSpec((2, None, rows, BLK), lambda p: (0, p, 0, 0)),
             pl.BlockSpec((8, 2 * QB), lambda p: (p, 0)),
         ],
         out_shape=[
-            jax.ShapeDtypeStruct((rows, D), BF16),
-            jax.ShapeDtypeStruct((rows, D), BF16),
-            jax.ShapeDtypeStruct((rows, D), F32),
-            jax.ShapeDtypeStruct((rows, D), F32),
-            jax.ShapeDtypeStruct((2, rows, D), BF16),
-            jax.ShapeDtypeStruct((8 * pairs, 2 * QB), F32),
+            jax.ShapeDtypeStruct((PAIRS, rows, BLK), BF16),
+            jax.ShapeDtypeStruct((PAIRS, rows, BLK), BF16),
+            jax.ShapeDtypeStruct((PAIRS, rows, BLK), F32),
+            jax.ShapeDtypeStruct((PAIRS, rows, BLK), F32),
+            jax.ShapeDtypeStruct((2, PAIRS, rows, BLK), BF16),
+            jax.ShapeDtypeStruct((8 * PAIRS, 2 * QB), F32),
         ],
         scratch_shapes=[
             pltpu.VMEM((blocks, SPAN, QB), F32),
@@ -1124,6 +1136,7 @@
             pltpu.VMEM((2, SPAN, 2 * QB), BF16),
             pltpu.VMEM((2 * rows, BLK), F32),
             pltpu.VMEM((2 * rows, BLK), F32),
+            pltpu.VMEM((blocks, 1, 2 * QB), F32),
         ],
         compiler_params=params(dimension_semantics=("arbitrary",)),
         cost_estimate=pl.CostEstimate(flops=40 << 30, bytes_accessed=32 << 20, transcendentals=20 << 20),
@@ -1342,15 +1355,16 @@
             grad = g_ref[here, :].astype(F32)
             normed, inv = norm_rows(x)
             g1, g2 = small_ref[4:5, :], small_ref[6:7, :]
-            attn = dot(o_ref[here, :], wo[...]) + small_ref[2:3, :]
+            attn = dot(side_by_side(o_ref, here), wo[...]) + small_ref[2:3, :]
             out_ref[...] = (x + attn + (mlp_ref[...] + small_ref[3:4, :])).astype(BF16)
-            dk_all = dk_ref[...].astype(F32) + halo_ref[0].astype(F32)
-            dk_all = rope_rows(dk_all, *spread_tables(cos_ref[...], -sin_ref[...]))
-            dv_low = (dv_ref[...].astype(F32) + halo_ref[1].astype(F32)).astype(BF16)
-            dq_low = dq_ref[...]
-            dp[here, :D] = dq_low
-            dp[here, D : 2 * D] = dk_all.astype(BF16)
-            dp[here, 2 * D :] = dv_low
+            back = spread_tables(cos_ref[...], -sin_ref[...])
+            for j in range(PAIRS):
+                cols = j * BLK
+                dk_all = dk_ref[j].astype(F32) + halo_ref[0, j].astype(F32)
+                dv_all = dv_ref[j].astype(F32) + halo_ref[1, j].astype(F32)
+                dp[here, cols : cols + BLK] = dq_ref[j]
+                dp[here, D + cols : D + cols + BLK] = rope(dk_all, *back).astype(BF16)
+                dp[here, 2 * D + cols : 2 * D + cols + BLK] = dv_all.astype(BF16)
 
             @pl.when(i == 0)
             def _():
@@ -1367,8 +1381,8 @@
             def add(row, value):
                 sum_ref[row : row + 1, :] += jnp.sum(value, axis=0, keepdims=True)
 
-            add(0, dq_low.astype(F32))
-            add(1, dv_low.astype(F32))
+            add(0, dp[here, :D].astype(F32))
+            add(1, dp[here, 2 * D :].astype(F32))
             add(2, grad)
             add(3, da * normed)
             add(4, da)
@@ -1400,7 +1414,7 @@
         @pl.when(i >= steps + q_cols)
         def _():
             c = i - steps - q_cols
-            stage[slot] = dot(o_ref[...], g_ref[:, pl.ds(pl.multiple_of(c * FB, FB), FB)], TN).astype(BF16)
+            stage[slot] = dot(side_by_side(o_ref), g_ref[:, pl.ds(pl.multiple_of(c * FB, FB), FB)], TN).astype(BF16)
             send(OUT_BASE, D // BLK, c)
 
         @pl.when(i == last - 1)
@@ -1411,6 +1425,7 @@
     here = lambda i, *_: (jnp.minimum(i, steps - 1), 0)
     whole = lambda *shape: pl.BlockSpec(shape, lambda i, *_: (0, 0))
     block = pl.BlockSpec((ROWB, D), here)
+    pairs = pl.BlockSpec((PAIRS, ROWB, BLK), lambda i, *_: (0, jnp.minimum(i, steps - 1), 0))
     table = pl.BlockSpec((ROT // 2, ROWB), lambda i, *_: (0, steps + jnp.minimum(i, steps - 1)))
     return pl.pallas_call(
         kernel,
@@ -1418,8 +1433,10 @@
             num_scalar_prefetch=2,
             grid=(last,),
             in_specs=[
-                ANY, block, whole(rows, D), whole(16, D), whole(rows, D), block, block, block, block, block,
-                pl.BlockSpec((2, ROWB, D), lambda i, *_: (0, jnp.minimum(i, steps - 1), 0)), table, table, ANY,
+                ANY, block, whole(rows, D), whole(16, D), pl.BlockSpec((PAIRS, rows, BLK), lambda i, *_: (0, 0, 0)),
+                block, block, pairs, pairs, pairs,
+                pl.BlockSpec((2, PAIRS, ROWB, BLK), lambda i, *_: (0, 0, jnp.minimum(i, steps - 1), 0)),
+                table, table, ANY,
             ],
             out_specs=[block, block, whole(8, D), ANY],
             scratch_shapes=[
@@ -1602,7 +1619,7 @@
         ],
         axis=1,
     ).reshape(SMALL)
-    head_peak = jnp.max(peaks.reshape(HEADS // 2, 8, 2, QB)[:, 0], axis=-1).reshape(HEADS)
+    head_peak = jnp.max(peaks.reshape(PAIRS, 8, 2, QB)[:, 0], axis=-1).reshape(HEADS)
     if ring:
         peak_rows = jnp.zeros((8, BLK), F32).at[:, :HEADS].set(head_peak[None, :])
         extra = jnp.concatenate([small_terms.reshape(SMALL_ROWS, BLK), peak_rows], axis=0)

time: 480 us -> 472 us (0.983)
  Pallas kernels: 438 us -> 430 us
    pallas_call x1, Pallas kernels: 83.6 us -> 74.8 us  [attend(): pl.pallas_call(kernel, grid=(PAIRS,), in_specs=[block, keys, keys, block,...]
where the time goes in v5:
time: 472 us; the launch traced here: 468 us
  Pallas kernels  430 us (91%)
  other arithmetic  15.6 us (3%)
  local copies, waits for them, and re-layouts  13.7 us (3%)
  starting transfers between devices  6.62 us (1%)
    pallas_call x1, Pallas kernels, sum_gradients(): pl.pallas_call(kernel, out_shape=[jax.ShapeDtypeStruct((OWNED, BLK), F32)...  106 us
    pallas_call x1, Pallas kernels, gather_weights(): pl.pallas_call(kernel, out_shape=[jax.ShapeDtypeStruct((32, rows, BLK), B...  99.7 us
    pallas_call x1, Pallas kernels, attend(): pl.pallas_call(kernel, grid=(PAIRS,), in_specs=[block, keys, keys, block,...  74.8 us
    pallas_call x1, Pallas kernels, feed_forward(): pl.pallas_call(kernel, grid_spec=pltpu.PrefetchScalarGridSpec(num_scalar_...  74.2 us
    pallas_call x1, Pallas kernels, finish(): pl.pallas_call(kernel, grid_spec=pltpu.PrefetchScalarGridSpec(num_scalar_...  39.1 us
    pallas_call x1, Pallas kernels, project(): pl.pallas_call(kernel, grid_spec=pltpu.PrefetchScalarGridSpec(num_scalar_...  27 us
  transfers between devices with their start and end apart: 1, of which 0 were waited for; matrix products, arithmetic and copies ran while one was open for 2% of the time, Pallas kernels for 16%

profile of v5, /device:TPU:16, one launch (start us, length us, event | category | flops | bytes accessed | tf_op | source)
XLA Modules:
  0.0 467.7 jit_solution(16172852664572258978)
XLA Ops:
  1.4 1.0 select_reduce_fusion
  4.5 1.5 convert_element_type.23
  6.1 0.9 pad_maximum_fusion.x_ref
  7.6 99.7 %gather_weights.1 = (bf16[32,3088,128]{2,1,0:T(8,128)(2,1)}, bf16[1024,1024]{1,0:T(8,128)(2,1)}, s32[8,1024]{1,0:T(8,128)}) custom-call(bf16[3088,128]{1,0:T(8,128)(2,1)} %pad_maximum_fusion.x_ref, bf16[1024,1024]{1,0:T(8,128)(2,1)} %tok_ref.5, s32[8,1024]{1,0:T(8,128)} %broadcast_in_dim.56.seg_ref), custom_call_target="tpu_custom_call" | custom-call | tf_op jit(solution)/shard_map/gather_weights/pallas_call | solution.py:384
  107.3 0.8 broadcast_select_fusion
  108.1 0.8 slice_convert_fusion
  109.5 2.1 slice_reduce_fusion
  111.7 1.3 copy.31.sk_ref
  113.0 1.3 concatenate.20.small_ref
  114.3 27.0 %project.1 = (bf16[8,1024,128]{2,1,0:T(8,128)(2,1)}, bf16[8,2048,128]{2,1,0:T(8,128)(2,1)}, bf16[8,2048,128]{2,1,0:T(8,128)(2,1)}, bf16[8,1024,128]{2,1,0:T(8,128)(2,1)}, bf16[1024,1024]{1,0:T(8,128)(2,1)}) custom-call(s32[768]{0:T(1024)} %get-tuple-element.111.w_rows_ref, bf16[98816,128]{1,0:T(8,128)(2,1)} %bitcast.29, ...), custom_call_target="tpu_custom_call" | custom-call | tf_op jit(solution)/shard_map/project/pallas_call | solution.py:912
  141.3 74.8 %attend.1 = (bf16[8,1024,128]{2,1,0:T(8,128)(2,1)}, bf16[8,1024,128]{2,1,0:T(8,128)(2,1)}, f32[8,1024,128]{2,1,0:T(8,128)}, f32[8,1024,128]{2,1,0:T(8,128)}, bf1...) custom-call(bf16[8,1024,128]{2,1,0:T(8,128)(2,1)} %get-tuple-element.67.q_ref, ...), custom_call_target="tpu_custom_call" | custom-call | flops 42949672960 | bytes 33554432 | tf_op jit(solution)/shard_map/attend/pallas_call | solution.py:1112
  216.1 6.6 %collective-permute-start = (bf16[2,8,1024,128]{3,2,1,0:T(8,128)(2,1)}, bf16[2,8,1024,128]{3,2,1,0:T(8,128)(2,1)}, u32[]{:S(2)}, u32[]{:S(2)}) collective-permute-start(bf16[2,8,1024,128]{3,2,1,0:T(8,128)(2,1)} %get-tuple-element.79), channel_id=1, source_target_pairs={{1,0},{2,1},{3,2},{4,3},{5,4},{6,5},{7,6},{9,8},{10,9},{11,10},{12... | collective-permute-start | bytes 12582920 | tf_op jit(solution)/shard_map/ppermute | solution.py:1530
  222.7 0.9 compare_reduce_fusion
  224.4 0.9 reshape.234.b_ref
  225.4 1.0 slice_reduce_fusion.8
  227.1 74.2 %feed_forward.1 = (f32[1024,1024]{1,0:T(8,128)}, f32[1024,1024]{1,0:T(8,128)}, f32[1,4096]{1,0:T(1,128)}, bf16[98304,128]{1,0:T(8,128)(2,1)}) custom-call(s32[768]{0:T(1024)} %get-tuple-element.111.w_rows_ref, s32[768]{0:T(1024)} %get-tuple-element.110.g_rows_ref, bf16[98816,128]{1,0:T(8,128)(2,1)} %bitcast.30, bf16[1024,1024]{1,0:T(8,128)(2,1)} %get-tuple-element.73.m_ref, ...), custom_call_target="tpu_custom_call" | custom-call | flops 55834574848 | bytes 50331648 | tf_op jit(solution)/shard_map/feed_forward/pallas_call | solution.py:1284
  301.9 1.4 reduce.30
  304.0 0.8 fusion.11
  305.7 39.1 %finish.1 = (bf16[1024,1024]{1,0:T(8,128)(2,1)}, f32[1024,1024]{1,0:T(8,128)}, f32[8,1024]{1,0:T(8,128)}, bf16[98304,128]{1,0:T(8,128)(2,1)}) custom-call(s32[768]{0:T(1024)} %get-tuple-element.111.w_rows_ref, s32[768]{0:T(1024)} %get-tuple-element.110.g_rows_ref, bf16[98816,128]{1,0:T(8,128)(2,1)} %bitcast.31, ...), custom_call_target="tpu_custom_call", output_to_operand_aliasing={{3}: (15, {})} | custom-call | tf_op jit(solution)/shard_map/finish/pallas_call | solution.py:1430
  347.5 106.0 %sum_gradients.1 = (f32[3072,128]{1,0:T(8,128)}, f32[104,128]{1,0:T(8,128)}) custom-call(bf16[98304,128]{1,0:T(8,128)(2,1)} %get-tuple-element.83.g_ref, f32[104,128]{1,0:T(8,128)} %pad_maximum_fusion.2.e_ref), custom_call_target="tpu_custom_call" | custom-call | tf_op jit(solution)/shard_map/sum_gradients/pallas_call | solution.py:746
  453.6 0.8 slice_bitcast_fusion
  454.4 1.2 fusion.14
  457.1 9.0 %update_tiles.1 = (f32[24,128,128]{2,1,0:T(8,128)}, bf16[24,128,128]{2,1,0:T(8,128)(2,1)}, f32[24,128,128]{2,1,0:T(8,128)}, f32[24,128,128]{2,1,0:T(8,128)}) custom-call(f32[24,128,128]{2,1,0:T(8,128)} %bitcast.32, f32[24,128,128]{2,1,0:T(8,128)} %w_ref.1, f32[24,128,128]{2,1,0:T(8,128)} %l_ref.1, f32[24,128,128]{2,1,0:T(8,128)} %r_ref.1, ...), custom_call_target="tpu_custom_call" | custom-call | tf_op jit(solution)/shard_map/update_tiles/pallas_call | solution.py:1497
  466.1 1.1 copy.37
  (46 shorter events, 11.4 us)
Async XLA Ops:
  3.0 4.0 copy-start.3
  3.3 104.0 %copy-start.1 = (f32[8,2048]{1,0:T(8,128)}, f32[8,2048]{1,0:T(8,128)S(1)}, u32[]{:S(2)}) copy-start(f32[8,2048]{1,0:T(8,128)S(1)} %get-tuple-element.108.sin_ref) | copy-start | bytes 196612
  3.3 104.0 %copy-start.2 = (f32[8,2048]{1,0:T(8,128)}, f32[8,2048]{1,0:T(8,128)S(1)}, u32[]{:S(2)}) copy-start(f32[8,2048]{1,0:T(8,128)S(1)} %get-tuple-element.109.cos_ref) | copy-start | bytes 196612
  216.1 89.6 %collective-permute-start = (bf16[2,8,1024,128]{3,2,1,0:T(8,128)(2,1)}, bf16[2,8,1024,128]{3,2,1,0:T(8,128)(2,1)}, u32[]{:S(2)}, u32[]{:S(2)}) collective-permute-start(bf16[2,8,1024,128]{3,2,1,0:T(8,128)(2,1)} %get-tuple-element.79), channel_id=1, source_target_pairs={{1,0},{2,1},{3,2},{4,3},{5,4},{6,5},{7,6},{9,8},{10,9},{11,10},{12... | collective-permute-start | bytes 12582920 | tf_op jit(solution)/shard_map/ppermute | solution.py:1530
  347.5 108.9 %copy-start.4 = (f32[384]{0:T(512)S(1)}, f32[384]{0:T(512)}, u32[]{:S(2)}) copy-start(f32[384]{0:T(512)} %param.26) | copy-start | bytes 4612
  347.5 108.9 %copy-start.5 = (f32[384]{0:T(512)S(1)}, f32[384]{0:T(512)}, u32[]{:S(2)}) copy-start(f32[384]{0:T(512)} %param.27) | copy-start | bytes 4612
  347.5 108.9 %copy-start.6 = (f32[384]{0:T(512)S(1)}, f32[384]{0:T(512)}, u32[]{:S(2)}) copy-start(f32[384]{0:T(512)} %param.28) | copy-start | bytes 4612
  457.1 9.0 %copy-start = (f32[3072,128]{1,0:T(8,128)S(1)}, f32[3072,128]{1,0:T(8,128)}, u32[]{:S(2)}) copy-start(f32[3072,128]{1,0:T(8,128)} %get-tuple-element.87) | copy-start | bytes 4718596

commit v6 on v5

--- a/solution.py
+++ b/solution.py
@@ -22,6 +22,9 @@
 OUT_BASE = QKV_TILES
 UP_BASE = QKV_TILES + OUT_TILES
 DOWN_BASE = UP_BASE + UP_TILES
+
+B_Q, B_V, B_O = slice(0, 1), slice(1, 2), slice(2, 3)
+B_DOWN, G1, C1, G2, C2 = slice(7, 8), slice(8, 9), slice(9, 10), slice(10, 11), slice(11, 12)
 
 NORM_EPS = 1e-05
 ADAM_EPS = 1e-08
@@ -409,7 +412,7 @@
 EXTRA_ROWS = SMALL_ROWS + 8
 
 
-def add_rows(dst, terms, rows, step=512):
+def add_rows(dst, terms, rows, step=256):
     def body(i, carry):
         at = pl.ds(pl.multiple_of(i * step, step), step)
         if len(terms) == 2 and dst.dtype == BF16:
@@ -424,8 +427,16 @@
     lax.fori_loop(0, rows // step, body, 0)
 
 
+SCHEDULE = [
+    "F0a", "F1a", "F0b", "F1b", "E0", "F2a", "S0a", "S0b", "D1a", "F2b",
+    "S1a", "S1b", "F3a", "E1", "F3b", "D1b", "D2a", "D2b", "S2a", "D3a",
+    "S2b", "T0a", "T0b", "E2", "D3b", "T1a", "T1b", "E3", "T2a", "T2b",
+    "E4", "S3a", "S3b", "T3a", "T3b",
+]
+
+
 def sum_gradients(grads, extra):
-    def kernel(g_ref, e_ref, out_ref, eout_ref, own, crecv, s1a, s1b, s2, zup, zdn, gup, gdn, epart, erecv, ls, ss, rs, zss, zrs, es, er):
+    def kernel(g_ref, e_ref, out_ref, eout_ref, own, crecv, s1a, s1b, s2, zup, zdn, gup, gdn, epart, erecv, ls, ss, rs, es, er):
         d = lax.axis_index("dp")
         s = lax.axis_index("seq")
         z = s // 2
@@ -436,9 +447,6 @@
         sib = z * 2 + 1 - c
         zpair = s + 2 - 4 * (z % 2)
         zfar = s + 4 - 8 * (z // 2)
-        top = pl.ds(0, HALF)
-        low = pl.ds(HALF, HALF)
-
         barrier = pltpu.get_barrier_semaphore()
 
         def greet(dev):
@@ -459,116 +467,225 @@
 
         order = [3 * (1 - z // 2), (2 + 3 * z) % 5, 1 + z % 2, z]
 
-        def owner_rows(dd, zz, cc):
-            return g_ref.at[pl.ds(pl.multiple_of((dd * 8 + zz * 2 + cc) * OWNED, OWNED), OWNED)]
-
-        def load(zz, dd):
-            return pltpu.make_async_copy(owner_rows(dd, zz, c), own.at[zz, dd], ls.at[zz, dd])
-
-        for k in range(4):
-            for dd in range(4):
-                load(order[k], dd).start()
-
-        pl.semaphore_wait(barrier, 4 + (z + 2) // 3 + (5 - z) // 3)
+        ends = (z == 0) | (z == 3)
+        inner = (z == 1) | (z == 2)
+
+        def in_plane(k, act):
+            if k == 3:
+                act()
+            elif k == 0:
+                pl.when(ends)(act)
 
         def remote(src, dst, ssem, rsem, dev):
             return pltpu.make_async_remote_copy(
                 src_ref=src, dst_ref=dst, send_sem=ssem, recv_sem=rsem, device_id=dev, device_id_type=MESH
             )
 
-        def core(zz, dd):
-            return remote(owner_rows(dd, zz, 1 - c), crecv.at[zz, dd], ss.at[zz, dd], rs.at[zz, dd], (d, sib))
-
-        def y_own(zz):
-            return remote(own.at[zz, yn, top], s1a.at[zz, 0], ss.at[zz, 4], rs.at[zz, 4], (yn, s))
-
-        def y_cross(zz):
-            return remote(own.at[zz, xyn, top], s1a.at[zz, 1], ss.at[zz, 5], rs.at[zz, 5], (yn, s))
-
-        def x_own(zz):
-            return remote(own.at[zz, xn, low], s1b.at[zz, 0], ss.at[zz, 6], rs.at[zz, 6], (xn, s))
-
-        def x_cross(zz):
-            return remote(own.at[zz, xyn, low], s1b.at[zz, 1], ss.at[zz, 7], rs.at[zz, 7], (xn, s))
-
-        def x_last(zz):
-            return remote(own.at[zz, xn, top], s2.at[zz, top], ss.at[zz, 8], rs.at[zz, 8], (xn, s))
-
-        def y_last(zz):
-            return remote(own.at[zz, yn, low], s2.at[zz, low], ss.at[zz, 9], rs.at[zz, 9], (yn, s))
-
-        def z_up(zz):
-            return remote(own.at[zz, d], zup.at[zz], zss.at[0, zz], zrs.at[0, zz], (d, s + 2))
-
-        def z_dn(zz):
-            return remote(own.at[zz, d], zdn.at[zz], zss.at[1, zz], zrs.at[1, zz], (d, s - 2))
-
-        def g_up(zz):
-            return remote(own.at[zz, xyn], gup.at[zz], zss.at[2, zz], zrs.at[2, zz], (d, s + 2))
-
-        def g_dn(zz):
-            return remote(own.at[zz, xyn], gdn.at[zz], zss.at[3, zz], zrs.at[3, zz], (d, s - 2))
-
-        ends = (z == 0) | (z == 3)
-        inner = (z == 1) | (z == 2)
-
-        def in_plane(k, body):
-            if k == 3:
-                body()
-            elif k == 0:
-                pl.when(ends)(body)
-
-        def cross(zz):
-            y_cross(zz).start()
-            x_cross(zz).start()
-
-        def along(zz, act):
-            @pl.when(zz > z)
-            def _():
-                act(g_up(zz))
-
-            @pl.when(zz < z)
-            def _():
-                act(g_dn(zz))
-
-        def outward(k, act):
-            zz = order[k]
-            if k == 0:
-                pl.when(inner)(lambda: along(zz, act))
-            elif k < 3:
-                along(zz, act)
-
-        def diagonal(k):
-            zz = order[k]
-            mine = own.at[zz, xyn]
-            if k < 3:
-
-                @pl.when(inner)
+        def part(h):
+            size = OWNED // 2
+            half = size // 2
+            rows = pl.ds(h * size, size)
+            top = pl.ds(h * size, half)
+            low = pl.ds(h * size + half, half)
+            here = pl.ds(h * half, half)
+
+            def owner_rows(dd, zz, cc):
+                return g_ref.at[pl.ds(pl.multiple_of((dd * 8 + zz * 2 + cc) * OWNED + h * size, size), size)]
+
+            def load(k, dd):
+                zz = order[k]
+                return pltpu.make_async_copy(owner_rows(dd, zz, c), own.at[zz, dd, rows], ls.at[zz * 2 + h, dd])
+
+            def hop(src, dst, kind, zz, dev):
+                return remote(src, dst, ss.at[zz * 2 + h, kind], rs.at[zz * 2 + h, kind], dev)
+
+            def core(zz, dd):
+                return hop(owner_rows(dd, zz, 1 - c), crecv.at[zz, dd, rows], dd, zz, (d, sib))
+
+            def y_own(zz):
+                return hop(own.at[zz, yn, top], s1a.at[zz, 0, here], 4, zz, (yn, s))
+
+            def y_cross(zz):
+                return hop(own.at[zz, xyn, top], s1a.at[zz, 1, here], 5, zz, (yn, s))
+
+            def x_own(zz):
+                return hop(own.at[zz, xn, low], s1b.at[zz, 0, here], 6, zz, (xn, s))
+
+            def x_cross(zz):
+                return hop(own.at[zz, xyn, low], s1b.at[zz, 1, here], 7, zz, (xn, s))
+
+            def x_last(zz):
+                return hop(own.at[zz, xn, top], s2.at[zz, top], 8, zz, (xn, s))
+
+            def y_last(zz):
+                return hop(own.at[zz, yn, low], s2.at[zz, low], 9, zz, (yn, s))
+
+            def z_up(zz):
+                return hop(own.at[zz, d, rows], zup.at[zz, rows], 10, zz, (d, s + 2))
+
+            def z_dn(zz):
+                return hop(own.at[zz, d, rows], zdn.at[zz, rows], 11, zz, (d, s - 2))
+
+            def g_up(zz):
+                return hop(own.at[zz, xyn, rows], gup.at[zz, rows], 12, zz, (d, s + 2))
+
+            def g_dn(zz):
+                return hop(own.at[zz, xyn, rows], gdn.at[zz, rows], 13, zz, (d, s - 2))
+
+            def cross(zz):
+                y_cross(zz).start()
+                x_cross(zz).start()
+
+            def along(zz, act):
+                @pl.when(zz > z)
                 def _():
-                    @pl.when(zz > z)
+                    act(g_up(zz))
+
+                @pl.when(zz < z)
+                def _():
+                    act(g_dn(zz))
+
+            def outward(k, act):
+                if k == 0:
+                    pl.when(inner)(lambda: along(order[k], act))
+                elif k < 3:
+                    along(order[k], act)
+
+            def issue(k):
+                for dd in (xyn, yn, xn, d):
+                    core(order[k], dd).start()
+
+            def first(k):
+                zz = order[k]
+
+                def one(dd, start):
+                    load(k, dd).wait()
+                    core(zz, dd).wait_recv()
+                    mine = own.at[zz, dd, rows]
+                    add_rows(mine, [mine, crecv.at[zz, dd, rows]], size)
+                    for cp in start:
+                        cp.start()
+
+                one(xyn, [])
+                if k == 0:
+                    pl.when(ends)(lambda: cross(zz))
+                    outward(0, lambda cp: cp.start())
+                elif k < 3:
+                    pl.when(ends)(lambda: along(zz, lambda cp: cp.start()))
+                one(yn, [y_own(zz)])
+                one(xn, [x_own(zz)])
+                one(d, [])
+
+            def diagonal(k):
+                zz = order[k]
+                mine = own.at[zz, xyn, rows]
+
+                def take(cp, came):
+                    cp.wait_recv()
+                    add_rows(mine, [mine, came.at[zz, rows]], size)
+
+                if k < 3:
+
+                    @pl.when(inner)
                     def _():
-                        g_up(zz).wait_recv()
-                        add_rows(mine, [mine, gup.at[zz]], OWNED)
-
-                    @pl.when(zz < z)
+                        pl.when(zz > z)(lambda: take(g_up(zz), gup))
+                        pl.when(zz < z)(lambda: take(g_dn(zz), gdn))
+                        along(zz, lambda cp: cp.start())
+                else:
+                    pl.when(z > 0)(lambda: take(g_up(zz), gup))
+                    pl.when(z < 3)(lambda: take(g_dn(zz), gdn))
+                    cross(zz)
+
+            def second(k):
+                zz = order[k]
+                a = own.at[zz, xn, top]
+                b = own.at[zz, yn, low]
+
+                def crossed():
+                    y_cross(zz).wait_recv()
+                    add_rows(a, [a, s1a.at[zz, 1, here]], half)
+
+                def crossed_low():
+                    x_cross(zz).wait_recv()
+                    add_rows(b, [b, s1b.at[zz, 1, here]], half)
+
+                in_plane(k, crossed)
+                x_last(zz).start()
+                in_plane(k, crossed_low)
+                y_last(zz).start()
+
+            def third(k):
+                zz = order[k]
+                for cp in (y_own(zz), x_own(zz), x_last(zz), y_last(zz)):
+                    cp.wait_recv()
+
+                def total(to_top, to_low, *came):
+                    add_rows(
+                        to_top, [own.at[zz, d, top], s1a.at[zz, 0, here], s2.at[zz, top]] + [x.at[zz, top] for x in came], half
+                    )
+                    add_rows(
+                        to_low, [own.at[zz, d, low], s1b.at[zz, 0, here], s2.at[zz, low]] + [x.at[zz, low] for x in came], half
+                    )
+
+                if k < 3:
+                    mine = (own.at[zz, d, top], own.at[zz, d, low])
+
+                    @pl.when((zz > z) & (z > 0))
                     def _():
-                        g_dn(zz).wait_recv()
-                        add_rows(mine, [mine, gdn.at[zz]], OWNED)
-
-                    along(zz, lambda cp: cp.start())
-            else:
-
-                @pl.when(z > 0)
-                def _():
-                    g_up(zz).wait_recv()
-                    add_rows(mine, [mine, gup.at[zz]], OWNED)
-
-                @pl.when(z < 3)
-                def _():
-                    g_dn(zz).wait_recv()
-                    add_rows(mine, [mine, gdn.at[zz]], OWNED)
-
-                cross(zz)
+                        z_up(zz).wait_recv()
+                        total(*mine, zup)
+
+                    @pl.when((zz < z) & (z < 3))
+                    def _():
+                        z_dn(zz).wait_recv()
+                        total(*mine, zdn)
+
+                    @pl.when(((zz > z) & (z == 0)) | ((zz < z) & (z == 3)))
+                    def _():
+                        total(*mine)
+
+                    pl.when(zz > z)(lambda: z_up(zz).start())
+                    pl.when(zz < z)(lambda: z_dn(zz).start())
+                else:
+                    result = (out_ref.at[top], out_ref.at[low])
+                    pl.when(z > 0)(lambda: z_up(zz).wait_recv())
+                    pl.when(z < 3)(lambda: z_dn(zz).wait_recv())
+                    pl.when(inner)(lambda: total(*result, zup, zdn))
+                    pl.when(z == 0)(lambda: total(*result, zdn))
+                    pl.when(z == 3)(lambda: total(*result, zup))
+
+            def sent(k):
+                zz = order[k]
+                for dd in range(4):
+                    core(zz, dd).wait_send()
+                for cp in (y_own(zz), x_own(zz), x_last(zz), y_last(zz)):
+                    cp.wait_send()
+
+                def crosses_sent():
+                    y_cross(zz).wait_send()
+                    x_cross(zz).wait_send()
+
+                in_plane(k, crosses_sent)
+                outward(k, lambda cp: cp.wait_send())
+                if k < 3:
+                    pl.when(zz > z)(lambda: z_up(zz).wait_send())
+                    pl.when(zz < z)(lambda: z_dn(zz).wait_send())
+
+            return dict(load=load, issue=issue, F=first, D=diagonal, S=second, T=third, sent=sent)
+
+        parts = {"a": part(0), "b": part(1)}
+        schedule = list(SCHEDULE)
+        firsts = [step for step in schedule if step[0] == "F"]
+        for step in firsts:
+            for dd in (xyn, yn, xn, d):
+                parts[step[2]]["load"](int(step[1]), dd).start()
+
+        pl.semaphore_wait(barrier, 4 + (z + 2) // 3 + (5 - z) // 3)
+
+        def issue_next():
+            if firsts:
+                step = firsts.pop(0)
+                parts[step[2]]["issue"](int(step[1]))
 
         def extra_step(i, dev):
             return remote(epart.at[i], erecv.at[i], es.at[i], er.at[i], dev)
@@ -587,161 +704,22 @@
             else:
                 eout_ref[...] = total
 
-        def issue(k):
-            for dd in (xyn, yn, xn, d):
-                core(order[k], dd).start()
-
-        issue(0)
+        issue_next()
         epart[0] = e_ref[...]
         extra_step(0, extra_devs[0]).start()
-
-        def first(k):
-            zz = order[k]
-            if k < 3:
-                issue(k + 1)
-
-            def one(dd, start):
-                load(zz, dd).wait()
-                core(zz, dd).wait_recv()
-                add_rows(own.at[zz, dd], [own.at[zz, dd], crecv.at[zz, dd]], OWNED)
-                for cp in start:
-                    cp.start()
-
-            one(xyn, [])
-            if k == 0:
-                pl.when(ends)(lambda: cross(zz))
-                outward(0, lambda cp: cp.start())
-            elif k < 3:
-                pl.when(ends)(lambda: along(zz, lambda cp: cp.start()))
-            one(yn, [y_own(zz)])
-            one(xn, [x_own(zz)])
-            one(d, [])
-
-        def second(k):
-            zz = order[k]
-            a = own.at[zz, xn, top]
-            b = own.at[zz, yn, low]
-
-            def crossed():
-                y_cross(zz).wait_recv()
-                add_rows(a, [a, s1a.at[zz, 1]], HALF)
-
-            def crossed_low():
-                x_cross(zz).wait_recv()
-                add_rows(b, [b, s1b.at[zz, 1]], HALF)
-
-            in_plane(k, crossed)
-            x_last(zz).start()
-            in_plane(k, crossed_low)
-            y_last(zz).start()
-
-        def third(k):
-            zz = order[k]
-            y_own(zz).wait_recv()
-            x_own(zz).wait_recv()
-            x_last(zz).wait_recv()
-            y_last(zz).wait_recv()
-            a = own.at[zz, d, top]
-            b = own.at[zz, d, low]
-            if k < 3:
-
-                @pl.when((zz > z) & (z > 0))
-                def _():
-                    z_up(zz).wait_recv()
-                    add_rows(a, [a, s1a.at[zz, 0], s2.at[zz, top], zup.at[zz, top]], HALF)
-                    add_rows(b, [b, s1b.at[zz, 0], s2.at[zz, low], zup.at[zz, low]], HALF)
-
-                @pl.when((zz < z) & (z < 3))
-                def _():
-                    z_dn(zz).wait_recv()
-                    add_rows(a, [a, s1a.at[zz, 0], s2.at[zz, top], zdn.at[zz, top]], HALF)
-                    add_rows(b, [b, s1b.at[zz, 0], s2.at[zz, low], zdn.at[zz, low]], HALF)
-
-                @pl.when(((zz > z) & (z == 0)) | ((zz < z) & (z == 3)))
-                def _():
-                    add_rows(a, [a, s1a.at[zz, 0], s2.at[zz, top]], HALF)
-                    add_rows(b, [b, s1b.at[zz, 0], s2.at[zz, low]], HALF)
-
-                @pl.when(zz > z)
-                def _():
-                    z_up(zz).start()
-
-                @pl.when(zz < z)
-                def _():
-                    z_dn(zz).start()
+        for step in schedule:
+            if step[0] == "E":
+                extra_add(int(step[1]))
             else:
-
-                @pl.when(z > 0)
-                def _():
-                    z_up(zz).wait_recv()
-
-                @pl.when(z < 3)
-                def _():
-                    z_dn(zz).wait_recv()
-
-                o_top = out_ref.at[top]
-                o_low = out_ref.at[low]
-
-                @pl.when((z > 0) & (z < 3))
-                def _():
-                    add_rows(o_top, [a, s1a.at[zz, 0], s2.at[zz, top], zup.at[zz, top], zdn.at[zz, top]], HALF)
-                    add_rows(o_low, [b, s1b.at[zz, 0], s2.at[zz, low], zup.at[zz, low], zdn.at[zz, low]], HALF)
-
-                @pl.when(z == 0)
-                def _():
-                    add_rows(o_top, [a, s1a.at[zz, 0], s2.at[zz, top], zdn.at[zz, top]], HALF)
-                    add_rows(o_low, [b, s1b.at[zz, 0], s2.at[zz, low], zdn.at[zz, low]], HALF)
-
-                @pl.when(z == 3)
-                def _():
-                    add_rows(o_top, [a, s1a.at[zz, 0], s2.at[zz, top], zup.at[zz, top]], HALF)
-                    add_rows(o_low, [b, s1b.at[zz, 0], s2.at[zz, low], zup.at[zz, low]], HALF)
-
-        first(0)
-        first(1)
-        extra_add(0)
-        second(0)
-        diagonal(1)
-        first(2)
-        second(1)
-        extra_add(1)
-        first(3)
-        diagonal(2)
-        second(2)
-        third(0)
-        extra_add(2)
-        diagonal(3)
-        extra_add(3)
-        third(1)
-        extra_add(4)
-        third(2)
-        second(3)
-        third(3)
+                if step[0] == "F":
+                    issue_next()
+                parts[step[2]][step[0]](int(step[1]))
 
         for i in range(5):
             extra_step(i, extra_devs[i]).wait_send()
         for k in range(4):
-            zz = order[k]
-            for dd in range(4):
-                core(zz, dd).wait_send()
-            for cp in (y_own(zz), x_own(zz), x_last(zz), y_last(zz)):
-                cp.wait_send()
-
-            def crosses_sent():
-                y_cross(zz).wait_send()
-                x_cross(zz).wait_send()
-
-            in_plane(k, crosses_sent)
-            outward(k, lambda cp: cp.wait_send())
-            if k < 3:
-
-                @pl.when(zz > z)
-                def _():
-                    z_up(zz).wait_send()
-
-                @pl.when(zz < z)
-                def _():
-                    z_dn(zz).wait_send()
+            for h in "ab":
+                parts[h]["sent"](k)
 
     return pl.pallas_call(
         kernel,
@@ -763,11 +741,9 @@
             pltpu.VMEM((4, OWNED, BLK), BF16),
             pltpu.VMEM((5, EXTRA_ROWS, BLK), F32),
             pltpu.VMEM((5, EXTRA_ROWS, BLK), F32),
-            pltpu.SemaphoreType.DMA((4, 4)),
-            pltpu.SemaphoreType.DMA((4, 10)),
-            pltpu.SemaphoreType.DMA((4, 10)),
-            pltpu.SemaphoreType.DMA((4, 4)),
-            pltpu.SemaphoreType.DMA((4, 4)),
+            pltpu.SemaphoreType.DMA((8, 4)),
+            pltpu.SemaphoreType.DMA((8, 14)),
+            pltpu.SemaphoreType.DMA((8, 14)),
             pltpu.SemaphoreType.DMA((5,)),
             pltpu.SemaphoreType.DMA((5,)),
         ],
@@ -803,9 +779,13 @@
     return [jnp.concatenate(t * 2, axis=0).T for t in (cos_t, fwd_t, back_t)]
 
 
+PROWS = 512
+
+
 def project(w_rows, w_all, prev_tokens, tokens, cotangent, smalls, tables):
     rows = tokens.shape[0]
     cos8, sin8 = tables
+    steps = rows // PROWS
 
     def kernel(
         w_rows_ref, w_ref, prev_ref, tok_ref, g_ref, small_ref, cos_ref, sin_ref,
@@ -842,12 +822,12 @@
             third_wait(1)
             third_wait(2)
 
-        @pl.when(i == 1)
+        @pl.when(i == steps)
         def _():
             third_wait(0)
             pltpu.make_async_copy(wo, wo, sems.at[3]).wait()
 
-        n = rows // ROWB
+        n = PROWS // ROWB
 
         def put(ref, at, pieces):
             for j in range(PAIRS):
@@ -860,9 +840,9 @@
             def prepare(c):
                 at = slice(c * ROWB, (c + 1) * ROWB)
                 normed, _ = norm_rows(x_ref[at, :].astype(F32))
-                ins[c] = (normed * small_ref[4:5, :] + small_ref[5:6, :]).astype(BF16)
+                ins[c] = (normed * small_ref[G1, :] + small_ref[C1, :]).astype(BF16)
                 if own:
-                    m_ref[at, :] = (normed * small_ref[6:7, :] + small_ref[7:8, :]).astype(BF16)
+                    m_ref[at, :] = (normed * small_ref[G2, :] + small_ref[C2, :]).astype(BF16)
                 yield
                 tabs[c] = spread_tables(cos_ref[:, at], sin_ref[:, at])
                 yield
@@ -871,10 +851,10 @@
                 at = slice(c * ROWB, (c + 1) * ROWB)
                 raw[c] = [dot(ins[c], wqkv[:, D : 2 * D])]
                 yield
-                put(v_ref, at, by_pair(dot(ins[c], wqkv[:, 2 * D :]) + small_ref[1:2, :]))
+                put(v_ref, at, by_pair(dot(ins[c], wqkv[:, 2 * D :]) + small_ref[B_V, :]))
                 yield
                 if own:
-                    raw[c].append(dot(ins[c], wqkv[:, :D]) + small_ref[0:1, :])
+                    raw[c].append(dot(ins[c], wqkv[:, :D]) + small_ref[B_Q, :])
                     yield
                     put(do_ref, at, by_pair(dot(g_ref[at, :], wo[...], NT)))
                     yield
@@ -897,25 +877,26 @@
                     parts.append(turn(c - 2))
                 interleave(*parts)
 
-        @pl.when(i == 0)
+        @pl.when(i < steps)
         def _():
             run(False)
 
-        @pl.when(i == 1)
+        @pl.when(i >= steps)
         def _():
             run(True)
 
-    block = pl.BlockSpec((rows, D), lambda i, *_: (0, 0))
-    here = pl.BlockSpec((PAIRS, rows, BLK), lambda i, *_: (0, i, 0))
-    own = pl.BlockSpec((PAIRS, rows, BLK), lambda i, *_: (0, 0, 0))
-    table = pl.BlockSpec((ROT // 2, rows), lambda i, *_: (0, i))
+    before = pl.BlockSpec((PROWS, D), lambda i, *_: (jnp.minimum(i, steps - 1), 0))
+    block = pl.BlockSpec((PROWS, D), lambda i, *_: (jnp.maximum(i - steps, 0), 0))
+    here = pl.BlockSpec((PAIRS, PROWS, BLK), lambda i, *_: (0, i, 0))
+    own = pl.BlockSpec((PAIRS, PROWS, BLK), lambda i, *_: (0, jnp.maximum(i - steps, 0), 0))
+    table = pl.BlockSpec((ROT // 2, PROWS), lambda i, *_: (0, i))
     return pl.pallas_call(
         kernel,
         grid_spec=pltpu.PrefetchScalarGridSpec(
             num_scalar_prefetch=1,
-            grid=(2,),
+            grid=(2 * steps,),
             in_specs=[
-                ANY, block, block, block,
+                ANY, before, block, block,
                 pl.BlockSpec((16, D), lambda i, *_: (0, 0)), table, table,
             ],
             out_specs=[own, here, here, own, block],
@@ -945,7 +926,7 @@
 SAFE_SCORE = 60.0
 
 
-def attend(q, k, v, d_out, seg_q, seg_k, cos8, sin8):
+def attend(q, k, v, d_out, prev_seg, seg, cos8, sin8):
     rows = q.shape[1]
     blocks = rows // QB
     scale = HEAD ** (-0.5)
@@ -969,8 +950,8 @@
         return jnp.concatenate([x, x], axis=1)
 
     def kernel(
-        q_ref, k_ref, v_ref, do_ref, sq_ref, sk_ref, cos_ref, sin_ref,
-        o_ref, dq_ref, dk_ref, dv_ref, halo_ref, peak_ref, bias, kt, vt, el_ref, ds_ref, dks, dvs, base,
+        q_ref, k_ref, v_ref, do_ref, pseg_ref, seg_ref, cos_ref, sin_ref,
+        o_ref, dq_ref, dk_ref, dv_ref, halo_ref, peak_ref, bias, kt, vt, el_ref, ds_ref, dks, dvs, base, key_seg,
     ):
         p = pl.program_id(0)
 
@@ -981,8 +962,13 @@
                 + lax.broadcasted_iota(jnp.int32, (SPAN, QB), 1)
                 - lax.broadcasted_iota(jnp.int32, (SPAN, QB), 0)
             )
+            before = jnp.where(lax.axis_index("seq") == 0, -1, pseg_ref[...]).astype(F32)
+            for part, numbers in enumerate((before, seg_ref[...].astype(F32))):
+                column = jnp.broadcast_to(numbers[:1, :], (BLK, rows)).T
+                key_seg[part * rows : (part + 1) * rows, :] = column
             for i in range(blocks):
-                same = sk_ref[i * QB : i * QB + SPAN, :] == sq_ref[:, i * QB : (i + 1) * QB]
+                query_seg = seg_ref[:1, i * QB : (i + 1) * QB].astype(F32)
+                same = key_seg[i * QB : i * QB + SPAN, :1] == query_seg
                 bias[i] = jnp.where((gap >= 0) & (gap < WINDOW) & same, 0.0, MASKED)
 
         kt[...] = k_ref[...].T
@@ -1094,8 +1080,8 @@
             peak_ref[...] = jnp.broadcast_to(top, peak_ref.shape)
             halo_ref[0] = dks[:rows, :].astype(BF16)
             halo_ref[1] = dvs[:rows, :].astype(BF16)
-            dk_ref[...] = dks[rows:, :]
-            dv_ref[...] = dvs[rows:, :]
+            dk_ref[...] = dks[rows:, :].astype(BF16)
+            dv_ref[...] = dvs[rows:, :].astype(BF16)
 
         base[...] = jnp.zeros_like(base)
 
@@ -1109,11 +1095,12 @@
     block = pl.BlockSpec((None, rows, BLK), lambda p: (p, 0, 0))
     keys = pl.BlockSpec((None, 2 * rows, BLK), lambda p: (p, 0, 0))
     whole = lambda *shape: pl.BlockSpec(shape, lambda p: (0, 0))
+    own_rot = pl.BlockSpec((half, rows), lambda p: (0, 1))
     return pl.pallas_call(
         kernel,
         grid=(PAIRS,),
         in_specs=[
-            block, keys, keys, block, whole(1, rows), whole(2 * rows, 1), whole(half, rows), whole(half, rows),
+            block, keys, keys, block, whole(8, rows), whole(8, rows), own_rot, own_rot,
         ],
         out_specs=[
             block, block, block, block,
@@ -1123,8 +1110,8 @@
         out_shape=[
             jax.ShapeDtypeStruct((PAIRS, rows, BLK), BF16),
             jax.ShapeDtypeStruct((PAIRS, rows, BLK), BF16),
-            jax.ShapeDtypeStruct((PAIRS, rows, BLK), F32),
-            jax.ShapeDtypeStruct((PAIRS, rows, BLK), F32),
+            jax.ShapeDtypeStruct((PAIRS, rows, BLK), BF16),
+            jax.ShapeDtypeStruct((PAIRS, rows, BLK), BF16),
             jax.ShapeDtypeStruct((2, PAIRS, rows, BLK), BF16),
             jax.ShapeDtypeStruct((8 * PAIRS, 2 * QB), F32),
         ],
@@ -1137,11 +1124,12 @@
             pltpu.VMEM((2 * rows, BLK), F32),
             pltpu.VMEM((2 * rows, BLK), F32),
             pltpu.VMEM((blocks, 1, 2 * QB), F32),
+            pltpu.VMEM((2 * rows, BLK), F32),
         ],
         compiler_params=params(dimension_semantics=("arbitrary",)),
         cost_estimate=pl.CostEstimate(flops=40 << 30, bytes_accessed=32 << 20, transcendentals=20 << 20),
         name="attend",
-    )(q, k, v, d_out, seg_q, seg_k, cos8, sin8)
+    )(q, k, v, d_out, prev_seg, seg, cos8, sin8)
 
 
 FB = 512
@@ -1165,8 +1153,8 @@
     steps = FF // FB
 
     def kernel(
-        w_rows_ref, g_rows_ref, w_ref, m_ref, g_ref, b_ref, out_ref, dm_ref, db_ref, gr_ref,
-        mt, wup, wdn, hs, dus, gup, gdn, u_ref, h_ref, wsem, gsem,
+        w_rows_ref, g_rows_ref, w_ref, m_ref, g_ref, b_ref, low_ref, dml_ref, db_ref, gr_ref,
+        mt, wup, wdn, hs, dus, gup, gdn, u_ref, h_ref, out_ref, dm_ref, wsem, gsem,
     ):
         f = pl.program_id(0)
         slot = f % 2
@@ -1273,6 +1261,8 @@
 
         @pl.when(f == steps - 1)
         def _():
+            low_ref[...] = out_ref[...].astype(BF16)
+            dml_ref[...] = dm_ref[...].astype(BF16)
             whole_wait(wup.at[1 - slot], wsem.at[0, 1 - slot])
             whole_wait(wdn.at[1 - slot], wsem.at[1, 1 - slot])
             for sl in range(2):
@@ -1298,13 +1288,15 @@
                 pltpu.VMEM((2, FB, D), BF16),
                 pltpu.VMEM((2, ROWB, FB), F32),
                 pltpu.VMEM((2, ROWB, FB), F32),
+                pltpu.VMEM((rows, D), F32),
+                pltpu.VMEM((rows, D), F32),
                 pltpu.SemaphoreType.DMA((2, 2)),
                 pltpu.SemaphoreType.DMA((2, 2)),
             ],
         ),
         out_shape=[
-            jax.ShapeDtypeStruct((rows, D), F32),
-            jax.ShapeDtypeStruct((rows, D), F32),
+            jax.ShapeDtypeStruct((rows, D), BF16),
+            jax.ShapeDtypeStruct((rows, D), BF16),
             jax.ShapeDtypeStruct((1, FF), F32),
             jax.ShapeDtypeStruct((TILES * BLK, BLK), BF16),
         ],
@@ -1354,9 +1346,9 @@
             x = tok_ref[...].astype(F32)
             grad = g_ref[here, :].astype(F32)
             normed, inv = norm_rows(x)
-            g1, g2 = small_ref[4:5, :], small_ref[6:7, :]
-            attn = dot(side_by_side(o_ref, here), wo[...]) + small_ref[2:3, :]
-            out_ref[...] = (x + attn + (mlp_ref[...] + small_ref[3:4, :])).astype(BF16)
+            g1, g2 = small_ref[G1, :], small_ref[G2, :]
+            attn = dot(side_by_side(o_ref, here), wo[...]) + small_ref[B_O, :]
+            out_ref[...] = (x + attn + (mlp_ref[...].astype(F32) + small_ref[B_DOWN, :])).astype(BF16)
             back = spread_tables(cos_ref[...], -sin_ref[...])
             for j in range(PAIRS):
                 cols = j * BLK
@@ -1371,8 +1363,8 @@
                 pltpu.make_async_copy(wqkv, wqkv, sems.at[1]).wait()
 
             da = dot(dp[here, :], wqkv[...], NT)
-            at[:, here] = (normed * g1 + small_ref[5:6, :]).astype(BF16).T
-            dmv = dm_ref[...]
+            at[:, here] = (normed * g1 + small_ref[C1, :]).astype(BF16).T
+            dmv = dm_ref[...].astype(F32)
             dn = da * g1 + dmv * g2
             mean_dn = jnp.mean(dn, axis=-1, keepdims=True)
             mean_dnn = jnp.mean(dn * normed, axis=-1, keepdims=True)
@@ -1553,7 +1545,7 @@
     seq_index = lax.axis_index("seq")
     owner_index = lax.axis_index(axes)
     first_place = seq_index * rows
-    seg_local = segments.reshape(1, rows)
+    seg_rows = jnp.broadcast_to(segments.reshape(1, rows), (8, rows))
 
     numbers = jnp.arange(TILES, dtype=jnp.int32)
     slot_of_tile = jnp.sum(
@@ -1562,33 +1554,29 @@
     g_rows = slot_of_tile * BLK
 
     if ring:
-        small_block = jnp.zeros((16 * BLK,), BF16).at[:small_count].set(small_params.astype(BF16))
+        features = small_count // 12
+        kinds = jnp.tile(small_params.reshape(features, 12).T, (1, BLK // features))
+        place = jnp.arange(BLK, dtype=jnp.int32) // features == owner_index % (BLK // features)
+        small_block = jnp.concatenate([jnp.where(place, kinds, 0.0), jnp.zeros((4, BLK), F32)], axis=0)
         payload = jnp.concatenate(
-            [tiles.astype(BF16).reshape(slot_count * BLK, BLK), small_block.reshape(16, BLK)], axis=0
+            [tiles.astype(BF16).reshape(slot_count * BLK, BLK), small_block.astype(BF16)], axis=0
         )
-        seg_rows = jnp.broadcast_to(seg_local, (8, rows))
         gathered, prev_tokens, prev_seg = gather_weights(payload, tokens, seg_rows)
         stride = payload.shape[0]
         w_all = gathered.reshape(-1, BLK)
         w_rows = slot_of_tile // slot_count * stride + slot_of_tile % slot_count * BLK
         tail = slot_count * BLK
-        small_all = gathered[:, tail : tail + small_count // BLK, :].reshape(SMALL)
-        prev_seg = prev_seg[:1]
+        group = BLK // features
+        by_kind = jnp.sum(gathered[:, tail:, :].astype(F32).reshape(D // BLK, group, 16, BLK), axis=1)
+        by_kind = by_kind.transpose(1, 0, 2).reshape(16, D)
     else:
         w_all = lax.all_gather(tiles.astype(BF16), axes, axis=0, tiled=True).reshape(-1, BLK)
         w_rows = g_rows
         small_all = lax.all_gather(small_params.astype(BF16), axes, axis=0, tiled=True)
-        prev_tokens, prev_seg = passed_along((tokens, seg_local), "seq", 1)
-
-    table = small_all.astype(F32).reshape(D, 12)
-    smalls = jnp.concatenate(
-        [
-            jnp.stack([table[:, r] for r in (0, 1, 2, 7, 8, 9, 10, 11)], axis=0),
-            jnp.zeros((8, D), F32),
-        ],
-        axis=0,
-    )
-    b_up = table[:, 3:7].reshape(1, FF)
+        by_kind = jnp.pad(small_all.astype(F32).reshape(D, 12).T, ((0, 4), (0, 0)))
+        prev_tokens, prev_seg = passed_along((tokens, seg_rows), "seq", 1)
+
+    b_up = by_kind[3:7].T.reshape(1, FF)
 
     half = ROT // 2
     exponent = jnp.arange(half, dtype=F32) * (2.0 / ROT)
@@ -1598,17 +1586,12 @@
     cos8, sin8 = jnp.cos(angle), jnp.sin(angle)
     tables = (cos8, sin8)
 
-    prev_seg = jnp.where(seq_index == 0, -1, prev_seg)
-    seg_k = jnp.concatenate([prev_seg, seg_local], axis=1).reshape(2 * rows, 1)
-
-    q, k, v, d_out, m = project(w_rows, w_all, prev_tokens, tokens, cotangent, smalls, tables)
-    attn_out, dq, dk, dv, halo, peaks = attend(
-        q, k, v, d_out, seg_local, seg_k, cos8[:, rows:], sin8[:, rows:]
-    )
+    q, k, v, d_out, m = project(w_rows, w_all, prev_tokens, tokens, cotangent, by_kind, tables)
+    attn_out, dq, dk, dv, halo, peaks = attend(q, k, v, d_out, prev_seg, seg_rows, cos8, sin8)
     halo = passed_along(halo, "seq", -1)
     mlp_out, dm, db_up, grads = feed_forward(w_rows, g_rows, w_all, m, cotangent, b_up)
     block_output, input_grad, sums, grads = finish(
-        w_rows, g_rows, w_all, tokens, cotangent, smalls, attn_out, mlp_out, dm, dq, dk, dv, halo, tables, grads
+        w_rows, g_rows, w_all, tokens, cotangent, by_kind, attn_out, mlp_out, dm, dq, dk, dv, halo, tables, grads
     )
 
     small_terms = jnp.concatenate(

time: 472 us -> 464 us (0.983)
  Pallas kernels: 430 us -> 424 us
  local copies, waits for them, and re-layouts: 13.7 us -> 8.8 us
where the time goes in v6:
time: 464 us; the launch traced here: 456 us
  Pallas kernels  424 us (91%)
  other arithmetic  14.9 us (3%)
  local copies, waits for them, and re-layouts  8.8 us (2%)
  starting transfers between devices  6.61 us (1%)
    pallas_call x1, Pallas kernels, sum_gradients(): pl.pallas_call(kernel, out_shape=[jax.ShapeDtypeStruct((OWNED, BLK), F32)...  104 us
    pallas_call x1, Pallas kernels, gather_weights(): pl.pallas_call(kernel, out_shape=[jax.ShapeDtypeStruct((32, rows, BLK), B...  99.7 us
    pallas_call x1, Pallas kernels, attend(): pl.pallas_call(kernel, grid=(PAIRS,), in_specs=[block, keys, keys, block,...  74.8 us
    pallas_call x1, Pallas kernels, feed_forward(): pl.pallas_call(kernel, grid_spec=pltpu.PrefetchScalarGridSpec(num_scalar_...  73.1 us
    pallas_call x1, Pallas kernels, finish(): pl.pallas_call(kernel, grid_spec=pltpu.PrefetchScalarGridSpec(num_scalar_...  38.8 us
    pallas_call x1, Pallas kernels, project(): pl.pallas_call(kernel, grid_spec=pltpu.PrefetchScalarGridSpec(num_scalar_...  24.6 us
  transfers between devices with their start and end apart: 1, of which 0 were waited for; matrix products, arithmetic and copies ran while one was open for 2% of the time, Pallas kernels for 16%

profile of v6, /device:TPU:16, one launch (start us, length us, event | category | flops | bytes accessed | tf_op | source)
XLA Modules:
  0.0 456.2 jit_solution(13024770954128947494)
XLA Ops:
  0.7 1.0 select_reduce_fusion
  2.3 0.8 reshape.217
  3.3 1.6 convert_element_type.15
  4.9 0.9 fusion.1.x_ref
  6.4 99.7 %gather_weights.1 = (bf16[32,3088,128]{2,1,0:T(8,128)(2,1)}, bf16[1024,1024]{1,0:T(8,128)(2,1)}, s32[8,1024]{1,0:T(8,128)}) custom-call(bf16[3088,128]{1,0:T(8,128)(2,1)} %fusion.1.x_ref, bf16[1024,1024]{1,0:T(8,128)(2,1)} %tok_ref.5, s32[8,1024]{1,0:T(8,128)} %broadcast_in_dim.59.seg_ref), custom_call_target="tpu_custom_call" | custom-call | tf_op jit(solution)/shard_map/gather_weights/pallas_call | solution.py:387
  106.1 0.9 convert_reduce_fusion
  107.7 1.0 multiply_sine_fusion
  108.7 24.6 %project.1 = (bf16[8,1024,128]{2,1,0:T(8,128)(2,1)}, bf16[8,2048,128]{2,1,0:T(8,128)(2,1)}, bf16[8,2048,128]{2,1,0:T(8,128)(2,1)}, bf16[8,1024,128]{2,1,0:T(8,128)(2,1)}, bf16[1024,1024]{1,0:T(8,128)(2,1)}) custom-call(s32[768]{0:T(1024)} %get-tuple-element.91.w_rows_ref, bf16[98816,128]{1,0:T(8,128)(2,1)} %bitcast.31, ...), custom_call_target="tpu_custom_call" | custom-call | tf_op jit(solution)/shard_map/project/pallas_call | solution.py:893
  133.2 74.8 %attend.1 = (bf16[8,1024,128]{2,1,0:T(8,128)(2,1)}, bf16[8,1024,128]{2,1,0:T(8,128)(2,1)}, bf16[8,1024,128]{2,1,0:T(8,128)(2,1)}, bf16[8,1024,128]{2,1,0:T(8,128...) custom-call(bf16[8,1024,128]{2,1,0:T(8,128)(2,1)} %get-tuple-element.55.q_ref, ...), custom_call_target="tpu_custom_call" | custom-call | flops 42949672960 | bytes 33554432 | tf_op jit(solution)/shard_map/attend/pallas_call | solution.py:1099
  208.1 6.6 %collective-permute-start = (bf16[2,8,1024,128]{3,2,1,0:T(8,128)(2,1)}, bf16[2,8,1024,128]{3,2,1,0:T(8,128)(2,1)}, u32[]{:S(2)}, u32[]{:S(2)}) collective-permute-start(bf16[2,8,1024,128]{3,2,1,0:T(8,128)(2,1)} %get-tuple-element.67), channel_id=1, source_target_pairs={{1,0},{2,1},{3,2},{4,3},{5,4},{6,5},{7,6},{9,8},{10,9},{11,10},{12... | collective-permute-start | bytes 12582920 | tf_op jit(solution)/shard_map/ppermute | solution.py:1522
  214.7 0.9 compare_reduce_fusion
  216.4 0.9 reshape.222.b_ref
  217.4 1.0 slice_reduce_fusion
  219.1 73.1 %feed_forward.1 = (bf16[1024,1024]{1,0:T(8,128)(2,1)}, bf16[1024,1024]{1,0:T(8,128)(2,1)}, f32[1,4096]{1,0:T(1,128)}, bf16[98304,128]{1,0:T(8,128)(2,1)}) custom-call(s32[768]{0:T(1024)} %get-tuple-element.91.w_rows_ref, s32[768]{0:T(1024)} %get-tuple-element.90.g_rows_ref, bf16[98816,128]{1,0:T(8,128)(2,1)} %bitcast.32, ...), custom_call_target="tpu_custom_call" | custom-call | flops 55834574848 | bytes 50331648 | tf_op jit(solution)/shard_map/feed_forward/pallas_call | solution.py:1274
  292.7 1.4 reduce.12
  294.9 0.8 fusion.14
  295.6 0.8 broadcast_compare_fusion
  296.5 38.8 %finish.1 = (bf16[1024,1024]{1,0:T(8,128)(2,1)}, f32[1024,1024]{1,0:T(8,128)}, f32[8,1024]{1,0:T(8,128)}, bf16[98304,128]{1,0:T(8,128)(2,1)}) custom-call(s32[768]{0:T(1024)} %get-tuple-element.91.w_rows_ref, s32[768]{0:T(1024)} %get-tuple-element.90.g_rows_ref, bf16[98816,128]{1,0:T(8,128)(2,1)} %bitcast.33, ...), custom_call_target="tpu_custom_call", output_to_operand_aliasing={{3}: (15, {})} | custom-call | tf_op jit(solution)/shard_map/finish/pallas_call | solution.py:1422
  335.3 0.8 slice_bitcast_fusion.3
  338.1 103.9 %sum_gradients.1 = (f32[3072,128]{1,0:T(8,128)}, f32[104,128]{1,0:T(8,128)}) custom-call(bf16[98304,128]{1,0:T(8,128)(2,1)} %get-tuple-element.71.g_ref, f32[104,128]{1,0:T(8,128)} %pad_maximum_fusion.1.e_ref), custom_call_target="tpu_custom_call" | custom-call | tf_op jit(solution)/shard_map/sum_gradients/pallas_call | solution.py:724
  442.0 0.8 slice_bitcast_fusion
  442.8 1.2 fusion.17
  445.6 9.0 %update_tiles.1 = (f32[24,128,128]{2,1,0:T(8,128)}, bf16[24,128,128]{2,1,0:T(8,128)(2,1)}, f32[24,128,128]{2,1,0:T(8,128)}, f32[24,128,128]{2,1,0:T(8,128)}) custom-call(f32[24,128,128]{2,1,0:T(8,128)} %bitcast.34, f32[24,128,128]{2,1,0:T(8,128)} %w_ref.1, f32[24,128,128]{2,1,0:T(8,128)} %l_ref.1, f32[24,128,128]{2,1,0:T(8,128)} %r_ref.1, ...), custom_call_target="tpu_custom_call" | custom-call | tf_op jit(solution)/shard_map/update_tiles/pallas_call | solution.py:1489
  454.6 1.1 copy.52
  (39 shorter events, 7.9 us)
Async XLA Ops:
  0.6 5.2 %copy-start.2 = (s32[1,1024]{1,0:T(1,128)S(1)}, s32[1,1024]{1,0:T(1,128)}, u32[]{:S(2)}) copy-start(s32[1,1024]{1,0:T(1,128)} %param.16) | copy-start | bytes 12292
  208.1 88.4 %collective-permute-start = (bf16[2,8,1024,128]{3,2,1,0:T(8,128)(2,1)}, bf16[2,8,1024,128]{3,2,1,0:T(8,128)(2,1)}, u32[]{:S(2)}, u32[]{:S(2)}) collective-permute-start(bf16[2,8,1024,128]{3,2,1,0:T(8,128)(2,1)} %get-tuple-element.67), channel_id=1, source_target_pairs={{1,0},{2,1},{3,2},{4,3},{5,4},{6,5},{7,6},{9,8},{10,9},{11,10},{12... | collective-permute-start | bytes 12582920 | tf_op jit(solution)/shard_map/ppermute | solution.py:1522
  338.1 106.8 %copy-start.1 = (f32[384]{0:T(512)S(1)}, f32[384]{0:T(512)}, u32[]{:S(2)}) copy-start(f32[384]{0:T(512)} %param.24) | copy-start | bytes 4612
  338.1 106.8 %copy-start.3 = (f32[384]{0:T(512)S(1)}, f32[384]{0:T(512)}, u32[]{:S(2)}) copy-start(f32[384]{0:T(512)} %param.25) | copy-start | bytes 4612
  338.1 106.8 %copy-start.4 = (f32[384]{0:T(512)S(1)}, f32[384]{0:T(512)}, u32[]{:S(2)}) copy-start(f32[384]{0:T(512)} %param.26) | copy-start | bytes 4612
  445.6 9.0 %copy-start = (f32[3072,128]{1,0:T(8,128)S(1)}, f32[3072,128]{1,0:T(8,128)}, u32[]{:S(2)}) copy-start(f32[3072,128]{1,0:T(8,128)} %get-tuple-element.75) | copy-start | bytes 4718596

commit v7 on v6

--- a/solution.py
+++ b/solution.py
@@ -951,7 +951,7 @@
 
     def kernel(
         q_ref, k_ref, v_ref, do_ref, pseg_ref, seg_ref, cos_ref, sin_ref,
-        o_ref, dq_ref, dk_ref, dv_ref, halo_ref, peak_ref, bias, kt, vt, el_ref, ds_ref, dks, dvs, base, key_seg,
+        o_ref, dq_ref, dk_ref, dv_ref, halo_ref, peak_ref, bias, kt, vt, el_ref, ds_ref, dks, dvs, key_seg,
     ):
         p = pl.program_id(0)
 
@@ -978,29 +978,31 @@
         reach = jnp.max(jnp.sum(k_float * k_float, axis=0)) * jnp.max(jnp.sum(q_float * q_float, axis=1))
         safe = reach < SAFE_SCORE * SAFE_SCORE
 
+        def rows_from(i, offset, count):
+            first = i * QB + offset
+            return pl.ds(first if isinstance(i, int) else pl.multiple_of(first, QB), count)
+
         def keys_at(ref, i, c):
-            return ref[i * QB + c * CHUNK : i * QB + (c + 1) * CHUNK, :]
+            return ref[rows_from(i, c * CHUNK, CHUNK), :]
 
         def prepare(i):
-            q_all = (q_ref[i * QB : (i + 1) * QB, :].astype(F32) * scale).astype(BF16)
+            q_all = (q_ref[rows_from(i, 0, QB), :].astype(F32) * scale).astype(BF16)
             return q_all, heads_apart(q_all.T)
 
         def scores(i, c, q_apart):
             return dot(keys_at(k_ref, i, c), q_apart) + two(bias[i, c * CHUNK : (c + 1) * CHUNK])
 
-        def row_tops(i):
-            q_apart = prepare(i)[1]
+        def row_tops(i, q_apart):
             for c in range(n):
                 t = fold(scores(i, c, q_apart), jnp.max)
                 most = t if c == 0 else jnp.maximum(most, t)
-            base[i] = jnp.max(most, axis=0, keepdims=True)
-
-        def forward(i, q_apart, found):
-            low = base[i]
+            return jnp.max(most, axis=0, keepdims=True)
+
+        def forward(i, q_apart, found, low=None):
             top8 = sum8 = None
             for c in range(n):
                 st = scores(i, c, q_apart)
-                e = jnp.exp(st - low)
+                e = jnp.exp(st if low is None else st - low)
                 el_ref[i % 2, c * CHUNK : (c + 1) * CHUNK] = e.astype(BF16)
                 t, u = fold(st, jnp.max), fold(e, jnp.sum)
                 top8, sum8 = (t, u) if c == 0 else (jnp.maximum(top8, t), sum8 + u)
@@ -1014,7 +1016,7 @@
             )
 
         def both(t, x_ref, i):
-            span = slice(i * QB, i * QB + SPAN)
+            span = rows_from(i, 0, SPAN)
             return jnp.concatenate(
                 [dot(t[:HEAD, span], x_ref[i % 2, :, :QB]), dot(t[HEAD:, span], x_ref[i % 2, :, QB:])], axis=0
             )
@@ -1022,8 +1024,8 @@
         def output(i, inv):
             raw = both(vt, el_ref, i)
             inv2 = per_head(inv)
-            o_ref[i * QB : (i + 1) * QB, :] = (raw * inv2).T.astype(BF16)
-            do_s = (do_ref[i * QB : (i + 1) * QB, :].astype(F32).T * inv2).astype(BF16)
+            o_ref[rows_from(i, 0, QB), :] = (raw * inv2).T.astype(BF16)
+            do_s = (do_ref[rows_from(i, 0, QB), :].astype(F32).T * inv2).astype(BF16)
             m = do_s.astype(F32) * raw
             mean = jnp.concatenate(
                 [jnp.sum(m[:HEAD], axis=0, keepdims=True), jnp.sum(m[HEAD:], axis=0, keepdims=True)], axis=1
@@ -1042,10 +1044,10 @@
             q_rows = stacked(q_all)
             for c in range(n):
                 w = slice(c * CHUNK, (c + 1) * CHUNK)
-                at = slice(i * QB + c * CHUNK, i * QB + (c + 1) * CHUNK)
+                at = rows_from(i, c * CHUNK, CHUNK)
                 v_part = dot(el_ref[i % 2, w], do_rows)
                 k_part = dot(ds_ref[i % 2, w], q_rows)
-                if i == 0 or c == n - 1:
+                if c == n - 1 or (isinstance(i, int) and i == 0):
                     dvs[at, :] = v_part
                     dks[at, :] = k_part
                 else:
@@ -1053,12 +1055,12 @@
                     dks[at, :] += k_part
                 yield
             dq = both(kt, ds_ref, i) * scale
-            cos_t, sin_t = cos_ref[:, i * QB : (i + 1) * QB], sin_ref[:, i * QB : (i + 1) * QB]
+            cos_t, sin_t = cos_ref[:, rows_from(i, 0, QB)], sin_ref[:, rows_from(i, 0, QB)]
             turned = []
             for h in range(2):
                 f, g = dq[h * HEAD : h * HEAD + half], dq[h * HEAD + half : h * HEAD + ROT]
                 turned += [f * cos_t + g * sin_t, g * cos_t - f * sin_t, dq[h * HEAD + ROT : (h + 1) * HEAD]]
-            dq_ref[i * QB : (i + 1) * QB, :] = jnp.concatenate(turned, axis=0).T.astype(BF16)
+            dq_ref[rows_from(i, 0, QB), :] = jnp.concatenate(turned, axis=0).T.astype(BF16)
             yield
 
         def run():
@@ -1078,19 +1080,30 @@
                     score_grads(i, do_s, mean)
                     held = (q_all, do_s)
             peak_ref[...] = jnp.broadcast_to(top, peak_ref.shape)
-            halo_ref[0] = dks[:rows, :].astype(BF16)
-            halo_ref[1] = dvs[:rows, :].astype(BF16)
-            dk_ref[...] = dks[rows:, :].astype(BF16)
-            dv_ref[...] = dvs[rows:, :].astype(BF16)
-
-        base[...] = jnp.zeros_like(base)
-
-        @pl.when(jnp.logical_not(safe))
-        def _():
-            for i in range(blocks):
-                row_tops(i)
-
-        run()
+
+        def run_shifted():
+            dks[:WINDOW, :] = jnp.zeros((WINDOW, BLK), F32)
+            dvs[:WINDOW, :] = jnp.zeros((WINDOW, BLK), F32)
+            peak_ref[...] = jnp.full(peak_ref.shape, MASKED, F32)
+
+            def body(i, carry):
+                q_all, q_apart = prepare(i)
+                found = []
+                interleave(forward(i, q_apart, found, row_tops(i, q_apart)))
+                do_s, mean = output(i, found[1])
+                score_grads(i, do_s, mean)
+                interleave(input_grads(i, q_all, do_s))
+                peak_ref[...] = jnp.maximum(peak_ref[...], found[0])
+                return carry
+
+            lax.fori_loop(0, blocks, body, 0)
+
+        pl.when(safe)(run)
+        pl.when(jnp.logical_not(safe))(run_shifted)
+        halo_ref[0] = dks[:rows, :].astype(BF16)
+        halo_ref[1] = dvs[:rows, :].astype(BF16)
+        dk_ref[...] = dks[rows:, :].astype(BF16)
+        dv_ref[...] = dvs[rows:, :].astype(BF16)
 
     block = pl.BlockSpec((None, rows, BLK), lambda p: (p, 0, 0))
     keys = pl.BlockSpec((None, 2 * rows, BLK), lambda p: (p, 0, 0))
@@ -1123,7 +1136,6 @@
             pltpu.VMEM((2, SPAN, 2 * QB), BF16),
             pltpu.VMEM((2 * rows, BLK), F32),
             pltpu.VMEM((2 * rows, BLK), F32),
-            pltpu.VMEM((blocks, 1, 2 * QB), F32),
             pltpu.VMEM((2 * rows, BLK), F32),
         ],
         compiler_params=params(dimension_semantics=("arbitrary",)),
@@ -1320,7 +1332,7 @@
     def kernel(
         w_rows_ref, g_rows_ref, w_ref, tok_ref, g_ref, small_ref, o_ref, mlp_ref, dm_ref, dq_ref, dk_ref, dv_ref,
         halo_ref, cos_ref, sin_ref, _,
-        out_ref, dx_ref, sum_ref, gr_ref, wqkv, wo, at, dp, stage, sems, gsem,
+        out_ref, dx_ref, sum_ref, gr_ref, wqkv, wo, at, dp, das, stage, sems, gsem,
     ):
         i = pl.program_id(0)
 
@@ -1335,44 +1347,48 @@
 
         @pl.when(i == 0)
         def _():
+            fetch(0, QKV_TILES, 3 * D // BLK, wqkv, sems.at[1])
             fetch(OUT_BASE, OUT_TILES, D // BLK, wo, sems.at[0])
-            fetch(0, QKV_TILES, 3 * D // BLK, wqkv, sems.at[1])
             sum_ref[...] = jnp.zeros_like(sum_ref)
+            pltpu.make_async_copy(wqkv, wqkv, sems.at[1]).wait()
+
+        @pl.when(i == 1)
+        def _():
             pltpu.make_async_copy(wo, wo, sems.at[0]).wait()
 
-        @pl.when(i < steps)
-        def _():
-            here = pl.ds(pl.multiple_of(i * ROWB, ROWB), ROWB)
+        def at_block(j):
+            return pl.ds(pl.multiple_of(j * ROWB, ROWB), ROWB)
+
+        def add(row, value):
+            sum_ref[row : row + 1, :] += jnp.sum(value, axis=0, keepdims=True)
+
+        def front():
+            here = at_block(i)
+            back_turn = spread_tables(cos_ref[...], -sin_ref[...])
+            for j in range(PAIRS):
+                cols = j * BLK
+                dk_all = dk_ref[j].astype(F32) + halo_ref[0, j].astype(F32)
+                dv_all = dv_ref[j].astype(F32) + halo_ref[1, j].astype(F32)
+                dp[here, cols : cols + BLK] = dq_ref[j]
+                dp[here, D + cols : D + cols + BLK] = rope(dk_all, *back_turn).astype(BF16)
+                dp[here, 2 * D + cols : 2 * D + cols + BLK] = dv_all.astype(BF16)
+            das[i % 2] = dot(dp[here, :], wqkv[...], NT)
+
+        def back():
+            here = at_block(i - 1)
             x = tok_ref[...].astype(F32)
             grad = g_ref[here, :].astype(F32)
             normed, inv = norm_rows(x)
             g1, g2 = small_ref[G1, :], small_ref[G2, :]
             attn = dot(side_by_side(o_ref, here), wo[...]) + small_ref[B_O, :]
             out_ref[...] = (x + attn + (mlp_ref[...].astype(F32) + small_ref[B_DOWN, :])).astype(BF16)
-            back = spread_tables(cos_ref[...], -sin_ref[...])
-            for j in range(PAIRS):
-                cols = j * BLK
-                dk_all = dk_ref[j].astype(F32) + halo_ref[0, j].astype(F32)
-                dv_all = dv_ref[j].astype(F32) + halo_ref[1, j].astype(F32)
-                dp[here, cols : cols + BLK] = dq_ref[j]
-                dp[here, D + cols : D + cols + BLK] = rope(dk_all, *back).astype(BF16)
-                dp[here, 2 * D + cols : 2 * D + cols + BLK] = dv_all.astype(BF16)
-
-            @pl.when(i == 0)
-            def _():
-                pltpu.make_async_copy(wqkv, wqkv, sems.at[1]).wait()
-
-            da = dot(dp[here, :], wqkv[...], NT)
+            da = das[(i - 1) % 2]
             at[:, here] = (normed * g1 + small_ref[C1, :]).astype(BF16).T
             dmv = dm_ref[...].astype(F32)
             dn = da * g1 + dmv * g2
             mean_dn = jnp.mean(dn, axis=-1, keepdims=True)
             mean_dnn = jnp.mean(dn * normed, axis=-1, keepdims=True)
             dx_ref[...] = grad + inv * (dn - mean_dn - normed * mean_dnn)
-
-            def add(row, value):
-                sum_ref[row : row + 1, :] += jnp.sum(value, axis=0, keepdims=True)
-
             add(0, dp[here, :D].astype(F32))
             add(1, dp[here, 2 * D :].astype(F32))
             add(2, grad)
@@ -1381,6 +1397,15 @@
             add(5, dmv * normed)
             add(6, dmv)
 
+        @pl.when(i == 0)
+        def _():
+            front()
+
+        @pl.when((i > 0) & (i < steps))
+        def _():
+            back()
+            front()
+
         slot = i % 2
 
         def drain(sl):
@@ -1397,28 +1422,38 @@
         def _():
             drain(slot)
 
-        @pl.when((i >= steps) & (i < steps + q_cols))
-        def _():
-            c = i - steps
+        def out_columns(c):
+            stage[slot] = dot(side_by_side(o_ref), g_ref[:, c * FB : (c + 1) * FB], TN).astype(BF16)
+            send(OUT_BASE, D // BLK, c)
+
+        @pl.when(i == steps)
+        def _():
+            out_columns(0)
+            back()
+
+        @pl.when((i > steps) & (i <= steps + q_cols))
+        def _():
+            c = i - steps - 1
             stage[slot] = dot(at[...], dp[:, pl.ds(pl.multiple_of(c * FB, FB), FB)]).astype(BF16)
             send(0, 3 * D // BLK, c)
 
-        @pl.when(i >= steps + q_cols)
-        def _():
-            c = i - steps - q_cols
-            stage[slot] = dot(side_by_side(o_ref), g_ref[:, pl.ds(pl.multiple_of(c * FB, FB), FB)], TN).astype(BF16)
-            send(OUT_BASE, D // BLK, c)
+        for c in range(1, o_cols):
+
+            @pl.when(i == steps + q_cols + c)
+            def _():
+                out_columns(c)
 
         @pl.when(i == last - 1)
         def _():
             drain(0)
             drain(1)
 
-    here = lambda i, *_: (jnp.minimum(i, steps - 1), 0)
+    ahead = lambda i: jnp.minimum(i, steps - 1)
+    behind = lambda i: jnp.clip(i - 1, 0, steps - 1)
     whole = lambda *shape: pl.BlockSpec(shape, lambda i, *_: (0, 0))
-    block = pl.BlockSpec((ROWB, D), here)
-    pairs = pl.BlockSpec((PAIRS, ROWB, BLK), lambda i, *_: (0, jnp.minimum(i, steps - 1), 0))
-    table = pl.BlockSpec((ROT // 2, ROWB), lambda i, *_: (0, steps + jnp.minimum(i, steps - 1)))
+    block = pl.BlockSpec((ROWB, D), lambda i, *_: (behind(i), 0))
+    pairs = pl.BlockSpec((PAIRS, ROWB, BLK), lambda i, *_: (0, ahead(i), 0))
+    table = pl.BlockSpec((ROT // 2, ROWB), lambda i, *_: (0, steps + ahead(i)))
     return pl.pallas_call(
         kernel,
         grid_spec=pltpu.PrefetchScalarGridSpec(
@@ -1427,7 +1462,7 @@
             in_specs=[
                 ANY, block, whole(rows, D), whole(16, D), pl.BlockSpec((PAIRS, rows, BLK), lambda i, *_: (0, 0, 0)),
                 block, block, pairs, pairs, pairs,
-                pl.BlockSpec((2, PAIRS, ROWB, BLK), lambda i, *_: (0, 0, jnp.minimum(i, steps - 1), 0)),
+                pl.BlockSpec((2, PAIRS, ROWB, BLK), lambda i, *_: (0, 0, ahead(i), 0)),
                 table, table, ANY,
             ],
             out_specs=[block, block, whole(8, D), ANY],
@@ -1436,6 +1471,7 @@
                 pltpu.VMEM((D, D), BF16),
                 pltpu.VMEM((D, rows), BF16),
                 pltpu.VMEM((rows, 3 * D), BF16),
+                pltpu.VMEM((2, ROWB, D), F32),
                 pltpu.VMEM((2, D, FB), BF16),
                 pltpu.SemaphoreType.DMA((2,)),
                 pltpu.SemaphoreType.DMA((2,)),
@@ -1462,11 +1498,21 @@
     return dot(a[0], b[0], dims) + (dot(a[0], b[1], dims) + dot(a[1], b[0], dims))
 
 
-def update_tiles(grads, tiles, left, right, first, second, scale):
+def update_tiles(ids, roots, grads, tiles, left, right, first, second):
     count = tiles.shape[0]
     group = max(g for g in (1, 2, 3, 4, 6, 8) if count % g == 0)
 
-    def kernel(g_ref, w_ref, l_ref, r_ref, m_ref, v_ref, s_ref, w_out, low_out, m_out, v_out):
+    def kernel(ids_ref, roots_ref, g_ref, w_ref, l_ref, r_ref, m_ref, v_ref, w_out, low_out, m_out, v_out):
+        lane = lax.broadcasted_iota(jnp.int32, (1, BLK), 1)
+
+        def column_scale(t):
+            number = ids_ref[pl.program_id(0) * group + t]
+            column = number % (3 * D // BLK)
+            head = column % PAIRS * 2
+            clipped = (number < QKV_TILES) & (column < 2 * PAIRS)
+            picked = jnp.where(lane < HEAD, roots_ref[head], roots_ref[head + 1])
+            return jnp.where(clipped, picked, 1.0)
+
         turned = []
         for t in range(group):
             l, r = halves(l_ref[t]), halves(r_ref[t])
@@ -1477,36 +1523,26 @@
             v_new = BETA * v_ref[t] + (1.0 - BETA) * turned[t] * turned[t]
             ratio = m_new / (jnp.sqrt(v_new) + ADAM_EPS)
             back = dot3(halves(dot3(l, halves(ratio))), r, NT)
-            w_new = (w_ref[t] - LEARN * back) * s_ref[t]
+            w_new = (w_ref[t] - LEARN * back) * column_scale(t)
             w_out[t] = w_new
             low_out[t] = w_new.astype(BF16)
             m_out[t] = m_new
             v_out[t] = v_new
 
-    block = pl.BlockSpec((group, BLK, BLK), lambda i: (i, 0, 0))
-    row = pl.BlockSpec((group, 1, BLK), lambda i: (i, 0, 0))
+    block = pl.BlockSpec((group, BLK, BLK), lambda i, *_: (i, 0, 0))
     like = lambda t: jax.ShapeDtypeStruct(tiles.shape, t)
     return pl.pallas_call(
         kernel,
-        grid=(count // group,),
-        in_specs=[block] * 6 + [row],
-        out_specs=[block] * 4,
+        grid_spec=pltpu.PrefetchScalarGridSpec(
+            num_scalar_prefetch=2,
+            grid=(count // group,),
+            in_specs=[block] * 6,
+            out_specs=[block] * 4,
+        ),
         out_shape=[like(F32), like(BF16), like(F32), like(F32)],
         compiler_params=params(dimension_semantics=("arbitrary",)),
         name="update_tiles",
-    )(grads, tiles, left, right, first, second, scale)
-
-
-def column_scales(tile_ids, factors):
-    columns = (tile_ids % (3 * D // BLK))[:, None] * BLK + jnp.arange(BLK, dtype=jnp.int32)[None, :]
-    head_index = columns % D // HEAD
-    root_factor = jnp.sqrt(factors)
-    picked = jnp.sum(
-        jnp.where(head_index[..., None] == jnp.arange(HEADS, dtype=jnp.int32), root_factor, 0.0),
-        axis=-1,
-    )
-    clipped = (tile_ids[:, None] < QKV_TILES) & (columns < 2 * D)
-    return jnp.where(clipped, picked, 1.0)
+    )(ids, roots, grads, tiles, left, right, first, second)
 
 
 def small_update(grads, params_, first_moment, second_moment):
@@ -1622,9 +1658,8 @@
     local_ids = lax.dynamic_slice_in_dim(tile_of_slot, owner_index * slot_count, slot_count, 0)
     limit = threshold[0]
     factors = limit / jnp.maximum(head_peak, limit)
-    scale = column_scales(local_ids, factors).reshape(slot_count, 1, BLK)
     new_tiles, new_low, new_first, new_second = update_tiles(
-        tile_grads, tiles, left_bases, right_bases, first_moments, second_moments, scale
+        local_ids, jnp.sqrt(factors), tile_grads, tiles, left_bases, right_bases, first_moments, second_moments
     )
     new_small, new_small_first, new_small_second = small_update(
         small_grads, small_params, small_first, small_second

time: 464 us -> 460 us (level)
  no operation moved by 1% of the time
where the time goes in v7:
time: 460 us; the launch traced here: 452 us
  Pallas kernels  421 us (92%)
  other arithmetic  12.8 us (3%)
  local copies, waits for them, and re-layouts  10.1 us (2%)
  starting transfers between devices  6.62 us (1%)
    pallas_call x1, Pallas kernels, sum_gradients(): pl.pallas_call(kernel, out_shape=[jax.ShapeDtypeStruct((OWNED, BLK), F32)...  104 us
    pallas_call x1, Pallas kernels, gather_weights(): pl.pallas_call(kernel, out_shape=[jax.ShapeDtypeStruct((32, rows, BLK), B...  99.7 us
    pallas_call x1, Pallas kernels, feed_forward(): pl.pallas_call(kernel, grid_spec=pltpu.PrefetchScalarGridSpec(num_scalar_...  73.2 us
    pallas_call x1, Pallas kernels, attend(): pl.pallas_call(kernel, grid=(PAIRS,), in_specs=[block, keys, keys, block,...  71.8 us
    pallas_call x1, Pallas kernels, finish(): pl.pallas_call(kernel, grid_spec=pltpu.PrefetchScalarGridSpec(num_scalar_...  38 us
    pallas_call x1, Pallas kernels, project(): pl.pallas_call(kernel, grid_spec=pltpu.PrefetchScalarGridSpec(num_scalar_...  24.6 us
    pallas_call x1, Pallas kernels, update_tiles(): pl.pallas_call(kernel, grid_spec=pltpu.PrefetchScalarGridSpec(num_scalar_...  9.51 us
  transfers between devices with their start and end apart: 1, of which 0 were waited for; matrix products, arithmetic and copies ran while one was open for 2% of the time, Pallas kernels for 16%

profile of v7, /device:TPU:16, one launch (start us, length us, event | category | flops | bytes accessed | tf_op | source)
XLA Modules:
  0.0 451.9 jit_solution(5743317607869325265)
XLA Ops:
  0.7 1.0 select_reduce_fusion
  2.3 0.8 reshape.111
  3.3 1.6 convert_element_type.15
  4.9 0.9 fusion.1.x_ref
  6.4 99.7 %gather_weights.1 = (bf16[32,3088,128]{2,1,0:T(8,128)(2,1)}, bf16[1024,1024]{1,0:T(8,128)(2,1)}, s32[8,1024]{1,0:T(8,128)}) custom-call(bf16[3088,128]{1,0:T(8,128)(2,1)} %fusion.1.x_ref, bf16[1024,1024]{1,0:T(8,128)(2,1)} %tok_ref.5, s32[8,1024]{1,0:T(8,128)} %broadcast_in_dim.42.seg_ref), custom_call_target="tpu_custom_call" | custom-call | tf_op jit(solution)/shard_map/gather_weights/pallas_call | solution.py:387
  106.1 0.9 convert_reduce_fusion
  107.7 1.0 multiply_sine_fusion
  108.6 24.6 %project.1 = (bf16[8,1024,128]{2,1,0:T(8,128)(2,1)}, bf16[8,2048,128]{2,1,0:T(8,128)(2,1)}, bf16[8,2048,128]{2,1,0:T(8,128)(2,1)}, bf16[8,1024,128]{2,1,0:T(8,128)(2,1)}, bf16[1024,1024]{1,0:T(8,128)(2,1)}) custom-call(s32[768]{0:T(1024)} %get-tuple-element.91.w_rows_ref, bf16[98816,128]{1,0:T(8,128)(2,1)} %bitcast.30, ...), custom_call_target="tpu_custom_call" | custom-call | tf_op jit(solution)/shard_map/project/pallas_call | solution.py:893
  133.2 71.8 %attend.1 = (bf16[8,1024,128]{2,1,0:T(8,128)(2,1)}, bf16[8,1024,128]{2,1,0:T(8,128)(2,1)}, bf16[8,1024,128]{2,1,0:T(8,128)(2,1)}, bf16[8,1024,128]{2,1,0:T(8,128...) custom-call(bf16[8,1024,128]{2,1,0:T(8,128)(2,1)} %get-tuple-element.55.q_ref, ...), custom_call_target="tpu_custom_call" | custom-call | flops 42949672960 | bytes 33554432 | tf_op jit(solution)/shard_map/attend/pallas_call | solution.py:1112
  205.0 6.6 %collective-permute-start = (bf16[2,8,1024,128]{3,2,1,0:T(8,128)(2,1)}, bf16[2,8,1024,128]{3,2,1,0:T(8,128)(2,1)}, u32[]{:S(2)}, u32[]{:S(2)}) collective-permute-start(bf16[2,8,1024,128]{3,2,1,0:T(8,128)(2,1)} %get-tuple-element.67), channel_id=1, source_target_pairs={{1,0},{2,1},{3,2},{4,3},{5,4},{6,5},{7,6},{9,8},{10,9},{11,10},{12... | collective-permute-start | bytes 12582920 | tf_op jit(solution)/shard_map/ppermute | solution.py:1558
  211.7 1.2 compare_reduce_fusion
  213.5 1.3 dynamic_slice.7.ids_ref
  215.0 0.9 reshape.116.b_ref
  216.0 1.0 slice_reduce_fusion
  217.7 73.2 %feed_forward.1 = (bf16[1024,1024]{1,0:T(8,128)(2,1)}, bf16[1024,1024]{1,0:T(8,128)(2,1)}, f32[1,4096]{1,0:T(1,128)}, bf16[98304,128]{1,0:T(8,128)(2,1)}) custom-call(s32[768]{0:T(1024)} %get-tuple-element.91.w_rows_ref, s32[768]{0:T(1024)} %get-tuple-element.90.g_rows_ref, bf16[98816,128]{1,0:T(8,128)(2,1)} %bitcast.31, ...), custom_call_target="tpu_custom_call" | custom-call | flops 55834574848 | bytes 50331648 | tf_op jit(solution)/shard_map/feed_forward/pallas_call | solution.py:1286
  291.4 1.4 reduce.12
  293.6 38.0 %finish.1 = (bf16[1024,1024]{1,0:T(8,128)(2,1)}, f32[1024,1024]{1,0:T(8,128)}, f32[8,1024]{1,0:T(8,128)}, bf16[98304,128]{1,0:T(8,128)(2,1)}) custom-call(s32[768]{0:T(1024)} %get-tuple-element.91.w_rows_ref, s32[768]{0:T(1024)} %get-tuple-element.90.g_rows_ref, bf16[98816,128]{1,0:T(8,128)(2,1)} %bitcast.32, ...), custom_call_target="tpu_custom_call", output_to_operand_aliasing={{3}: (15, {})} | custom-call | tf_op jit(solution)/shard_map/finish/pallas_call | solution.py:1457
  331.6 0.8 slice_bitcast_fusion.3
  332.4 0.8 slice_bitcast_fusion.1
  334.4 103.9 %sum_gradients.1 = (f32[3072,128]{1,0:T(8,128)}, f32[104,128]{1,0:T(8,128)}) custom-call(bf16[98304,128]{1,0:T(8,128)(2,1)} %get-tuple-element.71.g_ref, f32[104,128]{1,0:T(8,128)} %pad_maximum_fusion.1.e_ref), custom_call_target="tpu_custom_call" | custom-call | tf_op jit(solution)/shard_map/sum_gradients/pallas_call | solution.py:724
  438.3 0.8 slice_bitcast_fusion
  439.1 1.2 fusion.10
  441.0 9.5 %update_tiles.1 = (f32[24,128,128]{2,1,0:T(8,128)}, bf16[24,128,128]{2,1,0:T(8,128)(2,1)}, f32[24,128,128]{2,1,0:T(8,128)}, f32[24,128,128]{2,1,0:T(8,128)}) custom-call(s32[24]{0:T(128)} %dynamic_slice.7.ids_ref, f32[16]{0:T(128)} %get-tuple-element.86.roots_ref, f32[24,128,128]{2,1,0:T(8,128)} %bitcast.33, f32[24,128,128]{2,1,0:T(8,128)} %w_ref.1, ...), custom_call_target="tpu_custom_call" | custom-call | tf_op jit(solution)/shard_map/update_tiles/pallas_call | solution.py:1534
  450.5 1.1 copy.52
  (35 shorter events, 6.2 us)
Async XLA Ops:
  0.6 5.2 %copy-start.2 = (s32[1,1024]{1,0:T(1,128)S(1)}, s32[1,1024]{1,0:T(1,128)}, u32[]{:S(2)}) copy-start(s32[1,1024]{1,0:T(1,128)} %param.16) | copy-start | bytes 12292
  205.0 88.5 %collective-permute-start = (bf16[2,8,1024,128]{3,2,1,0:T(8,128)(2,1)}, bf16[2,8,1024,128]{3,2,1,0:T(8,128)(2,1)}, u32[]{:S(2)}, u32[]{:S(2)}) collective-permute-start(bf16[2,8,1024,128]{3,2,1,0:T(8,128)(2,1)} %get-tuple-element.67), channel_id=1, source_target_pairs={{1,0},{2,1},{3,2},{4,3},{5,4},{6,5},{7,6},{9,8},{10,9},{11,10},{12... | collective-permute-start | bytes 12582920 | tf_op jit(solution)/shard_map/ppermute | solution.py:1558
  334.4 105.9 %copy-start.1 = (f32[384]{0:T(512)S(1)}, f32[384]{0:T(512)}, u32[]{:S(2)}) copy-start(f32[384]{0:T(512)} %param.24) | copy-start | bytes 4612
  334.4 106.0 %copy-start.3 = (f32[384]{0:T(512)S(1)}, f32[384]{0:T(512)}, u32[]{:S(2)}) copy-start(f32[384]{0:T(512)} %param.25) | copy-start | bytes 4612
  334.4 106.0 %copy-start.4 = (f32[384]{0:T(512)S(1)}, f32[384]{0:T(512)}, u32[]{:S(2)}) copy-start(f32[384]{0:T(512)} %param.26) | copy-start | bytes 4612
  441.0 9.5 %copy-start = (f32[3072,128]{1,0:T(8,128)S(1)}, f32[3072,128]{1,0:T(8,128)}, u32[]{:S(2)}) copy-start(f32[3072,128]{1,0:T(8,128)} %get-tuple-element.75) | copy-start | bytes 4718596

commit v8 on v7

--- a/solution.py
+++ b/solution.py
@@ -951,7 +951,7 @@
 
     def kernel(
         q_ref, k_ref, v_ref, do_ref, pseg_ref, seg_ref, cos_ref, sin_ref,
-        o_ref, dq_ref, dk_ref, dv_ref, halo_ref, peak_ref, bias, kt, vt, el_ref, ds_ref, dks, dvs, key_seg,
+        o_ref, dq_ref, dk_ref, dv_ref, halo_ref, peak_ref, bias, kt, vt, el_ref, ds_ref, dks, dvs, key_seg, tops,
     ):
         p = pl.program_id(0)
 
@@ -1079,12 +1079,12 @@
                     do_s, mean = output(i, inv)
                     score_grads(i, do_s, mean)
                     held = (q_all, do_s)
-            peak_ref[...] = jnp.broadcast_to(top, peak_ref.shape)
+            tops[...] = jnp.broadcast_to(top, tops.shape)
 
         def run_shifted():
             dks[:WINDOW, :] = jnp.zeros((WINDOW, BLK), F32)
             dvs[:WINDOW, :] = jnp.zeros((WINDOW, BLK), F32)
-            peak_ref[...] = jnp.full(peak_ref.shape, MASKED, F32)
+            tops[...] = jnp.full(tops.shape, MASKED, F32)
 
             def body(i, carry):
                 q_all, q_apart = prepare(i)
@@ -1093,13 +1093,16 @@
                 do_s, mean = output(i, found[1])
                 score_grads(i, do_s, mean)
                 interleave(input_grads(i, q_all, do_s))
-                peak_ref[...] = jnp.maximum(peak_ref[...], found[0])
+                tops[...] = jnp.maximum(tops[...], found[0])
                 return carry
 
             lax.fori_loop(0, blocks, body, 0)
 
         pl.when(safe)(run)
         pl.when(jnp.logical_not(safe))(run_shifted)
+        head_tops = [jnp.max(tops[0:1, h * QB : (h + 1) * QB], axis=1, keepdims=True) for h in range(2)]
+        lane = lax.broadcasted_iota(jnp.int32, peak_ref.shape, 1)
+        peak_ref[...] = jnp.where(lane == 0, head_tops[0], head_tops[1])
         halo_ref[0] = dks[:rows, :].astype(BF16)
         halo_ref[1] = dvs[:rows, :].astype(BF16)
         dk_ref[...] = dks[rows:, :].astype(BF16)
@@ -1118,7 +1121,7 @@
         out_specs=[
             block, block, block, block,
             pl.BlockSpec((2, None, rows, BLK), lambda p: (0, p, 0, 0)),
-            pl.BlockSpec((8, 2 * QB), lambda p: (p, 0)),
+            pl.BlockSpec((8, BLK), lambda p: (p, 0)),
         ],
         out_shape=[
             jax.ShapeDtypeStruct((PAIRS, rows, BLK), BF16),
@@ -1126,7 +1129,7 @@
             jax.ShapeDtypeStruct((PAIRS, rows, BLK), BF16),
             jax.ShapeDtypeStruct((PAIRS, rows, BLK), BF16),
             jax.ShapeDtypeStruct((2, PAIRS, rows, BLK), BF16),
-            jax.ShapeDtypeStruct((8 * PAIRS, 2 * QB), F32),
+            jax.ShapeDtypeStruct((8 * PAIRS, BLK), F32),
         ],
         scratch_shapes=[
             pltpu.VMEM((blocks, SPAN, QB), F32),
@@ -1137,6 +1140,7 @@
             pltpu.VMEM((2 * rows, BLK), F32),
             pltpu.VMEM((2 * rows, BLK), F32),
             pltpu.VMEM((2 * rows, BLK), F32),
+            pltpu.VMEM((8, 2 * QB), F32),
         ],
         compiler_params=params(dimension_semantics=("arbitrary",)),
         cost_estimate=pl.CostEstimate(flops=40 << 30, bytes_accessed=32 << 20, transcendentals=20 << 20),
@@ -1502,11 +1506,13 @@
     count = tiles.shape[0]
     group = max(g for g in (1, 2, 3, 4, 6, 8) if count % g == 0)
 
+    first_slot = lambda: (lax.axis_index("dp") * lax.axis_size("seq") + lax.axis_index("seq")) * count
+
     def kernel(ids_ref, roots_ref, g_ref, w_ref, l_ref, r_ref, m_ref, v_ref, w_out, low_out, m_out, v_out):
         lane = lax.broadcasted_iota(jnp.int32, (1, BLK), 1)
 
         def column_scale(t):
-            number = ids_ref[pl.program_id(0) * group + t]
+            number = ids_ref[first_slot() + pl.program_id(0) * group + t]
             column = number % (3 * D // BLK)
             head = column % PAIRS * 2
             clipped = (number < QKV_TILES) & (column < 2 * PAIRS)
@@ -1638,7 +1644,7 @@
         ],
         axis=1,
     ).reshape(SMALL)
-    head_peak = jnp.max(peaks.reshape(PAIRS, 8, 2, QB)[:, 0], axis=-1).reshape(HEADS)
+    head_peak = peaks.reshape(PAIRS, 8, BLK)[:, 0, :2].reshape(HEADS)
     if ring:
         peak_rows = jnp.zeros((8, BLK), F32).at[:, :HEADS].set(head_peak[None, :])
         extra = jnp.concatenate([small_terms.reshape(SMALL_ROWS, BLK), peak_rows], axis=0)
@@ -1655,11 +1661,10 @@
         small_grads = lax.psum_scatter(small_terms, axes, scatter_dimension=0, tiled=True)
         head_peak = lax.pmax(head_peak, axes)
 
-    local_ids = lax.dynamic_slice_in_dim(tile_of_slot, owner_index * slot_count, slot_count, 0)
     limit = threshold[0]
     factors = limit / jnp.maximum(head_peak, limit)
     new_tiles, new_low, new_first, new_second = update_tiles(
-        local_ids, jnp.sqrt(factors), tile_grads, tiles, left_bases, right_bases, first_moments, second_moments
+        tile_of_slot, jnp.sqrt(factors), tile_grads, tiles, left_bases, right_bases, first_moments, second_moments
     )
     new_small, new_small_first, new_small_second = small_update(
         small_grads, small_params, small_first, small_second

time: 460 us -> 458 us (level)
  transfers between devices with their start and end apart: 1 -> 1, of which waited for: 0 -> 0; matrix products, arithmetic and copies ran while one was open for 2% -> 1% of each run, Pallas kernels for 16% -> 16%
where the time goes in v8:
time: 458 us; the launch traced here: 450 us
  Pallas kernels  421 us (92%)
  other arithmetic  11.8 us (3%)
  local copies, waits for them, and re-layouts  9.56 us (2%)
  starting transfers between devices  6.61 us (1%)
    pallas_call x1, Pallas kernels, sum_gradients(): pl.pallas_call(kernel, out_shape=[jax.ShapeDtypeStruct((OWNED, BLK), F32)...  104 us
    pallas_call x1, Pallas kernels, gather_weights(): pl.pallas_call(kernel, out_shape=[jax.ShapeDtypeStruct((32, rows, BLK), B...  99.7 us
    pallas_call x1, Pallas kernels, feed_forward(): pl.pallas_call(kernel, grid_spec=pltpu.PrefetchScalarGridSpec(num_scalar_...  73.1 us
    pallas_call x1, Pallas kernels, attend(): pl.pallas_call(kernel, grid=(PAIRS,), in_specs=[block, keys, keys, block,...  71.8 us
    pallas_call x1, Pallas kernels, finish(): pl.pallas_call(kernel, grid_spec=pltpu.PrefetchScalarGridSpec(num_scalar_...  38 us
    pallas_call x1, Pallas kernels, project(): pl.pallas_call(kernel, grid_spec=pltpu.PrefetchScalarGridSpec(num_scalar_...  24.6 us
    pallas_call x1, Pallas kernels, update_tiles(): pl.pallas_call(kernel, grid_spec=pltpu.PrefetchScalarGridSpec(num_scalar_...  9.55 us
  transfers between devices with their start and end apart: 1, of which 0 were waited for; matrix products, arithmetic and copies ran while one was open for 1% of the time, Pallas kernels for 16%

profile of v8, /device:TPU:16, one launch (start us, length us, event | category | flops | bytes accessed | tf_op | source)
XLA Modules:
  0.0 450.2 jit_solution(14431151920173762279)
XLA Ops:
  0.7 1.0 select_reduce_fusion
  2.3 0.8 reshape.111
  3.3 1.6 convert_element_type.15
  4.9 0.9 fusion.1.x_ref
  6.4 99.7 %gather_weights.1 = (bf16[32,3088,128]{2,1,0:T(8,128)(2,1)}, bf16[1024,1024]{1,0:T(8,128)(2,1)}, s32[8,1024]{1,0:T(8,128)}) custom-call(bf16[3088,128]{1,0:T(8,128)(2,1)} %fusion.1.x_ref, bf16[1024,1024]{1,0:T(8,128)(2,1)} %tok_ref.5, s32[8,1024]{1,0:T(8,128)} %broadcast_in_dim.42.seg_ref), custom_call_target="tpu_custom_call" | custom-call | tf_op jit(solution)/shard_map/gather_weights/pallas_call | solution.py:387
  106.1 0.9 convert_reduce_fusion
  107.7 1.0 multiply_sine_fusion
  108.6 24.6 %project.1 = (bf16[8,1024,128]{2,1,0:T(8,128)(2,1)}, bf16[8,2048,128]{2,1,0:T(8,128)(2,1)}, bf16[8,2048,128]{2,1,0:T(8,128)(2,1)}, bf16[8,1024,128]{2,1,0:T(8,128)(2,1)}, bf16[1024,1024]{1,0:T(8,128)(2,1)}) custom-call(s32[768]{0:T(1024)} %get-tuple-element.91.w_rows_ref, bf16[98816,128]{1,0:T(8,128)(2,1)} %bitcast.33, ...), custom_call_target="tpu_custom_call" | custom-call | tf_op jit(solution)/shard_map/project/pallas_call | solution.py:893
  133.2 71.8 %attend.1 = (bf16[8,1024,128]{2,1,0:T(8,128)(2,1)}, bf16[8,1024,128]{2,1,0:T(8,128)(2,1)}, bf16[8,1024,128]{2,1,0:T(8,128)(2,1)}, bf16[8,1024,128]{2,1,0:T(8,128...) custom-call(bf16[8,1024,128]{2,1,0:T(8,128)(2,1)} %get-tuple-element.55.q_ref, ...), custom_call_target="tpu_custom_call" | custom-call | flops 42949672960 | bytes 33554432 | tf_op jit(solution)/shard_map/attend/pallas_call | solution.py:1115
  205.0 6.6 %collective-permute-start = (bf16[2,8,1024,128]{3,2,1,0:T(8,128)(2,1)}, bf16[2,8,1024,128]{3,2,1,0:T(8,128)(2,1)}, u32[]{:S(2)}, u32[]{:S(2)}) collective-permute-start(bf16[2,8,1024,128]{3,2,1,0:T(8,128)(2,1)} %get-tuple-element.67), channel_id=1, source_target_pairs={{1,0},{2,1},{3,2},{4,3},{5,4},{6,5},{7,6},{9,8},{10,9},{11,10},{12... | collective-permute-start | bytes 12582920 | tf_op jit(solution)/shard_map/ppermute | solution.py:1564
  211.7 1.2 compare_reduce_fusion
  213.7 0.9 reshape.116.b_ref
  214.7 0.8 slice.49
  216.2 73.1 %feed_forward.1 = (bf16[1024,1024]{1,0:T(8,128)(2,1)}, bf16[1024,1024]{1,0:T(8,128)(2,1)}, f32[1,4096]{1,0:T(1,128)}, bf16[98304,128]{1,0:T(8,128)(2,1)}) custom-call(s32[768]{0:T(1024)} %get-tuple-element.91.w_rows_ref, s32[768]{0:T(1024)} %get-tuple-element.90.g_rows_ref, bf16[98816,128]{1,0:T(8,128)(2,1)} %bitcast.34, ...), custom_call_target="tpu_custom_call" | custom-call | flops 55834574848 | bytes 50331648 | tf_op jit(solution)/shard_map/feed_forward/pallas_call | solution.py:1290
  289.7 1.4 reduce.11
  291.9 38.0 %finish.1 = (bf16[1024,1024]{1,0:T(8,128)(2,1)}, f32[1024,1024]{1,0:T(8,128)}, f32[8,1024]{1,0:T(8,128)}, bf16[98304,128]{1,0:T(8,128)(2,1)}) custom-call(s32[768]{0:T(1024)} %get-tuple-element.91.w_rows_ref, s32[768]{0:T(1024)} %get-tuple-element.90.g_rows_ref, bf16[98816,128]{1,0:T(8,128)(2,1)} %bitcast.35, ...), custom_call_target="tpu_custom_call", output_to_operand_aliasing={{3}: (15, {})} | custom-call | tf_op jit(solution)/shard_map/finish/pallas_call | solution.py:1461
  329.9 0.8 slice_bitcast_fusion.3
  330.6 0.8 slice_bitcast_fusion.1
  332.6 103.9 %sum_gradients.1 = (f32[3072,128]{1,0:T(8,128)}, f32[104,128]{1,0:T(8,128)}) custom-call(bf16[98304,128]{1,0:T(8,128)(2,1)} %get-tuple-element.71.g_ref, f32[104,128]{1,0:T(8,128)} %pad_maximum_fusion.1.e_ref), custom_call_target="tpu_custom_call" | custom-call | tf_op jit(solution)/shard_map/sum_gradients/pallas_call | solution.py:724
  436.6 0.8 slice_bitcast_fusion
  437.4 1.2 fusion.10
  438.6 0.7 fusion.8
  439.3 9.6 %update_tiles.1 = (f32[24,128,128]{2,1,0:T(8,128)}, bf16[24,128,128]{2,1,0:T(8,128)(2,1)}, f32[24,128,128]{2,1,0:T(8,128)}, f32[24,128,128]{2,1,0:T(8,128)}) custom-call(s32[768]{0:T(1024)} %ids_ref.1, f32[16]{0:T(128)} %get-tuple-element.86.roots_ref, f32[24,128,128]{2,1,0:T(8,128)} %bitcast.36, f32[24,128,128]{2,1,0:T(8,128)} %w_ref.1, ...), custom_call_target="tpu_custom_call" | custom-call | tf_op jit(solution)/shard_map/update_tiles/pallas_call | solution.py:1540
  448.8 1.1 copy.58
  (34 shorter events, 5.5 us)
Async XLA Ops:
  0.6 5.2 %copy-start.2 = (s32[1,1024]{1,0:T(1,128)S(1)}, s32[1,1024]{1,0:T(1,128)}, u32[]{:S(2)}) copy-start(s32[1,1024]{1,0:T(1,128)} %param.16) | copy-start | bytes 12292
  205.0 86.8 %collective-permute-start = (bf16[2,8,1024,128]{3,2,1,0:T(8,128)(2,1)}, bf16[2,8,1024,128]{3,2,1,0:T(8,128)(2,1)}, u32[]{:S(2)}, u32[]{:S(2)}) collective-permute-start(bf16[2,8,1024,128]{3,2,1,0:T(8,128)(2,1)} %get-tuple-element.67), channel_id=1, source_target_pairs={{1,0},{2,1},{3,2},{4,3},{5,4},{6,5},{7,6},{9,8},{10,9},{11,10},{12... | collective-permute-start | bytes 12582920 | tf_op jit(solution)/shard_map/ppermute | solution.py:1564
  332.6 105.9 %copy-start.1 = (f32[384]{0:T(512)S(1)}, f32[384]{0:T(512)}, u32[]{:S(2)}) copy-start(f32[384]{0:T(512)} %param.24) | copy-start | bytes 4612
  332.6 105.9 %copy-start.3 = (f32[384]{0:T(512)S(1)}, f32[384]{0:T(512)}, u32[]{:S(2)}) copy-start(f32[384]{0:T(512)} %param.25) | copy-start | bytes 4612
  332.6 105.9 %copy-start.4 = (f32[384]{0:T(512)S(1)}, f32[384]{0:T(512)}, u32[]{:S(2)}) copy-start(f32[384]{0:T(512)} %param.26) | copy-start | bytes 4612
  439.3 9.6 %copy-start = (f32[3072,128]{1,0:T(8,128)S(1)}, f32[3072,128]{1,0:T(8,128)}, u32[]{:S(2)}) copy-start(f32[3072,128]{1,0:T(8,128)} %get-tuple-element.75) | copy-start | bytes 4718596

commit v9 on v8

--- a/solution.py
+++ b/solution.py
@@ -1234,8 +1234,8 @@
         db = [None]
 
         def stage2(c):
-            step = ROWB // 8
-            for k in range(8):
+            step = ROWB // 16
+            for k in range(16):
                 at = slice(k * step, (k + 1) * step)
                 to = slice(c * ROWB + k * step, c * ROWB + (k + 1) * step)
                 hidden, slope = gelu_parts(u_ref[c % 2, at, :])

time: 458 us -> 458 us (level)
  no operation moved by 1% of the time
where the time goes in v9:
time: 458 us; the launch traced here: 450 us
  Pallas kernels  421 us (92%)
  other arithmetic  11.8 us (3%)
  local copies, waits for them, and re-layouts  9.56 us (2%)
  starting transfers between devices  6.61 us (1%)
    pallas_call x1, Pallas kernels, sum_gradients(): pl.pallas_call(kernel, out_shape=[jax.ShapeDtypeStruct((OWNED, BLK), F32)...  104 us
    pallas_call x1, Pallas kernels, gather_weights(): pl.pallas_call(kernel, out_shape=[jax.ShapeDtypeStruct((32, rows, BLK), B...  99.7 us
    pallas_call x1, Pallas kernels, feed_forward(): pl.pallas_call(kernel, grid_spec=pltpu.PrefetchScalarGridSpec(num_scalar_...  73.1 us
    pallas_call x1, Pallas kernels, attend(): pl.pallas_call(kernel, grid=(PAIRS,), in_specs=[block, keys, keys, block,...  71.8 us
    pallas_call x1, Pallas kernels, finish(): pl.pallas_call(kernel, grid_spec=pltpu.PrefetchScalarGridSpec(num_scalar_...  38 us
    pallas_call x1, Pallas kernels, project(): pl.pallas_call(kernel, grid_spec=pltpu.PrefetchScalarGridSpec(num_scalar_...  24.6 us
    pallas_call x1, Pallas kernels, update_tiles(): pl.pallas_call(kernel, grid_spec=pltpu.PrefetchScalarGridSpec(num_scalar_...  9.56 us
  transfers between devices with their start and end apart: 1, of which 0 were waited for; matrix products, arithmetic and copies ran while one was open for 1% of the time, Pallas kernels for 16%

profile of v9, /device:TPU:16, one launch (start us, length us, event | category | flops | bytes accessed | tf_op | source)
XLA Modules:
  0.0 450.2 jit_solution(121802913834005367)
XLA Ops:
  0.7 1.0 select_reduce_fusion
  2.3 0.8 reshape.111
  3.3 1.6 convert_element_type.15
  4.9 0.9 fusion.1.x_ref
  6.4 99.7 %gather_weights.1 = (bf16[32,3088,128]{2,1,0:T(8,128)(2,1)}, bf16[1024,1024]{1,0:T(8,128)(2,1)}, s32[8,1024]{1,0:T(8,128)}) custom-call(bf16[3088,128]{1,0:T(8,128)(2,1)} %fusion.1.x_ref, bf16[1024,1024]{1,0:T(8,128)(2,1)} %tok_ref.5, s32[8,1024]{1,0:T(8,128)} %broadcast_in_dim.42.seg_ref), custom_call_target="tpu_custom_call" | custom-call | tf_op jit(solution)/shard_map/gather_weights/pallas_call | solution.py:387
  106.1 0.9 convert_reduce_fusion
  107.7 1.0 multiply_sine_fusion
  108.6 24.6 %project.1 = (bf16[8,1024,128]{2,1,0:T(8,128)(2,1)}, bf16[8,2048,128]{2,1,0:T(8,128)(2,1)}, bf16[8,2048,128]{2,1,0:T(8,128)(2,1)}, bf16[8,1024,128]{2,1,0:T(8,128)(2,1)}, bf16[1024,1024]{1,0:T(8,128)(2,1)}) custom-call(s32[768]{0:T(1024)} %get-tuple-element.91.w_rows_ref, bf16[98816,128]{1,0:T(8,128)(2,1)} %bitcast.33, ...), custom_call_target="tpu_custom_call" | custom-call | tf_op jit(solution)/shard_map/project/pallas_call | solution.py:893
  133.2 71.8 %attend.1 = (bf16[8,1024,128]{2,1,0:T(8,128)(2,1)}, bf16[8,1024,128]{2,1,0:T(8,128)(2,1)}, bf16[8,1024,128]{2,1,0:T(8,128)(2,1)}, bf16[8,1024,128]{2,1,0:T(8,128...) custom-call(bf16[8,1024,128]{2,1,0:T(8,128)(2,1)} %get-tuple-element.55.q_ref, ...), custom_call_target="tpu_custom_call" | custom-call | flops 42949672960 | bytes 33554432 | tf_op jit(solution)/shard_map/attend/pallas_call | solution.py:1115
  205.0 6.6 %collective-permute-start = (bf16[2,8,1024,128]{3,2,1,0:T(8,128)(2,1)}, bf16[2,8,1024,128]{3,2,1,0:T(8,128)(2,1)}, u32[]{:S(2)}, u32[]{:S(2)}) collective-permute-start(bf16[2,8,1024,128]{3,2,1,0:T(8,128)(2,1)} %get-tuple-element.67), channel_id=1, source_target_pairs={{1,0},{2,1},{3,2},{4,3},{5,4},{6,5},{7,6},{9,8},{10,9},{11,10},{12... | collective-permute-start | bytes 12582920 | tf_op jit(solution)/shard_map/ppermute | solution.py:1564
  211.7 1.2 compare_reduce_fusion
  213.7 0.9 reshape.116.b_ref
  214.7 0.8 slice.49
  216.2 73.1 %feed_forward.1 = (bf16[1024,1024]{1,0:T(8,128)(2,1)}, bf16[1024,1024]{1,0:T(8,128)(2,1)}, f32[1,4096]{1,0:T(1,128)}, bf16[98304,128]{1,0:T(8,128)(2,1)}) custom-call(s32[768]{0:T(1024)} %get-tuple-element.91.w_rows_ref, s32[768]{0:T(1024)} %get-tuple-element.90.g_rows_ref, bf16[98816,128]{1,0:T(8,128)(2,1)} %bitcast.34, ...), custom_call_target="tpu_custom_call" | custom-call | flops 55834574848 | bytes 50331648 | tf_op jit(solution)/shard_map/feed_forward/pallas_call | solution.py:1290
  289.7 1.4 reduce.11
  291.9 38.0 %finish.1 = (bf16[1024,1024]{1,0:T(8,128)(2,1)}, f32[1024,1024]{1,0:T(8,128)}, f32[8,1024]{1,0:T(8,128)}, bf16[98304,128]{1,0:T(8,128)(2,1)}) custom-call(s32[768]{0:T(1024)} %get-tuple-element.91.w_rows_ref, s32[768]{0:T(1024)} %get-tuple-element.90.g_rows_ref, bf16[98816,128]{1,0:T(8,128)(2,1)} %bitcast.35, ...), custom_call_target="tpu_custom_call", output_to_operand_aliasing={{3}: (15, {})} | custom-call | tf_op jit(solution)/shard_map/finish/pallas_call | solution.py:1461
  329.9 0.8 slice_bitcast_fusion.3
  330.6 0.8 slice_bitcast_fusion.1
  332.6 103.9 %sum_gradients.1 = (f32[3072,128]{1,0:T(8,128)}, f32[104,128]{1,0:T(8,128)}) custom-call(bf16[98304,128]{1,0:T(8,128)(2,1)} %get-tuple-element.71.g_ref, f32[104,128]{1,0:T(8,128)} %pad_maximum_fusion.1.e_ref), custom_call_target="tpu_custom_call" | custom-call | tf_op jit(solution)/shard_map/sum_gradients/pallas_call | solution.py:724
  436.6 0.8 slice_bitcast_fusion
  437.4 1.2 fusion.10
  438.6 0.7 fusion.8
  439.3 9.6 %update_tiles.1 = (f32[24,128,128]{2,1,0:T(8,128)}, bf16[24,128,128]{2,1,0:T(8,128)(2,1)}, f32[24,128,128]{2,1,0:T(8,128)}, f32[24,128,128]{2,1,0:T(8,128)}) custom-call(s32[768]{0:T(1024)} %ids_ref.1, f32[16]{0:T(128)} %get-tuple-element.86.roots_ref, f32[24,128,128]{2,1,0:T(8,128)} %bitcast.36, f32[24,128,128]{2,1,0:T(8,128)} %w_ref.1, ...), custom_call_target="tpu_custom_call" | custom-call | tf_op jit(solution)/shard_map/update_tiles/pallas_call | solution.py:1540
  448.8 1.1 copy.58
  (34 shorter events, 5.5 us)
Async XLA Ops:
  0.6 5.2 %copy-start.2 = (s32[1,1024]{1,0:T(1,128)S(1)}, s32[1,1024]{1,0:T(1,128)}, u32[]{:S(2)}) copy-start(s32[1,1024]{1,0:T(1,128)} %param.16) | copy-start | bytes 12292
  205.0 86.8 %collective-permute-start = (bf16[2,8,1024,128]{3,2,1,0:T(8,128)(2,1)}, bf16[2,8,1024,128]{3,2,1,0:T(8,128)(2,1)}, u32[]{:S(2)}, u32[]{:S(2)}) collective-permute-start(bf16[2,8,1024,128]{3,2,1,0:T(8,128)(2,1)} %get-tuple-element.67), channel_id=1, source_target_pairs={{1,0},{2,1},{3,2},{4,3},{5,4},{6,5},{7,6},{9,8},{10,9},{11,10},{12... | collective-permute-start | bytes 12582920 | tf_op jit(solution)/shard_map/ppermute | solution.py:1564
  332.6 105.9 %copy-start.1 = (f32[384]{0:T(512)S(1)}, f32[384]{0:T(512)}, u32[]{:S(2)}) copy-start(f32[384]{0:T(512)} %param.24) | copy-start | bytes 4612
  332.6 105.9 %copy-start.3 = (f32[384]{0:T(512)S(1)}, f32[384]{0:T(512)}, u32[]{:S(2)}) copy-start(f32[384]{0:T(512)} %param.25) | copy-start | bytes 4612
  332.6 105.9 %copy-start.4 = (f32[384]{0:T(512)S(1)}, f32[384]{0:T(512)}, u32[]{:S(2)}) copy-start(f32[384]{0:T(512)} %param.26) | copy-start | bytes 4612
  439.3 9.6 %copy-start = (f32[3072,128]{1,0:T(8,128)S(1)}, f32[3072,128]{1,0:T(8,128)}, u32[]{:S(2)}) copy-start(f32[3072,128]{1,0:T(8,128)} %get-tuple-element.75) | copy-start | bytes 4718596
